TPU v7x, 128 devices: a whole 4x4x4 slice. The times are simulated.
128 devices in a mesh: section: 8 (over y_hi, x), dp: 16 (over y_lo, z, core).
Axes of the slice: x: 4, y: 4 (y_hi: 2, y_lo: 2; y = y_hi * 2 + y_lo), z: 4, core: 2. Of those that a mesh axis runs over, the one named last changes fastest.
Arguments:
- inputs: bfloat16 [2, 1024, 4096], P(None, 'dp'), may hold values from -6 to 6
- cotangent: bfloat16 [2, 1024, 4096], P(None, 'dp'), may hold values from -0.13183594 to 0.13183594
- w_in: bfloat16 [16, 4096, 256], P('section'), as said below
- w_out: bfloat16 [16, 256, 4096], P('section'), as said below
- gain: float32 [16, 4096], P('section'), as said below
Outputs:
- grad_in: float32 [8, 4096, 256], P('section', 'dp')
- grad_out: float32 [8, 256, 4096], P('section', None, 'dp')
- grad_gain: float32 [8, 4096], P('section', 'dp')
Inputs may be any that keep to these rules, and one draw needn't show every extreme that they name: `w_in`: rows 2 j and 2 (7 - j) + 1 hold the same layer j, so that a device holds a layer of the down relay and the mirrored layer of the up relay. `w_out`: rows 2 j and 2 (7 - j) + 1 hold the same layer j. `gain`: rows 2 j and 2 (7 - j) + 1 hold the same layer j.
All inputs are finite; a program needn't handle non-finite values.
Results may differ from a plain program's by a relative error of at most 0.03.
Values may be sent and summed in bfloat16 or wider, within the bound.
No kernel may reach another device: no remote copies, remote signals or barrier semaphores. Data moves between devices by JAX's collectives and lax.ppermute only.
A program may use at most 128 MiB of HBM per device.

v0:
```python
import functools

import jax
import jax.numpy as jnp
from jax import lax
from jax.experimental import pallas as pl
from jax.experimental.pallas import tpu as pltpu
from jax.sharding import PartitionSpec as P

epsilon = 1e-05
STAGES = (0, 1, 2, 3, 2, 1, 0, 1, 2, 3, 2, 1, 0)
LAST = len(STAGES) - 1
MICROS = 2
bf16 = jnp.bfloat16
f32 = jnp.float32
VMEM = pl.BlockSpec(memory_space=pltpu.VMEM)
ANY = pl.BlockSpec(memory_space=pl.ANY)
LOADS = 4
MIB = 2**20


def matmul(left, right):
    return jnp.dot(left, right, preferred_element_type=f32)


def transposed_matmul(left, right):
    return lax.dot_general(left, right, (((0,), (0,)), ((), ())), preferred_element_type=f32)


def place():
    sections = lax.axis_size("section")
    position = lax.axis_index("section")
    half = (position >= sections // 2).astype(jnp.int32)
    fold = jnp.where(half == 0, position, sections - 1 - position)
    return fold, half


def call(body, name, reads, updates=(), places=(), new=(), scratch=(), limit=16):
    n_read, n_update, n_place = len(reads), len(updates), len(places)

    def kernel(*refs):
        ins, outs = refs[: n_read + n_update + n_place], refs[n_read + n_update + n_place :]
        for old, now in zip(ins[n_read : n_read + n_update], outs):
            now[...] = old[...]
        body(ins[:n_read], *outs)

    shapes = [pltpu.VMEM(a.shape, a.dtype) for a in updates]
    shapes += [jax.ShapeDtypeStruct(a.shape, a.dtype) for a in places]
    shapes += list(new)
    kept = [VMEM] * n_update + [ANY] * n_place
    return pl.pallas_call(
        kernel,
        out_shape=tuple(shapes),
        in_specs=[spec for _, spec in reads] + kept,
        out_specs=tuple(kept + [VMEM] * len(new)),
        input_output_aliases={n_read + i: i for i in range(n_update + n_place)},
        scratch_shapes=list(scratch),
        compiler_params=pltpu.CompilerParams(vmem_limit_bytes=limit * MIB),
        cost_estimate=pl.CostEstimate(flops=10**9, bytes_accessed=4 * MIB, transcendentals=0),
        name=name,
    )(*[a for a, _ in reads], *updates, *places)


def load(copy, sources, targets, sems):
    waits = []
    for which, (source, target) in enumerate(zip(sources, targets)):
        size = source.shape[1] // LOADS
        pieces = []
        for i in range(LOADS):
            part = pl.ds(i * size, size)
            pieces.append(
                pltpu.make_async_copy(
                    source.at[copy, part], target.at[part], sems.at[which * LOADS + i]
                )
            )
        for piece in pieces:
            piece.start()
        waits.append(pieces)
    return waits


def wait_all(pieces):
    for piece in pieces:
        piece.wait()


def forward(source, rows, gain, weight_in, weight_out, pack_ref, pre, scale, ready=None):
    chips = pack_ref.shape[0]
    micro, width = source.shape
    chunk = width // chips
    wide = source.astype(f32)
    scaling = lax.rsqrt(jnp.mean(wide * wide, axis=-1, keepdims=True) + epsilon)
    normal = wide * scaling
    if ready is not None:
        wait_all(ready[0])
    before = matmul((normal * gain[...]).astype(bf16), weight_in[...])
    inner = (before * jax.nn.sigmoid(before)).astype(bf16)
    pre[rows, :] = before
    scale[rows, :] = jnp.broadcast_to(scaling, (micro, 128))
    for chip in range(chips):
        pack_ref[chip, :, :chunk] = normal[:, chip * chunk : (chip + 1) * chunk].astype(bf16)
        pack_ref[chip, :, chunk:] = inner
    if ready is not None:
        wait_all(ready[1])
    if weight_out is not None:
        return (wide + matmul(inner, weight_out[...])).astype(bf16)


def backward(grad, rows, gain, weight_in_t, weight_out_t, pack_ref, pre, scale, hats):
    chips = pack_ref.shape[0]
    width = grad.shape[1]
    chunk = width // chips
    before = pre[rows, :]
    sigma = jax.nn.sigmoid(before)
    d_inner = matmul(grad, weight_out_t[...])
    delta = (d_inner * sigma * (1.0 + before * (1.0 - sigma))).astype(bf16)
    for chip in range(chips):
        pack_ref[chip, :, :chunk] = grad[:, chip * chunk : (chip + 1) * chunk]
        pack_ref[chip, :, chunk:] = delta
    if hats is None:
        return None
    mixed = jnp.sum(delta.astype(f32) * before, axis=-1, keepdims=True) / width
    scaled = matmul(delta, weight_in_t[...]) * gain[...]
    scaling = scale[rows, :1]
    result = []
    for chip in range(chips):
        part = slice(chip * chunk, (chip + 1) * chunk)
        normal = hats(chip).astype(f32)
        result.append(
            (grad[:, part].astype(f32) + scaling * (scaled[:, part] - normal * mixed)).astype(bf16)
        )
    return jnp.concatenate(result, axis=1)


def on_device(inputs, cotangent, w_in, w_out, gain):
    sections = lax.axis_size("section")
    parts = lax.axis_size("dp")
    chips = parts // 2
    rows, width = inputs.shape[1:]
    micro = rows // MICROS
    branch = w_in.shape[2]
    chunk = width // chips
    pack = chunk + branch

    dma = pltpu.SemaphoreType.DMA
    block = pltpu.VMEM((micro, width), bf16)
    packed = pltpu.VMEM((chips, micro, pack), bf16)
    in_shape, out_shape = pltpu.VMEM((width, branch), bf16), pltpu.VMEM((branch, width), bf16)
    in_turned, out_turned = out_shape, in_shape
    row_shape = pltpu.VMEM((1, width), f32)
    pre_shapes = (pltpu.VMEM((rows, branch), f32), pltpu.VMEM((rows, 128), f32))
    load_sems = dma((2 * LOADS,))
    same_core = [list(range(core, parts, 2)) for core in range(2)]
    fold_here, _ = place()

    def of_micro(m):
        return pl.ds(m * micro, micro)

    def send_on(sent, stage):
        a, b = STAGES[stage], STAGES[stage + 1]
        pairs = [(a, b), (sections - 1 - a, sections - 1 - b)]
        return lax.ppermute(sent, "section", pairs)

    def exchange(array):
        return lax.all_to_all(array, "dp", 0, 0, axis_index_groups=same_core, tiled=False)

    def new_boxes(name, *layers):
        shapes = [jax.ShapeDtypeStruct((chips, n * rows, pack), bf16) for n in layers]
        return pl.pallas_call(
            lambda *refs: None, out_shape=tuple(shapes), out_specs=(ANY,) * len(shapes), name=name
        )()

    def in_vmem(*arrays):
        return [(a, VMEM) for a in arrays]

    (early,) = new_boxes("early_box", 1)

    def start_kernel(reads, box, sent, weight_in, weight_out, gain_1, gain_2, pre, scale, staged, stash, sem, sems):
        inputs, source_in, source_out, source_gain = reads
        fold, half = place()
        ready = load(half, (source_in, source_out), (weight_in, weight_out), sems)
        gain_1[...] = source_gain[pl.ds(half, 1), :]
        gain_2[...] = source_gain[pl.ds(1 - half, 1), :]

        @pl.when(fold == STAGES[0])
        def _():
            copy = pltpu.make_async_copy(inputs.at[half, of_micro(0)], staged, sem)
            copy.start()
            copy.wait()
            sent[...] = forward(
                staged[...], of_micro(0), gain_1, weight_in, weight_out, stash, pre, scale, ready
            )
            out = pltpu.make_async_copy(stash, box.at[:, of_micro(0), :], sem)
            out.start()
            out.wait()

        @pl.when(fold != STAGES[0])
        def _():
            wait_all(ready[0] + ready[1])

    moved = [None] * MICROS
    early, sent, weight_in, weight_out, gain_1, gain_2, pre_1, scale_1 = call(
        start_kernel,
        "forward_0_0",
        [(inputs, ANY), (w_in, ANY), (w_out, ANY), (gain, VMEM)],
        places=(early,),
        new=(block, in_shape, out_shape, row_shape, row_shape) + pre_shapes,
        scratch=[block, packed, dma(()), load_sems],
        limit=52,
    )
    moved[0] = send_on(sent, 0)
    for m in range(1, MICROS):

        def input_kernel(reads, pre, scale, box, sent, staged, stash, sem, m=m):
            inputs, weight_in, weight_out, gain_1 = reads
            fold, half = place()

            @pl.when(fold == STAGES[0])
            def _():
                copy = pltpu.make_async_copy(inputs.at[half, of_micro(m)], staged, sem)
                copy.start()
                copy.wait()
                sent[...] = forward(
                    staged[...], of_micro(m), gain_1, weight_in, weight_out, stash, pre, scale
                )
                out = pltpu.make_async_copy(stash, box.at[:, of_micro(m), :], sem)
                out.start()
                out.wait()

        pre_1, scale_1, early, sent = call(
            input_kernel,
            "forward_0_%d" % m,
            [(inputs, ANY)] + in_vmem(weight_in, weight_out, gain_1),
            (pre_1, scale_1),
            (early,),
            (block,),
            [block, packed, dma(())],
        )
        moved[m] = send_on(sent, 0)

    def forward_kernel(stage, layer, m, reads, pre, scale, box, sent, stash, sem):
        moved, weight_in, weight_out, gain = reads
        fold, _ = place()

        @pl.when(fold == STAGES[stage])
        def _():
            sent[...] = forward(
                moved[...], of_micro(m), gain, weight_in, weight_out, stash, pre, scale
            )
            out = pltpu.make_async_copy(stash, box.at[:, pl.ds(layer * rows + m * micro, micro), :], sem)
            out.start()
            out.wait()

    def forward_stage(stage, layer, m, weights, kept, box):
        pre, scale, box, sent = call(
            functools.partial(forward_kernel, stage, layer, m),
            "forward_%d_%d" % (stage, m),
            in_vmem(moved[m], *weights),
            kept,
            (box,),
            (block,),
            [packed, dma(())],
        )
        moved[m] = send_on(sent, stage)
        return (pre, scale), box

    kept_1 = (pre_1, scale_1)
    for m in range(MICROS):
        kept_1, early = forward_stage(1, 0, m, (weight_in, weight_out, gain_1), kept_1, early)

    hat_early = lax.cond(fold_here <= 1, exchange, lambda a: a, early)
    (boxes,) = new_boxes("boxes", 2)
    hat_early, boxes, early, gain_1, gain_2, kept_1, w_in, w_out = lax.optimization_barrier(
        (hat_early, boxes, early, gain_1, gain_2, kept_1, w_in, w_out)
    )

    def load_both(reads, *refs):
        weights, (pre, scale), sems = refs[:4], refs[4:6], refs[6:]
        _, half = place()
        waits = load(half, reads, weights[:2], sems[0])
        waits += load(1 - half, reads, weights[2:], sems[1])
        for pieces in waits:
            wait_all(pieces)

    *weights, pre_2, scale_2 = call(
        load_both,
        "load",
        [(w_in, ANY), (w_out, ANY)],
        new=(in_shape, out_shape, in_shape, out_shape) + pre_shapes,
        scratch=[load_sems, load_sems],
        limit=48,
    )
    weights_1, weights_2 = (*weights[:2], gain_1), (*weights[2:], gain_2)
    kept_2 = (pre_2, scale_2)

    for m in range(MICROS):
        kept_1, boxes = forward_stage(2, 0, m, weights_1, kept_1, boxes)

    def turning_kernel(m, reads, pre_1, scale_1, pre_2, scale_2, box, sent, stash, sems):
        moved, in_1, out_1, gain_1, in_2, out_2, gain_2 = reads
        fold, _ = place()

        @pl.when(fold == STAGES[3])
        def _():
            copies = [
                pltpu.make_async_copy(
                    stash.at[i], box.at[:, pl.ds(i * rows + m * micro, micro), :], sems.at[i]
                )
                for i in range(2)
            ]
            sent[...] = forward(
                moved[...], of_micro(m), gain_1, in_1, out_1, stash.at[0], pre_1, scale_1
            )
            copies[0].start()
            sent[...] = forward(
                sent[...], of_micro(m), gain_2, in_2, out_2, stash.at[1], pre_2, scale_2
            )
            copies[1].start()
            wait_all(copies)

    packed_2 = pltpu.VMEM((2, chips, micro, pack), bf16)
    for m in range(MICROS):
        *kept, boxes, sent = call(
            functools.partial(turning_kernel, m),
            "forward_3_%d" % m,
            in_vmem(moved[m], *weights_1, *weights_2),
            kept_1 + kept_2,
            (boxes,),
            (block,),
            [packed_2, dma((2,))],
        )
        kept_1, kept_2 = tuple(kept[:2]), tuple(kept[2:])
        moved[m] = send_on(sent, 3)
    for m in range(MICROS):
        kept_2, boxes = forward_stage(4, 1, m, weights_2, kept_2, boxes)

    def turn(weight_in, weight_out, weight_in_t, weight_out_t):
        @pl.loop(0, width // branch)
        def _(tile):
            part = pl.ds(pl.multiple_of(tile * branch, branch), branch)
            weight_in_t[:, part] = weight_in[part, :].T
            weight_out_t[part, :] = weight_out[:, part].T

    turned_2 = call(
        lambda reads, *refs: turn(*reads, *refs),
        "turn",
        in_vmem(*weights[2:]),
        new=(in_turned, out_turned),
    )
    for m in range(MICROS):
        kept_2, boxes = forward_stage(5, 0, m, weights_2, kept_2, boxes)

    def middle_kernel(m, reads, pre, scale, box, sent, staged, stash, sem, sems):
        moved, cotangent, weight_in, weight_in_t, weight_out_t, gain = reads
        fold, half = place()

        @pl.when(fold == STAGES[6])
        def _():
            copy = pltpu.make_async_copy(cotangent.at[half, of_micro(m)], staged, sem)
            copy.start()
            copies = [
                pltpu.make_async_copy(
                    stash.at[i], box.at[:, pl.ds(i * rows + m * micro, micro), :], sems.at[i]
                )
                for i in range(2)
            ]
            forward(moved[...], of_micro(m), gain, weight_in, None, stash.at[0], pre, scale)
            copies[0].start()
            copy.wait()
            sent[...] = backward(
                staged[...], of_micro(m), gain, weight_in_t, weight_out_t, stash.at[1], pre, scale,
                lambda chip: stash[0, chip, :, :chunk],
            )
            copies[1].start()
            wait_all(copies)

    for m in range(MICROS):
        pre, scale, boxes, sent = call(
            functools.partial(middle_kernel, m),
            "middle_%d" % m,
            [(moved[m], VMEM), (cotangent, ANY)] + in_vmem(weights[2], *turned_2, gain_2),
            kept_2,
            (boxes,),
            (block,),
            [block, packed_2, dma(()), dma((2,))],
        )
        kept_2 = (pre, scale)
        moved[m] = send_on(sent, 6)

    hat_block = pltpu.VMEM((chips, micro, chunk), bf16)

    def fetch(source, layer, m, target, sem):
        source = source.at[:, pl.ds(layer * rows + m * micro, micro), pl.ds(0, chunk)]
        return pltpu.make_async_copy(source, target, sem)

    def backward_kernel(stage, m, hat_layer, layer, reads, box, *refs):
        moved, weight_in_t, weight_out_t, gain, pre, scale = reads[:6]
        sent = refs[0] if stage < LAST else None
        hats, stash, sems = refs[-3:]
        fold, _ = place()

        @pl.when(fold == STAGES[stage])
        def _():
            if sent is not None:
                source = reads[6] if len(reads) > 6 else box
                coming = fetch(source, hat_layer, m, hats, sems.at[0])
                coming.start()

            def normal(chip):
                if chip == 0:
                    coming.wait()
                return hats[chip]

            result = backward(
                moved[...], of_micro(m), gain, weight_in_t, weight_out_t, stash, pre, scale,
                normal if sent is not None else None,
            )
            out = pltpu.make_async_copy(
                stash, box.at[:, pl.ds(layer * rows + m * micro, micro), :], sems.at[1]
            )
            out.start()
            if sent is not None:
                sent[...] = result
            out.wait()

    def backward_stage(stage, m, weights, kept, source, hat_layer, box, layer):
        reads = in_vmem(moved[m], *weights, *kept)
        if source is not None:
            reads.append((source, ANY))
        out = call(
            functools.partial(backward_kernel, stage, m, hat_layer, layer),
            "backward_%d_%d" % (stage, m),
            reads,
            (),
            (box,),
            (block,) if stage < LAST else (),
            [hat_block, packed, dma((2,))],
        )
        if stage < LAST:
            moved[m] = send_on(out[1], stage)
        return out[0]

    for m in range(MICROS):
        boxes = backward_stage(7, m, (*turned_2, gain_2), kept_2, None, 0, boxes, 1)

    both = lax.cond(fold_here < sections, exchange, lambda a: a, boxes)
    late, last = new_boxes("late_boxes", 1, 1)
    both, boxes, late, last, gain_1, gain_2, kept_1, kept_2, early, w_in, w_out = lax.optimization_barrier(
        (both, boxes, late, last, gain_1, gain_2, kept_1, kept_2, early, w_in, w_out)
    )

    def load_turned(reads, in_1, out_1, in_2, out_2, raw_in, raw_out, sems):
        _, half = place()
        for copy, turned in ((half, (in_1, out_1)), (1 - half, (in_2, out_2))):
            waits = load(copy, reads, (raw_in, raw_out), sems)
            wait_all(waits[0] + waits[1])
            turn(raw_in, raw_out, *turned)

    turned = call(
        load_turned,
        "load_turned",
        [(w_in, ANY), (w_out, ANY)],
        new=(in_turned, out_turned, in_turned, out_turned),
        scratch=[in_shape, out_shape, load_sems],
        limit=48,
    )
    turned_1, turned_2 = (*turned[:2], gain_1), (*turned[2:], gain_2)

    for m in range(MICROS):
        late = backward_stage(8, m, turned_2, kept_2, boxes, 1, late, 0)

    def back_turning_kernel(m, reads, late, last, sent, hats, stash, sems):
        moved, in_2, out_2, gain_2, pre_2, scale_2, in_1, out_1, gain_1, pre_1, scale_1, boxes = reads
        fold, _ = place()

        @pl.when(fold == STAGES[9])
        def _():
            coming = [fetch(boxes, layer, m, hats.at[layer], sems.at[layer]) for layer in range(2)]
            for piece in coming:
                piece.start()

            def normal(layer, chip):
                if chip == 0:
                    coming[layer].wait()
                return hats[layer, chip]

            sent[...] = backward(
                moved[...], of_micro(m), gain_2, in_2, out_2, stash.at[0], pre_2, scale_2,
                functools.partial(normal, 1),
            )
            copies = [
                pltpu.make_async_copy(stash.at[i], box.at[:, of_micro(m), :], sems.at[2 + i])
                for i, box in enumerate((late, last))
            ]
            copies[0].start()
            sent[...] = backward(
                sent[...], of_micro(m), gain_1, in_1, out_1, stash.at[1], pre_1, scale_1,
                functools.partial(normal, 0),
            )
            copies[1].start()
            wait_all(copies)

    for m in range(MICROS):
        late, last, sent = call(
            functools.partial(back_turning_kernel, m),
            "backward_9_%d" % m,
            in_vmem(moved[m], *turned_2, *kept_2, *turned_1, *kept_1) + [(boxes, ANY)],
            (),
            (late, last),
            (block,),
            [pltpu.VMEM((2, chips, micro, chunk), bf16), packed_2, dma((4,))],
        )
        moved[m] = send_on(sent, 9)
    for m in range(MICROS):
        last = backward_stage(10, m, turned_1, kept_1, boxes, 0, last, 0)
    for m in range(MICROS):
        late = backward_stage(11, m, turned_1, kept_1, early, 0, late, 0)
    for m in range(MICROS):
        late = backward_stage(LAST, m, turned_1, kept_1, None, 0, late, 0)

    late, last = lax.optimization_barrier((late, last))
    last = lax.cond(fold_here >= 2, exchange, lambda a: a, last)
    late = exchange(late)

    def products(reads, keep, send, whole_in, whole_out):
        early, both, late, last = reads
        fold, half = place()
        core = lax.rem(lax.axis_index("dp"), 2)
        mine = pl.ds(pl.multiple_of(core * branch, branch), branch)
        theirs = pl.ds(pl.multiple_of((1 - core) * branch, branch), branch)

        def product(slot, hat, up):
            def rows_of(ref, part):
                return ref[:, :, part].reshape(chips * rows, -1)

            narrow, wide = slice(chunk, pack), slice(0, chunk)
            whole_in[...] = transposed_matmul(rows_of(hat, wide), rows_of(up, narrow))
            whole_out[...] = transposed_matmul(rows_of(hat, narrow), rows_of(up, wide))
            keep[slot, 0] = whole_in[mine, :]
            keep[slot, 1] = whole_out[:, mine]
            send[slot, 0] = whole_in[theirs, :].astype(bf16)
            send[slot, 1] = whole_out[:, theirs].astype(bf16)

        low, high = both.at[:, :rows], both.at[:, rows:]

        @pl.when(fold <= 1)
        def _():
            product(half, early, late)
            product(1 - half, low, high)

        @pl.when(fold > 1)
        def _():
            product(half, low, last)
            product(1 - half, high, late)

    keep, send = call(
        products,
        "products",
        in_vmem(hat_early, both, late, last),
        new=(pltpu.VMEM((2, 2, branch, branch), f32), pltpu.VMEM((2, 2, branch, branch), bf16)),
        scratch=[pltpu.VMEM((2 * branch, branch), f32), pltpu.VMEM((branch, 2 * branch), f32)],
    )
    total = keep + lax.ppermute(send, "dp", [(i, i ^ 1) for i in range(parts)]).astype(f32)
    mirror = [(s, sections - 1 - s) for s in range(sections)]
    total = total[0] + lax.ppermute(total[1].astype(bf16), "section", mirror).astype(f32)
    start = lax.axis_index("dp") * branch
    own_gain = lax.dynamic_slice_in_dim(gain[0], start, branch, 0)
    own_in = lax.dynamic_slice_in_dim(w_in[0], start, branch, 0).astype(f32)
    grad_in = total[0] * own_gain[:, None]
    grad_gain = jnp.sum(total[0] * own_in, axis=1)
    return (grad_in[None], total[1][None], grad_gain[None])


def solution(mesh):
    return jax.shard_map(
        on_device,
        mesh=mesh,
        in_specs=(
            P(None, "dp", None),
            P(None, "dp", None),
            P("section", None, None),
            P("section", None, None),
            P("section", None),
        ),
        out_specs=(P("section", "dp", None), P("section", None, "dp"), P("section", "dp")),
        check_vma=False,
    )
```

profile of v0, /device:TPU:18, one launch (start us, length us, event | category | flops | bytes accessed | tf_op | source)
XLA Modules:
  0.0 184.3 jit_solution(18399820217486386162)
XLA Ops:
  0.7 3.1 %forward_0_0.1 = (bf16[8,64,768]{2,1,0:T(8,128)(2,1)}, bf16[32,4096]{1,0:T(8,128)(2,1)S(1)}, bf16[4096,256]{1,0:T(8,128)(2,1)S(1)}, bf16[256,4096]{1,0:T(8,128)(...) custom-call(bf16[2,64,4096]{2,1,0:T(8,128)(2,1)} %refs_0_.3, ...), custom_call_target="tpu_custom_call", output_to_operand_aliasing={{0}: (4, {})} | custom-call | flops 1000000000 | bytes 4194304 | tf_op jit(solution)/shard_map/forward_0_0/pallas_call | solution.py:51
  3.7 0.7 collective-permute-start.1
  4.5 0.7 collective-permute-start
  5.2 1.3 collective-permute-start.3
  6.6 1.3 collective-permute-start.2
  7.9 1.1 conditional.3
  7.9 1.1 copy.76
  9.0 3.8 %load.1 = (bf16[4096,256]{1,0:T(8,128)(2,1)S(1)}, bf16[256,4096]{1,0:T(8,128)(2,1)S(1)}, bf16[4096,256]{1,0:T(8,128)(2,1)S(1)}, bf16[256,4096]{1,0:T(8,128)(2,1)...) custom-call(bf16[2,4096,256]{2,1,0:T(8,128)(2,1)} %refs_0_.5, bf16[2,256,4096]{2,1,0:T(8,128)(2,1)} %refs_1_.7), custom_call_target="tpu_custom_call" | custom-call | flops 1000000000 | bytes 4194304 | tf_op jit(solution)/shard_map/load/pallas_call | solution.py:51
  12.8 11.5 %collective-permute-done.3.refs_0_ = bf16[32,4096]{1,0:T(8,128)(2,1)S(1)} collective-permute-done((bf16[32,4096]{1,0:T(8,128)(2,1)S(1)}, bf16[32,4096]{1,0:T(8,128)(2,1)S(1)}, u32[]{:S(2)}, u32[]{:S(2)}) %collective-permute-start.3) | collective-permute-done | bytes 262176 | tf_op jit(solution)/shard_map/ppermute | solution.py:162
  24.4 1.6 forward_2_0.1
  26.0 1.3 collective-permute-start.5
  27.3 2.7 %collective-permute-done.2.refs_0_ = bf16[32,4096]{1,0:T(8,128)(2,1)S(1)} collective-permute-done((bf16[32,4096]{1,0:T(8,128)(2,1)S(1)}, bf16[32,4096]{1,0:T(8,128)(2,1)S(1)}, u32[]{:S(2)}, u32[]{:S(2)}) %collective-permute-start.2) | collective-permute-done | bytes 262176 | tf_op jit(solution)/shard_map/ppermute | solution.py:162
  30.0 1.6 forward_2_1.1
  31.6 1.3 collective-permute-start.4
  33.0 1.3 collective-permute-start.7
  34.3 3.3 %collective-permute-done.4.refs_0_ = bf16[32,4096]{1,0:T(8,128)(2,1)S(1)} collective-permute-done((bf16[32,4096]{1,0:T(8,128)(2,1)S(1)}, bf16[32,4096]{1,0:T(8,128)(2,1)S(1)}, u32[]{:S(2)}, u32[]{:S(2)}) %collective-permute-start.4) | collective-permute-done | bytes 262176 | tf_op jit(solution)/shard_map/ppermute | solution.py:162
  37.6 1.3 collective-permute-start.6
  38.9 3.3 %collective-permute-done.7.refs_0_ = bf16[32,4096]{1,0:T(8,128)(2,1)S(1)} collective-permute-done((bf16[32,4096]{1,0:T(8,128)(2,1)S(1)}, bf16[32,4096]{1,0:T(8,128)(2,1)S(1)}, u32[]{:S(2)}, u32[]{:S(2)}) %collective-permute-start.7) | collective-permute-done | bytes 262176 | tf_op jit(solution)/shard_map/ppermute | solution.py:162
  42.2 1.6 forward_4_0.1
  43.8 7.6 %collective-permute-start.9 = (bf16[32,4096]{1,0:T(8,128)(2,1)S(1)}, bf16[32,4096]{1,0:T(8,128)(2,1)S(1)}, u32[]{:S(2)}, u32[]{:S(2)}) collective-permute-start(bf16[32,4096]{1,0:T(8,128)(2,1)S(1)} %get-tuple-element.200), channel_id=1, source_target_pairs={{32,16},{80,96},{33,17},{81,97},{34,18},{82,98},{35,19},{83,99},{3... | collective-permute-start | bytes 786440 | tf_op jit(solution)/shard_map/ppermute | solution.py:162
  51.4 1.6 forward_4_1.1
  53.0 1.5 collective-permute-start.8
  54.5 3.1 %collective-permute-done.9.refs_0_ = bf16[32,4096]{1,0:T(8,128)(2,1)S(1)} collective-permute-done((bf16[32,4096]{1,0:T(8,128)(2,1)S(1)}, bf16[32,4096]{1,0:T(8,128)(2,1)S(1)}, u32[]{:S(2)}, u32[]{:S(2)}) %collective-permute-start.9) | collective-permute-done | bytes 262176 | tf_op jit(solution)/shard_map/ppermute | solution.py:162
  57.6 0.7 collective-permute-start.11
  58.3 2.1 %collective-permute-done.8.refs_0_ = bf16[32,4096]{1,0:T(8,128)(2,1)S(1)} collective-permute-done((bf16[32,4096]{1,0:T(8,128)(2,1)S(1)}, bf16[32,4096]{1,0:T(8,128)(2,1)S(1)}, u32[]{:S(2)}, u32[]{:S(2)}) %collective-permute-start.8) | collective-permute-done | bytes 262176 | tf_op jit(solution)/shard_map/ppermute | solution.py:162
  60.5 0.8 collective-permute-start.10
  61.3 2.0 %turn.1 = (bf16[256,4096]{1,0:T(8,128)(2,1)S(1)}, bf16[4096,256]{1,0:T(8,128)(2,1)S(1)}) custom-call(bf16[4096,256]{1,0:T(8,128)(2,1)S(1)} %get-tuple-element.177.refs_4_.refs_1_.refs_0_.refs_2_, bf16[256,4096]{1,0:T(8,128)(2,1)S(1)} %get-tuple-element.178.refs_5_.refs_2_.refs_1_), custom_call_target="tpu_custom_call" | custom-call | flops 1000000000 | bytes 4194304 | tf_op jit(solution)/shard_map/turn/pallas_call | solution.py:51
  64.1 0.7 collective-permute-start.12
  64.8 0.7 backward_7_0.1
  65.5 1.3 collective-permute-start.15
  66.9 0.7 backward_7_1.1
  67.6 1.3 collective-permute-start.14
  68.9 22.7 %conditional.4 = (bf16[8,128,768]{2,1,0:T(8,128)(2,1)S(1)}) conditional(s32[]{:T(128)} %convert_element_type.28, bf16[8,128,768]{2,1,0:T(8,128)(2,1)} %get-tuple-element.238.refs_6_.refs_11_, bf16[8,128,768]{2,1,0:T(8,128)(2,1)} %get-tuple-element.238.refs_6_.refs_11_), branch_computations={%region_2.3_spmd, %region_3.4_spmd} | conditional | bytes 3145736 | solution.py:446
  68.9 22.7 %all_to_all.18 = bf16[8,128,768]{2,1,0:T(8,128)(2,1)S(1)} all-to-all(bf16[8,128,768]{2,1,0:T(8,128)(2,1)} %param.3), channel_id=1, replica_groups={{0,2,4,6,8,10,12,14},{1,3,5,7,9,11,13,15},{16,18,20,22,24,26,28,30},{17..., dimensions={0} | all-to-all | bytes 3145728 | tf_op jit(solution)/shard_map/cond/branch_1_fun/all_to_all | solution.py:165
  91.6 1.2 copy-done.7
  92.7 8.3 %load_turned.1 = (bf16[256,4096]{1,0:T(8,128)(2,1)S(1)}, bf16[4096,256]{1,0:T(8,128)(2,1)S(1)}, bf16[256,4096]{1,0:T(8,128)(2,1)S(1)}, bf16[4096,256]{1,0:T(8,128)(2,1)S(1)}) custom-call(bf16[2,4096,256]{2,1,0:T(8,128)(2,1)} %refs_0_.5, bf16[2,256,4096]{2,1,0:T(8,128)(2,1)} %refs_1_.7), custom_call_target="tpu_custom_call" | custom-call | flops 1000000000 | bytes 4194304 | tf_op jit(solution)/shard_map/load_turned/pallas_call | solution.py:51
  101.1 1.5 backward_8_0.1
  102.6 1.3 collective-permute-start.17
  103.9 2.5 %backward_8_1.1 = (bf16[8,64,768]{2,1,0:T(8,128)(2,1)S(1)}, bf16[32,4096]{1,0:T(8,128)(2,1)S(1)}) custom-call(bf16[32,4096]{1,0:T(8,128)(2,1)} %collective-permute-done.14.refs_0_, bf16[256,4096]{1,0:T(8,128)(2,1)S(1)} %get-tuple-element.233.refs_1_, bf16[4096,256]{1,0:T(8,128)(2,1)S(1)} %get-tuple-element.234.refs_2_, ...), custom_call_target="tpu_custom_call", output_to_operand_aliasing={{0}: (7, {})} | custom-call | flops 1000000000 | bytes 4194304 | tf_op jit(solution)/shard_map/backward_8_1/pallas_call | solution.py:51
  106.5 1.3 collective-permute-start.16
  107.8 1.5 collective-permute-done.17.refs_0_
  109.3 1.3 collective-permute-start.19
  110.6 1.5 collective-permute-done.16.refs_0_
  112.1 1.3 collective-permute-start.18
  113.4 7.9 %collective-permute-done.19.refs_0_ = bf16[32,4096]{1,0:T(8,128)(2,1)S(1)} collective-permute-done((bf16[32,4096]{1,0:T(8,128)(2,1)S(1)}, bf16[32,4096]{1,0:T(8,128)(2,1)S(1)}, u32[]{:S(2)}, u32[]{:S(2)}) %collective-permute-start.19) | collective-permute-done | bytes 262176 | tf_op jit(solution)/shard_map/ppermute | solution.py:162
  121.3 1.5 backward_10_0.1
  122.8 5.2 %collective-permute-start.21 = (bf16[32,4096]{1,0:T(8,128)(2,1)S(1)}, bf16[32,4096]{1,0:T(8,128)(2,1)S(1)}, u32[]{:S(2)}, u32[]{:S(2)}) collective-permute-start(bf16[32,4096]{1,0:T(8,128)(2,1)S(1)} %get-tuple-element.259), channel_id=1, source_target_pairs={{32,16},{80,96},{33,17},{81,97},{34,18},{82,98},{35,19},{83,99},{3... | collective-permute-start | bytes 786440 | tf_op jit(solution)/shard_map/ppermute | solution.py:162
  128.0 1.5 backward_10_1.1
  129.6 1.3 collective-permute-start.20
  130.9 1.0 collective-permute-done.21.refs_0_
  131.9 0.7 backward_11_0.1
  133.3 1.5 collective-permute-done.20.refs_0_
  134.8 0.7 backward_11_1.1
  135.5 1.4 collective-permute-start.22
  136.9 1.6 copy-done.1
  138.5 1.0 backward_12_1.1
  139.5 15.3 %conditional.5 = (bf16[8,64,768]{2,1,0:T(8,128)(2,1)}) conditional(s32[]{:T(128)} %convert_element_type.29, bf16[8,64,768]{2,1,0:T(8,128)(2,1)} %copy-done.6, bf16[8,64,768]{2,1,0:T(8,128)(2,1)} %copy-done.6), branch_computations={%region_4.5_spmd, %region_5.6_spmd} | conditional | bytes 3145736 | solution.py:522
  139.5 1.2 copy.130
  140.8 14.0 %all_to_all.19 = bf16[8,64,768]{2,1,0:T(8,128)(2,1)} all-to-all(bf16[8,64,768]{2,1,0:T(8,128)(2,1)S(1)} %copy.130), channel_id=1, replica_groups={{0,2,4,6,8,10,12,14},{1,3,5,7,9,11,13,15},{16,18,20,22,24,26,28,30},{17..., dimensions={0} | all-to-all | bytes 1572864 | tf_op jit(solution)/shard_map/cond/branch_1_fun/all_to_all | solution.py:165
  154.7 12.6 %all_to_all.20.refs_2_ = bf16[8,64,768]{2,1,0:T(8,128)(2,1)S(1)} all-to-all(bf16[8,64,768]{2,1,0:T(8,128)(2,1)S(1)} %backward_12_1.1), channel_id=1, replica_groups={{0,2,4,6,8,10,12,14},{1,3,5,7,9,11,13,15},{16,18,20,22,24,26,28,30},{17..., dimensions={0} | all-to-all | bytes 1572864 | tf_op jit(solution)/shard_map/all_to_all | solution.py:165
  167.4 2.4 %products.1 = (f32[2,2,256,256]{3,2,1,0:T(8,128)S(1)}, bf16[2,2,256,256]{3,2,1,0:T(8,128)(2,1)S(1)}) custom-call(bf16[8,64,768]{2,1,0:T(8,128)(2,1)} %copy-done.9, bf16[8,128,768]{2,1,0:T(8,128)(2,1)S(1)} %copy-done.8, bf16[8,64,768]{2,1,0:T(8,128)(2,1)S(1)} %all_to_all.20.refs_2_, bf16[8,64,768]{2,1,0:T(8,128)(2,1)} %get-tuple-element.275.refs_3_), custom_call_target="tpu_custom_call" | custom-call | flops 1000000000 | bytes 4194304 | tf_op jit(solution)/shard_map/products/pallas_call | solution.py:51
  169.9 1.9 %collective-permute-done.24 = bf16[2,2,256,256]{3,2,1,0:T(8,128)(2,1)S(1)} collective-permute-done((bf16[2,2,256,256]{3,2,1,0:T(8,128)(2,1)S(1)}, bf16[2,2,256,256]{3,2,1,0:T(8,128)(2,1)S(1)}, u32[]{:S(2)}, u32[]{:S(2)}) %collective-permute-start.24) | collective-permute-done | bytes 524320 | tf_op jit(solution)/shard_map/ppermute | solution.py:563
  172.1 10.7 %collective-permute-done.25 = bf16[2,256,256]{2,1,0:T(8,128)(2,1)S(1)} collective-permute-done((bf16[2,256,256]{2,1,0:T(8,128)(2,1)S(1)}, bf16[2,256,256]{2,1,0:T(8,128)(2,1)S(1)}, u32[]{:S(2)}, u32[]{:S(2)}) %collective-permute-start.25) | collective-permute-done | bytes 262176 | tf_op jit(solution)/shard_map/ppermute | solution.py:565
  182.9 1.5 multiply_reduce_fusion
  (58 shorter events, 2.3 us)
Async XLA Ops:
  0.6 3.8 %copy-start.4 = (bf16[2,64,4096]{2,1,0:T(8,128)(2,1)S(1)}, bf16[2,64,4096]{2,1,0:T(8,128)(2,1)}, u32[]{:S(2)}) copy-start(bf16[2,64,4096]{2,1,0:T(8,128)(2,1)} %refs_0_.3) | copy-start | bytes 3145732
  3.7 1.4 collective-permute-start.1
  4.5 2.0 %collective-permute-start = (bf16[32,4096]{1,0:T(8,128)(2,1)S(1)}, bf16[32,4096]{1,0:T(8,128)(2,1)S(1)}, u32[]{:S(2)}, u32[]{:S(2)}) collective-permute-start(bf16[32,4096]{1,0:T(8,128)(2,1)S(1)} %get-tuple-element.150), channel_id=1, source_target_pairs={{0,16},{112,96},{1,17},{113,97},{2,18},{114,98},{3,19},{115,99},{4... | collective-permute-start | bytes 786440 | tf_op jit(solution)/shard_map/ppermute | solution.py:162
  5.2 19.2 %collective-permute-start.3 = (bf16[32,4096]{1,0:T(8,128)(2,1)S(1)}, bf16[32,4096]{1,0:T(8,128)(2,1)S(1)}, u32[]{:S(2)}, u32[]{:S(2)}) collective-permute-start(bf16[32,4096]{1,0:T(8,128)(2,1)S(1)} %get-tuple-element.169), channel_id=1, source_target_pairs={{16,32},{96,80},{17,33},{97,81},{18,34},{98,82},{19,35},{99,83},{2... | collective-permute-start | bytes 786440 | tf_op jit(solution)/shard_map/ppermute | solution.py:162
  6.6 23.4 %collective-permute-start.2 = (bf16[32,4096]{1,0:T(8,128)(2,1)S(1)}, bf16[32,4096]{1,0:T(8,128)(2,1)S(1)}, u32[]{:S(2)}, u32[]{:S(2)}) collective-permute-start(bf16[32,4096]{1,0:T(8,128)(2,1)S(1)} %get-tuple-element.163), channel_id=1, source_target_pairs={{16,32},{96,80},{17,33},{97,81},{18,34},{98,82},{19,35},{99,83},{2... | collective-permute-start | bytes 786440 | tf_op jit(solution)/shard_map/ppermute | solution.py:162
  9.0 3.8 %copy-start.9 = (bf16[8,64,768]{2,1,0:T(8,128)(2,1)}, bf16[8,64,768]{2,1,0:T(8,128)(2,1)S(1)}, u32[]{:S(2)}) copy-start(bf16[8,64,768]{2,1,0:T(8,128)(2,1)S(1)} %get-tuple-element.273.refs_0_) | copy-start | bytes 2359300
  26.0 6.9 %collective-permute-start.5 = (bf16[32,4096]{1,0:T(8,128)(2,1)S(1)}, bf16[32,4096]{1,0:T(8,128)(2,1)S(1)}, u32[]{:S(2)}, u32[]{:S(2)}) collective-permute-start(bf16[32,4096]{1,0:T(8,128)(2,1)S(1)} %get-tuple-element.180), channel_id=1, source_target_pairs={{32,48},{80,64},{33,49},{81,65},{34,50},{82,66},{35,51},{83,67},{3... | collective-permute-start | bytes 786440 | tf_op jit(solution)/shard_map/ppermute | solution.py:162
  31.6 6.0 %collective-permute-start.4 = (bf16[32,4096]{1,0:T(8,128)(2,1)S(1)}, bf16[32,4096]{1,0:T(8,128)(2,1)S(1)}, u32[]{:S(2)}, u32[]{:S(2)}) collective-permute-start(bf16[32,4096]{1,0:T(8,128)(2,1)S(1)} %get-tuple-element.176), channel_id=1, source_target_pairs={{32,48},{80,64},{33,49},{81,65},{34,50},{82,66},{35,51},{83,67},{3... | collective-permute-start | bytes 786440 | tf_op jit(solution)/shard_map/ppermute | solution.py:162
  33.0 9.3 %collective-permute-start.7 = (bf16[32,4096]{1,0:T(8,128)(2,1)S(1)}, bf16[32,4096]{1,0:T(8,128)(2,1)S(1)}, u32[]{:S(2)}, u32[]{:S(2)}) collective-permute-start(bf16[32,4096]{1,0:T(8,128)(2,1)S(1)} %get-tuple-element.192), channel_id=1, source_target_pairs={{48,32},{64,80},{49,33},{65,81},{50,34},{66,82},{51,35},{67,83},{5... | collective-permute-start | bytes 786440 | tf_op jit(solution)/shard_map/ppermute | solution.py:162
  37.6 13.8 %collective-permute-start.6 = (bf16[32,4096]{1,0:T(8,128)(2,1)S(1)}, bf16[32,4096]{1,0:T(8,128)(2,1)S(1)}, u32[]{:S(2)}, u32[]{:S(2)}) collective-permute-start(bf16[32,4096]{1,0:T(8,128)(2,1)S(1)} %get-tuple-element.191), channel_id=1, source_target_pairs={{48,32},{64,80},{49,33},{65,81},{50,34},{66,82},{51,35},{67,83},{5... | collective-permute-start | bytes 786440 | tf_op jit(solution)/shard_map/ppermute | solution.py:162
  43.8 13.8 %collective-permute-start.9 = (bf16[32,4096]{1,0:T(8,128)(2,1)S(1)}, bf16[32,4096]{1,0:T(8,128)(2,1)S(1)}, u32[]{:S(2)}, u32[]{:S(2)}) collective-permute-start(bf16[32,4096]{1,0:T(8,128)(2,1)S(1)} %get-tuple-element.200), channel_id=1, source_target_pairs={{32,16},{80,96},{33,17},{81,97},{34,18},{82,98},{35,19},{83,99},{3... | collective-permute-start | bytes 786440 | tf_op jit(solution)/shard_map/ppermute | solution.py:162
  53.0 7.4 %collective-permute-start.8 = (bf16[32,4096]{1,0:T(8,128)(2,1)S(1)}, bf16[32,4096]{1,0:T(8,128)(2,1)S(1)}, u32[]{:S(2)}, u32[]{:S(2)}) collective-permute-start(bf16[32,4096]{1,0:T(8,128)(2,1)S(1)} %get-tuple-element.199), channel_id=1, source_target_pairs={{32,16},{80,96},{33,17},{81,97},{34,18},{82,98},{35,19},{83,99},{3... | collective-permute-start | bytes 786440 | tf_op jit(solution)/shard_map/ppermute | solution.py:162
  57.6 5.6 %collective-permute-start.11 = (bf16[32,4096]{1,0:T(8,128)(2,1)S(1)}, bf16[32,4096]{1,0:T(8,128)(2,1)S(1)}, u32[]{:S(2)}, u32[]{:S(2)}) collective-permute-start(bf16[32,4096]{1,0:T(8,128)(2,1)S(1)} %get-tuple-element.210), channel_id=1, source_target_pairs={{16,0},{96,112},{17,1},{97,113},{18,2},{98,114},{19,3},{99,115},{2... | collective-permute-start | bytes 786440 | tf_op jit(solution)/shard_map/ppermute | solution.py:162
  60.5 2.8 %copy-start.3 = (bf16[2,64,4096]{2,1,0:T(8,128)(2,1)S(1)}, bf16[2,64,4096]{2,1,0:T(8,128)(2,1)}, u32[]{:S(2)}) copy-start(bf16[2,64,4096]{2,1,0:T(8,128)(2,1)} %refs_1_.6) | copy-start | bytes 3145732
  60.5 3.6 %collective-permute-start.10 = (bf16[32,4096]{1,0:T(8,128)(2,1)S(1)}, bf16[32,4096]{1,0:T(8,128)(2,1)S(1)}, u32[]{:S(2)}, u32[]{:S(2)}) collective-permute-start(bf16[32,4096]{1,0:T(8,128)(2,1)S(1)} %get-tuple-element.207), channel_id=1, source_target_pairs={{16,0},{96,112},{17,1},{97,113},{18,2},{98,114},{19,3},{99,115},{2... | collective-permute-start | bytes 786440 | tf_op jit(solution)/shard_map/ppermute | solution.py:162
  63.3 1.4 collective-permute-start.13
  64.1 2.7 %collective-permute-start.12 = (bf16[32,4096]{1,0:T(8,128)(2,1)S(1)}, bf16[32,4096]{1,0:T(8,128)(2,1)S(1)}, u32[]{:S(2)}, u32[]{:S(2)}) collective-permute-start(bf16[32,4096]{1,0:T(8,128)(2,1)S(1)} %get-tuple-element.217), channel_id=1, source_target_pairs={{0,16},{112,96},{1,17},{113,97},{2,18},{114,98},{3,19},{115,99},{4... | collective-permute-start | bytes 786440 | tf_op jit(solution)/shard_map/ppermute | solution.py:162
  65.5 35.5 %collective-permute-start.15 = (bf16[32,4096]{1,0:T(8,128)(2,1)}, bf16[32,4096]{1,0:T(8,128)(2,1)S(1)}, u32[]{:S(2)}, u32[]{:S(2)}) collective-permute-start(bf16[32,4096]{1,0:T(8,128)(2,1)} %get-tuple-element.239), channel_id=1, source_target_pairs={{16,32},{96,80},{17,33},{97,81},{18,34},{98,82},{19,35},{99,83},{2... | collective-permute-start | bytes 786440 | tf_op jit(solution)/shard_map/ppermute | solution.py:162
  67.6 36.3 %collective-permute-start.14 = (bf16[32,4096]{1,0:T(8,128)(2,1)}, bf16[32,4096]{1,0:T(8,128)(2,1)}, u32[]{:S(2)}, u32[]{:S(2)}) collective-permute-start(bf16[32,4096]{1,0:T(8,128)(2,1)} %get-tuple-element.230), channel_id=1, source_target_pairs={{16,32},{96,80},{17,33},{97,81},{18,34},{98,82},{19,35},{99,83},{2... | collective-permute-start | bytes 786440 | tf_op jit(solution)/shard_map/ppermute | solution.py:162
  91.6 1.2 copy-start.7
  92.7 8.3 %copy-start.2 = (bf16[8,64,768]{2,1,0:T(8,128)(2,1)S(1)}, bf16[8,64,768]{2,1,0:T(8,128)(2,1)}, u32[]{:S(2)}) copy-start(bf16[8,64,768]{2,1,0:T(8,128)(2,1)} %get-tuple-element.240.refs_7_) | copy-start | bytes 2359300
  101.0 33.7 %copy-start = (bf16[4096,256]{1,0:T(8,128)(2,1)}, bf16[4096,256]{1,0:T(8,128)(2,1)S(1)}, u32[]{:S(2)}) copy-start(bf16[4096,256]{1,0:T(8,128)(2,1)S(1)} %get-tuple-element.244.refs_7_.refs_2_) | copy-start | bytes 6291460
  102.6 6.7 %collective-permute-start.17 = (bf16[32,4096]{1,0:T(8,128)(2,1)S(1)}, bf16[32,4096]{1,0:T(8,128)(2,1)S(1)}, u32[]{:S(2)}, u32[]{:S(2)}) collective-permute-start(bf16[32,4096]{1,0:T(8,128)(2,1)S(1)} %get-tuple-element.248), channel_id=1, source_target_pairs={{32,48},{80,64},{33,49},{81,65},{34,50},{82,66},{35,51},{83,67},{3... | collective-permute-start | bytes 786440 | tf_op jit(solution)/shard_map/ppermute | solution.py:162
  103.9 5.3 %copy-start.5 = (bf16[8,64,768]{2,1,0:T(8,128)(2,1)S(1)}, bf16[8,64,768]{2,1,0:T(8,128)(2,1)}, u32[]{:S(2)}) copy-start(bf16[8,64,768]{2,1,0:T(8,128)(2,1)} %get-tuple-element.250.refs_13_) | copy-start | bytes 2359300
  106.5 5.6 %collective-permute-start.16 = (bf16[32,4096]{1,0:T(8,128)(2,1)S(1)}, bf16[32,4096]{1,0:T(8,128)(2,1)S(1)}, u32[]{:S(2)}, u32[]{:S(2)}) collective-permute-start(bf16[32,4096]{1,0:T(8,128)(2,1)S(1)} %get-tuple-element.242), channel_id=1, source_target_pairs={{32,48},{80,64},{33,49},{81,65},{34,50},{82,66},{35,51},{83,67},{3... | collective-permute-start | bytes 786440 | tf_op jit(solution)/shard_map/ppermute | solution.py:162
  109.3 12.0 %collective-permute-start.19 = (bf16[32,4096]{1,0:T(8,128)(2,1)S(1)}, bf16[32,4096]{1,0:T(8,128)(2,1)S(1)}, u32[]{:S(2)}, u32[]{:S(2)}) collective-permute-start(bf16[32,4096]{1,0:T(8,128)(2,1)S(1)} %get-tuple-element.254), channel_id=1, source_target_pairs={{48,32},{64,80},{49,33},{65,81},{50,34},{66,82},{51,35},{67,83},{5... | collective-permute-start | bytes 786440 | tf_op jit(solution)/shard_map/ppermute | solution.py:162
  112.1 15.9 %collective-permute-start.18 = (bf16[32,4096]{1,0:T(8,128)(2,1)S(1)}, bf16[32,4096]{1,0:T(8,128)(2,1)S(1)}, u32[]{:S(2)}, u32[]{:S(2)}) collective-permute-start(bf16[32,4096]{1,0:T(8,128)(2,1)S(1)} %get-tuple-element.253), channel_id=1, source_target_pairs={{48,32},{64,80},{49,33},{65,81},{50,34},{66,82},{51,35},{67,83},{5... | collective-permute-start | bytes 786440 | tf_op jit(solution)/shard_map/ppermute | solution.py:162
  122.8 9.1 %collective-permute-start.21 = (bf16[32,4096]{1,0:T(8,128)(2,1)S(1)}, bf16[32,4096]{1,0:T(8,128)(2,1)S(1)}, u32[]{:S(2)}, u32[]{:S(2)}) collective-permute-start(bf16[32,4096]{1,0:T(8,128)(2,1)S(1)} %get-tuple-element.259), channel_id=1, source_target_pairs={{32,16},{80,96},{33,17},{81,97},{34,18},{82,98},{35,19},{83,99},{3... | collective-permute-start | bytes 786440 | tf_op jit(solution)/shard_map/ppermute | solution.py:162
  129.6 3.0 %copy-start.6 = (bf16[8,64,768]{2,1,0:T(8,128)(2,1)}, bf16[8,64,768]{2,1,0:T(8,128)(2,1)S(1)}, u32[]{:S(2)}) copy-start(bf16[8,64,768]{2,1,0:T(8,128)(2,1)S(1)} %get-tuple-element.267) | copy-start | bytes 2359300
  129.6 5.2 %collective-permute-start.20 = (bf16[32,4096]{1,0:T(8,128)(2,1)S(1)}, bf16[32,4096]{1,0:T(8,128)(2,1)S(1)}, u32[]{:S(2)}, u32[]{:S(2)}) collective-permute-start(bf16[32,4096]{1,0:T(8,128)(2,1)S(1)} %get-tuple-element.257), channel_id=1, source_target_pairs={{32,16},{80,96},{33,17},{81,97},{34,18},{82,98},{35,19},{83,99},{3... | collective-permute-start | bytes 786440 | tf_op jit(solution)/shard_map/ppermute | solution.py:162
  132.6 4.3 %collective-permute-start.23 = (bf16[32,4096]{1,0:T(8,128)(2,1)}, bf16[32,4096]{1,0:T(8,128)(2,1)S(1)}, u32[]{:S(2)}, u32[]{:S(2)}) collective-permute-start(bf16[32,4096]{1,0:T(8,128)(2,1)} %get-tuple-element.263), channel_id=1, source_target_pairs={{16,0},{96,112},{17,1},{97,113},{18,2},{98,114},{19,3},{99,115},{2... | collective-permute-start | bytes 786440 | tf_op jit(solution)/shard_map/ppermute | solution.py:162
  135.5 3.0 %collective-permute-start.22 = (bf16[32,4096]{1,0:T(8,128)(2,1)}, bf16[32,4096]{1,0:T(8,128)(2,1)}, u32[]{:S(2)}, u32[]{:S(2)}) collective-permute-start(bf16[32,4096]{1,0:T(8,128)(2,1)} %get-tuple-element.262), channel_id=1, source_target_pairs={{16,0},{96,112},{17,1},{97,113},{18,2},{98,114},{19,3},{99,115},{2... | collective-permute-start | bytes 786440 | tf_op jit(solution)/shard_map/ppermute | solution.py:162
  136.9 1.6 copy-start.1
  139.5 27.9 %copy-start.8 = (bf16[8,128,768]{2,1,0:T(8,128)(2,1)S(1)}, bf16[8,128,768]{2,1,0:T(8,128)(2,1)}, u32[]{:S(2)}) copy-start(bf16[8,128,768]{2,1,0:T(8,128)(2,1)} %copy-done.7) | copy-start | bytes 4718596
  169.8 2.3 %slice-start.1 = ((f32[2,4096]{1,0:T(2,128)}), f32[1,4096]{1,0:T(1,128)S(1)}, s32[]{:S(2)}) async-start(f32[2,4096]{1,0:T(2,128)} %refs_3_.1), calls=%async_computation.5 | async-start | bytes 32768 | tf_op jit(solution)/shard_map/slice | solution.py:567
  169.8 2.0 %collective-permute-start.24 = (bf16[2,2,256,256]{3,2,1,0:T(8,128)(2,1)S(1)}, bf16[2,2,256,256]{3,2,1,0:T(8,128)(2,1)S(1)}, u32[]{:S(2)}, u32[]{:S(2)}) collective-permute-start(bf16[2,2,256,256]{3,2,1,0:T(8,128)(2,1)S(1)} %get-tuple-element.269), channel_id=1, source_target_pairs={{0,1},{1,0},{2,3},{3,2},{4,5},{5,4},{6,7},{7,6},{8,9},{9,8},{10,11... | collective-permute-start | bytes 1572872 | tf_op jit(solution)/shard_map/ppermute | solution.py:563
  172.0 10.8 %collective-permute-start.25 = (bf16[2,256,256]{2,1,0:T(8,128)(2,1)S(1)}, bf16[2,256,256]{2,1,0:T(8,128)(2,1)S(1)}, u32[]{:S(2)}, u32[]{:S(2)}) collective-permute-start(bf16[2,256,256]{2,1,0:T(8,128)(2,1)S(1)} %fusion.1), channel_id=1, source_target_pairs={{0,112},{16,96},{32,80},{48,64},{64,48},{80,32},{96,16},{112,0},{1... | collective-permute-start | bytes 786440 | tf_op jit(solution)/shard_map/ppermute | solution.py:565
  172.1 10.8 %slice-start = ((bf16[2,4096,256]{2,1,0:T(8,128)(2,1)}), bf16[1,4096,256]{2,1,0:T(8,128)(2,1)S(1)}, s32[]{:S(2)}) async-start(bf16[2,4096,256]{2,1,0:T(8,128)(2,1)} %refs_0_.5), calls=%async_computation.4 | async-start | bytes 4194304 | tf_op jit(solution)/shard_map/slice | solution.py:568
where the time goes:
time: 188 us; the launch traced here: 184 us
  waiting for transfers between devices  51.9 us (28%)
  blocking collectives  49.3 us (26%)
  starting transfers between devices  37.5 us (20%)
  Pallas kernels  37.4 us (20%)
  local copies, waits for them, and re-layouts  5.22 us (3%)
    all_to_all x3, blocking collectives, exchange(): lax.all_to_all(array, 'dp', 0, 0, axis_index_groups=same_core, tiled=False)  49.3 us
    ppermute x24, waiting for transfers between devices, send_on(): return lax.ppermute(sent, 'section', pairs)  39.3 us
    pallas_call x30, Pallas kernels, call(): pl.pallas_call(kernel, out_shape=tuple(shapes), in_specs=[spec for _, spe...  37.4 us
    ppermute x24, starting transfers between devices, send_on(): return lax.ppermute(sent, 'section', pairs)  37.4 us
    ppermute x1, waiting for transfers between devices, on_device(): lax.ppermute(total[1].astype(bf16), 'section', mirror).astype(f32)  10.7 us
  transfers between devices with their start and end apart: 26, of which 13 were waited for; matrix products, arithmetic and copies ran while one was open for 1% of the time, Pallas kernels for 17%

commit v1 on v0

v1 whole, which is shorter than its diff:
```python
import functools

import jax
import jax.numpy as jnp
from jax import lax
from jax.experimental import pallas as pl
from jax.experimental.pallas import tpu as pltpu
from jax.sharding import PartitionSpec as P

epsilon = 1e-05
STAGES = (0, 1, 2, 3, 2, 1, 0, 1, 2, 3, 2, 1, 0)
LAST = len(STAGES) - 1
MICROS = 2
bf16 = jnp.bfloat16
f32 = jnp.float32
VMEM = pl.BlockSpec(memory_space=pltpu.VMEM)
HBM = pl.BlockSpec(memory_space=pltpu.HBM)
LOADS = 4
MIB = 2**20


def matmul(left, right):
    return jnp.dot(left, right, preferred_element_type=f32)


def transposed_matmul(left, right):
    return lax.dot_general(left, right, (((0,), (0,)), ((), ())), preferred_element_type=f32)


def place():
    sections = lax.axis_size("section")
    position = lax.axis_index("section")
    half = (position >= sections // 2).astype(jnp.int32)
    fold = jnp.where(half == 0, position, sections - 1 - position)
    return fold, half


def call(body, name, reads, updates=(), places=(), new=(), scratch=(), limit=16):
    n_read, n_update, n_place = len(reads), len(updates), len(places)

    def kernel(*refs):
        ins, outs = refs[: n_read + n_update + n_place], refs[n_read + n_update + n_place :]
        for old, now in zip(ins[n_read : n_read + n_update], outs):
            now[...] = old[...]
        body(ins[:n_read], *outs)

    shapes = [pltpu.VMEM(a.shape, a.dtype) for a in updates]
    shapes += [pltpu.HBM(a.shape, a.dtype) for a in places]
    shapes += list(new)
    kept = [VMEM] * n_update + [HBM] * n_place
    return pl.pallas_call(
        kernel,
        out_shape=tuple(shapes),
        in_specs=[spec for _, spec in reads] + kept,
        out_specs=tuple(kept + [VMEM] * len(new)),
        input_output_aliases={n_read + i: i for i in range(n_update + n_place)},
        scratch_shapes=list(scratch),
        compiler_params=pltpu.CompilerParams(vmem_limit_bytes=limit * MIB),
        cost_estimate=pl.CostEstimate(flops=10**9, bytes_accessed=4 * MIB, transcendentals=0),
        name=name,
    )(*[a for a, _ in reads], *updates, *places)


def load(copy, sources, targets, sems):
    waits = []
    for which, (source, target) in enumerate(zip(sources, targets)):
        size = source.shape[1] // LOADS
        pieces = []
        for i in range(LOADS):
            part = pl.ds(i * size, size)
            pieces.append(
                pltpu.make_async_copy(
                    source.at[copy, part], target.at[part], sems.at[which * LOADS + i]
                )
            )
        for piece in pieces:
            piece.start()
        waits.append(pieces)
    return waits


def wait_all(pieces):
    for piece in pieces:
        piece.wait()


def forward(source, gain, weight_in, weight_out, out, ready=None):
    chips = out.rows.shape[0]
    micro, width = source.shape
    branch = weight_in.shape[1]
    chunk = width // chips
    wide = source.astype(f32)
    scaling = lax.rsqrt(jnp.mean(wide * wide, axis=-1, keepdims=True) + epsilon)
    normal = wide * scaling
    if ready is not None:
        wait_all(ready[0])
    before = matmul((normal * gain[...]).astype(bf16), weight_in[...])
    inner = (before * jax.nn.sigmoid(before)).astype(bf16)
    out.kept[:, :branch] = before
    out.kept[:, branch:] = jnp.broadcast_to(scaling, (micro, 128))
    for chip in range(chips):
        out.rows[chip, :, :chunk] = normal[:, chip * chunk : (chip + 1) * chunk].astype(bf16)
        out.rows[chip, :, chunk:] = inner
    out.start()
    if ready is not None:
        wait_all(ready[1])
    if weight_out is not None:
        return (wide + matmul(inner, weight_out[...])).astype(bf16)


def backward(grad, gain, weight_in_t, weight_out_t, out, saved, hats):
    chips = out.rows.shape[0]
    width = grad.shape[1]
    branch = weight_in_t.shape[0]
    chunk = width // chips
    d_inner = matmul(grad, weight_out_t[...])
    kept = saved()
    before = kept[:, :branch]
    sigma = jax.nn.sigmoid(before)
    delta = (d_inner * sigma * (1.0 + before * (1.0 - sigma))).astype(bf16)
    for chip in range(chips):
        out.rows[chip, :, :chunk] = grad[:, chip * chunk : (chip + 1) * chunk]
        out.rows[chip, :, chunk:] = delta
    out.start()
    if hats is None:
        return None
    mixed = jnp.sum(delta.astype(f32) * before, axis=-1, keepdims=True) / width
    scaled = matmul(delta, weight_in_t[...]) * gain[...]
    scaling = kept[:, branch : branch + 1]
    result = []
    for chip in range(chips):
        part = slice(chip * chunk, (chip + 1) * chunk)
        normal = hats(chip).astype(f32)
        result.append(
            (grad[:, part].astype(f32) + scaling * (scaled[:, part] - normal * mixed)).astype(bf16)
        )
    return jnp.concatenate(result, axis=1)


def on_device(inputs, cotangent, w_in, w_out, gain):
    sections = lax.axis_size("section")
    parts = lax.axis_size("dp")
    chips = parts // 2
    rows, width = inputs.shape[1:]
    micro = rows // MICROS
    branch = w_in.shape[2]
    chunk = width // chips
    pack = chunk + branch

    def in_hbm(array):
        return pltpu.with_memory_space_constraint(array, pltpu.HBM)

    raw_in, raw_out = w_in, w_out
    inputs, cotangent, w_in, w_out = map(in_hbm, (inputs, cotangent, w_in, w_out))
    dma = pltpu.SemaphoreType.DMA
    block = pltpu.VMEM((micro, width), bf16)
    packed = pltpu.VMEM((chips, micro, pack), bf16)
    in_shape, out_shape = pltpu.VMEM((width, branch), bf16), pltpu.VMEM((branch, width), bf16)
    in_turned, out_turned = out_shape, in_shape
    row_shape = pltpu.VMEM((1, width), f32)
    load_sems = dma((2 * LOADS,))
    fold_here, _ = place()
    same_core = [list(range(core, parts, 2)) for core in range(2)]

    def of_micro(m):
        return pl.ds(m * micro, micro)

    def send_on(sent, stage):
        a, b = STAGES[stage], STAGES[stage + 1]
        pairs = [(a, b), (sections - 1 - a, sections - 1 - b)]
        return lax.ppermute(sent, "section", pairs)

    def copy_kernel(reads, target, sems):
        copies = [
            pltpu.make_async_copy(reads[0].at[chip], target.at[chip], sems.at[chip])
            for chip in range(chips)
        ]
        for copy in copies:
            copy.start()
        wait_all(copies)

    def exchange(array, keep_in_vmem=False):
        array = lax.all_to_all(array, "dp", 0, 0, axis_index_groups=same_core, tiled=False)
        if keep_in_vmem:
            return array
        array = pltpu.with_memory_space_constraint(array, pltpu.VMEM)
        (target,) = new_boxes("unstage_box", [array.shape])
        (target,) = call(copy_kernel, "unstage", [(array, VMEM)], places=(target,), scratch=[dma((chips,))])
        return target

    def new_boxes(name, shapes):
        shapes = [pltpu.HBM(shape, bf16) for shape in shapes]
        return pl.pallas_call(
            lambda *refs: None, out_shape=tuple(shapes), out_specs=(HBM,) * len(shapes), name=name
        )()

    def in_vmem(*arrays):
        return [(a, VMEM) for a in arrays]

    (box_early,) = new_boxes("box_early", [(chips, rows, pack)])
    box_two, box_far = new_boxes("box_far", [(chips, rows, pack), (chips, 2 * rows, pack)])
    box_near, box_one = new_boxes("box_near", [(chips, 2 * rows, pack), (chips, rows, pack)])
    box_late, box_late_two, box_end = new_boxes(
        "box_late", [(chips, n * rows, pack) for n in (2, 3, 1)]
    )
    (hats,) = new_boxes("hats", [(chips, 2 * rows, chunk)])

    def start_kernel(reads, box, kept, sent, gain, weight_in, weight_out, staged, sem, load_sems, *scratch):
        inputs, source_in, source_out, source_gain = reads
        fold, half = place()

        @pl.when(fold <= 1)
        def _():
            ready = load(half, (source_in, source_out), (weight_in, weight_out), load_sems)
            gain[...] = source_gain[pl.ds(half, 1), :]

            @pl.when(fold == STAGES[0])
            def _():
                copy = pltpu.make_async_copy(inputs.at[half, of_micro(0)], staged, sem)
                copy.start()
                copy.wait()
                out = Keeper(0, scratch, box, layer=0, kept=kept)
                sent[...] = forward(staged[...], gain, weight_in, weight_out, out, ready)
                out.wait()

            @pl.when(fold != STAGES[0])
            def _():
                wait_all(ready[0] + ready[1])

    class Keeper:
        def __init__(self, m, scratch, box, slot=0, layer=0, hats=None, kept=None):
            self.rows, self.kept, sems = scratch
            own = pl.ds(layer * rows + m * micro, micro)
            at = pl.ds(slot * rows + m * micro, micro)
            pairs = [(self.rows, box.at[:, at, :])]
            if hats is not None:
                pairs.append((self.rows.at[:, :, pl.ds(0, chunk)], hats.at[:, own, :]))
            if kept is not None:
                pairs.append((self.kept, kept.at[own, :]))
            self.copies = [
                pltpu.make_async_copy(source, target, sems.at[i])
                for i, (source, target) in enumerate(pairs)
            ]

        def start(self):
            for copy in self.copies:
                copy.start()

        def wait(self):
            wait_all(self.copies)

    kept_shape = pltpu.HBM((2 * rows, branch + 128), f32)
    kept_block = pltpu.VMEM((micro, branch + 128), f32)
    (kept,) = pl.pallas_call(
        lambda *refs: None, out_shape=(kept_shape,), out_specs=(HBM,), name="kept"
    )()

    copies = 3

    def keeping(n=1):
        return [
            pltpu.VMEM((n, chips, micro, pack), bf16),
            pltpu.VMEM((n, micro, branch + 128), f32),
            dma((n, copies)),
        ]

    keeping_one = [packed, kept_block, dma((copies,))]
    moved = [None] * MICROS
    box_early, kept, sent, *weights_1 = call(
        start_kernel,
        "forward_0_0",
        [(inputs, HBM), (w_in, HBM), (w_out, HBM), (gain, VMEM)],
        places=(box_early, kept),
        new=(block, row_shape, in_shape, out_shape),
        scratch=[block, dma(()), load_sems] + keeping_one,
    )
    moved[0] = send_on(sent, 0)
    for m in range(1, MICROS):

        def input_kernel(reads, box, kept, sent, staged, sem, *scratch, m=m):
            inputs, *weights = reads
            fold, half = place()

            @pl.when(fold == STAGES[0])
            def _():
                copy = pltpu.make_async_copy(inputs.at[half, of_micro(m)], staged, sem)
                copy.start()
                copy.wait()
                out = Keeper(m, scratch, box, layer=0, kept=kept)
                sent[...] = forward(staged[...], *weights, out)
                out.wait()

        box_early, kept, sent = call(
            input_kernel,
            "forward_0_%d" % m,
            [(inputs, HBM)] + in_vmem(*weights_1),
            places=(box_early, kept),
            new=(block,),
            scratch=[block, dma(())] + keeping_one,
        )
        moved[m] = send_on(sent, 0)

    def turn(weight_in, weight_out, weight_in_t, weight_out_t):
        @pl.loop(0, width // branch)
        def _(tile):
            part = pl.ds(pl.multiple_of(tile * branch, branch), branch)
            weight_in_t[:, part] = weight_in[part, :].T
            weight_out_t[part, :] = weight_out[:, part].T

    def fresh_weights(name, here, layers, plain, turned):
        def kernel(reads, *refs):
            source_in, source_out, source_gain = reads
            fold, half = place()
            sems, raw = refs[-1], refs[-3:-1]

            @pl.when(here(fold))
            def _():
                waits, at = [], 0
                for i, layer in enumerate(layers):
                    copy = half if layer == 0 else 1 - half
                    gain, *targets = refs[at : at + 1 + 2 * (plain + turned)]
                    at += 1 + 2 * (plain + turned)
                    gain[...] = source_gain[pl.ds(copy, 1), :]
                    loaded = targets[:2] if plain else raw
                    waits.append(load(copy, (source_in, source_out), loaded, sems.at[i]))
                    if turned:
                        wait_all(waits[i][0] + waits[i][1])
                        turn(*loaded, *targets[-2:])
                if not turned:
                    for wait in waits:
                        wait_all(wait[0] + wait[1])

        shapes = (row_shape,) + (in_shape, out_shape) * plain + (in_turned, out_turned) * turned
        outs = call(
            kernel,
            name,
            [(in_hbm(raw_in), HBM), (in_hbm(raw_out), HBM), (gain, VMEM)],
            new=shapes * len(layers),
            scratch=[in_shape, out_shape, dma((len(layers), 2 * LOADS))],
        )
        return [outs[i * len(shapes) : (i + 1) * len(shapes)] for i in range(len(layers))]

    def forward_kernel(stage, slots, m, reads, box, hats, kept, sent, stash, stash_kept, sems):
        moved = reads[0]
        layers = list(slots)
        weights = [reads[1 + 3 * i : 4 + 3 * i] for i in range(len(layers))]
        fold, _ = place()

        @pl.when(fold == STAGES[stage])
        def _():
            outs = [
                Keeper(
                    m,
                    (stash.at[i], stash_kept.at[i], sems.at[i]),
                    box,
                    slot=slots[layer],
                    layer=layer,
                    hats=hats,
                    kept=kept,
                )
                for i, layer in enumerate(layers)
            ]
            for i, out in enumerate(outs):
                source = moved if i == 0 else sent
                sent[...] = forward(source[...], *weights[i], out)
            for out in outs:
                out.wait()

    def forward_stage(stage, slots, box, weights):
        nonlocal hats, kept
        for m in range(MICROS):
            box, hats, kept, sent = call(
                functools.partial(forward_kernel, stage, slots, m),
                "forward_%d_%d" % (stage, m),
                in_vmem(moved[m], *[a for layer in slots for a in weights[layer]]),
                places=(box, hats, kept),
                new=(block,),
                scratch=keeping(len(slots)),
            )
            moved[m] = send_on(sent, stage)
        return box

    box_early = forward_stage(1, {0: 0}, box_early, [weights_1])

    def none(name, array):
        return new_boxes(name, [array.shape])[0]

    box_early, kept = lax.optimization_barrier((box_early, kept))
    got_early = lax.cond(fold_here <= 1, exchange, functools.partial(none, "none_early"), box_early)
    got_early, box_two, box_far, kept, hats, raw_in, raw_out = lax.optimization_barrier(
        (got_early, box_two, box_far, kept, hats, raw_in, raw_out)
    )
    weights = fresh_weights("load_far", lambda fold: fold >= 2, (0, 1), 1, 0)
    box_two = forward_stage(2, {0: 0}, box_two, weights)
    box_far = forward_stage(3, {0: 0, 1: 1}, box_far, weights)
    box_late_two = forward_stage(4, {1: 2}, box_late_two, weights)

    box_two, box_far, kept = lax.optimization_barrier((box_two, box_far, kept))
    got_two, got_far = lax.switch(
        jnp.maximum(fold_here - 1, 0),
        (
            lambda two, far: (none("none_two", two), none("none_far", far)),
            lambda two, far: (exchange(two), none("none_far", far)),
            lambda two, far: (none("none_two", two), exchange(far)),
        ),
        box_two,
        box_far,
    )
    got_two, got_far, box_near, box_one, kept, hats, raw_in, raw_out = lax.optimization_barrier(
        (got_two, got_far, box_near, box_one, kept, hats, raw_in, raw_out)
    )
    (near,) = fresh_weights("load_near", lambda fold: fold <= 1, (1,), 1, 1)
    box_one = forward_stage(5, {1: 0}, box_one, [None, near[:3]])

    def middle_kernel(m, reads, box, kept, sent, staged, sem, stash, stash_kept, sems):
        moved, cotangent, gain, weight_in, weight_in_t, weight_out_t = reads
        fold, half = place()

        @pl.when(fold == STAGES[6])
        def _():
            copy = pltpu.make_async_copy(cotangent.at[half, of_micro(m)], staged, sem)
            copy.start()
            outs = [
                Keeper(m, (stash.at[i], stash_kept.at[0], sems.at[i]), box, slot=i)
                for i in range(2)
            ]
            forward(moved[...], gain, weight_in, None, outs[0])
            copy.wait()
            sent[...] = backward(
                staged[...], gain, weight_in_t, weight_out_t, outs[1], lambda: stash_kept.at[0],
                lambda chip: stash[0, chip, :, :chunk],
            )
            for out in outs:
                out.wait()

    for m in range(MICROS):
        box_near, kept, sent = call(
            functools.partial(middle_kernel, m),
            "middle_%d" % m,
            [(moved[m], VMEM), (cotangent, HBM)] + in_vmem(near[0], near[1], near[3], near[4]),
            places=(box_near, kept),
            new=(block,),
            scratch=[block, dma(())] + keeping(2),
        )
        moved[m] = send_on(sent, 6)

    def saved_rows(name, here, layer):
        def kernel(reads, hats_out, kept_out, sems):
            fold, _ = place()
            at = pl.ds(layer * rows, rows)

            @pl.when(here(fold))
            def _():
                copies = [
                    pltpu.make_async_copy(reads[0].at[chip, at, :], hats_out.at[chip], sems.at[chip])
                    for chip in range(chips)
                ]
                copies.append(pltpu.make_async_copy(reads[1].at[at, :], kept_out, sems.at[chips]))
                for copy in copies:
                    copy.start()
                wait_all(copies)

        return call(
            kernel,
            name,
            [(in_hbm(hats), HBM), (in_hbm(kept), HBM)],
            new=(pltpu.VMEM((chips, rows, chunk), bf16), pltpu.VMEM((rows, branch + 128), f32)),
            scratch=[dma((chips + 1,))],
        )

    def backward_kernel(stage, slots, m, reads, box, kept, *refs):
        moved = reads[0]
        layers = list(slots)
        weights = [reads[1 + 5 * i : 4 + 5 * i] for i in range(len(layers))]
        saved = [reads[4 + 5 * i : 6 + 5 * i] for i in range(len(layers))]
        sent = refs[0] if stage < LAST else None
        stash, stash_kept, sems = refs[-3:]
        fold, _ = place()

        @pl.when(fold == STAGES[stage])
        def _():
            outs = [
                Keeper(m, (stash.at[i], stash_kept.at[i], sems.at[i]), box, slot=slots[layer])
                for i, layer in enumerate(layers)
            ]
            for i, out in enumerate(outs):
                source = moved if i == 0 else sent
                have_hats, have = saved[i]
                result = backward(
                    source[...], *weights[i], out, lambda have=have: have.at[of_micro(m)],
                    (lambda chip, hats=have_hats: hats[chip, of_micro(m), :])
                    if sent is not None
                    else None,
                )
                if sent is not None:
                    sent[...] = result
            for out in outs:
                out.wait()

    def backward_stage(stage, slots, box, weights):
        nonlocal kept
        n = len(slots)
        for m in range(MICROS):
            box, kept, *sent = call(
                functools.partial(backward_kernel, stage, slots, m),
                "backward_%d_%d" % (stage, m),
                in_vmem(moved[m], *[a for layer in slots for a in weights[layer]]) ,
                places=(box, kept),
                new=(block,) if stage < LAST else (),
                scratch=keeping(n),
            )
            if sent:
                moved[m] = send_on(sent[0], stage)
        return box

    saved_2 = saved_rows("saved_near_2", lambda fold: fold == 1, 1)
    box_late = backward_stage(7, {1: 0}, box_late, [None, (near[0], *near[3:], *saved_2)])

    box_near, box_one, kept = lax.optimization_barrier((box_near, box_one, kept))
    got_near, got_one = lax.switch(
        jnp.minimum(fold_here, 2),
        (
            lambda near, one: (exchange(near), none("none_one", one)),
            lambda near, one: (none("none_near", near), exchange(one)),
            lambda near, one: (none("none_near", near), none("none_one", one)),
        ),
        box_near,
        box_one,
    )
    got_near, got_one, box_late, box_late_two, box_end, kept, raw_in, raw_out = lax.optimization_barrier(
        (got_near, got_one, box_late, box_late_two, box_end, kept, raw_in, raw_out)
    )
    (far_2,) = fresh_weights("turn_far_2", lambda fold: fold >= 2, (1,), 0, 1)
    far_2 = (*far_2, *saved_rows("saved_far_2", lambda fold: fold >= 2, 1))
    box_late_two = backward_stage(8, {1: 0}, box_late_two, [None, far_2])
    kept, raw_in, raw_out = lax.optimization_barrier((kept, raw_in, raw_out))
    (far_1,) = fresh_weights("turn_far_1", lambda fold: fold >= 2, (0,), 0, 1)
    far_1 = (*far_1, *saved_rows("saved_far_1", lambda fold: fold >= 2, 0))
    box_late = backward_stage(9, {1: 0, 0: 1}, box_late, [far_1, far_2])
    box_late_two = backward_stage(10, {0: 1}, box_late_two, [far_1])
    kept, raw_in, raw_out = lax.optimization_barrier((kept, raw_in, raw_out))
    (near_1,) = fresh_weights("turn_near_1", lambda fold: fold <= 1, (0,), 0, 1)
    near_1 = (*near_1, *saved_rows("saved_near_1", lambda fold: fold <= 1, 0))
    box_late = backward_stage(11, {0: 1}, box_late, [near_1])
    box_end = backward_stage(LAST, {0: 0}, box_end, [near_1])

    def products(pick, reads, keep, send, whole_in, whole_out):
        _, half = place()
        core = lax.rem(lax.axis_index("dp"), 2)
        mine = pl.ds(pl.multiple_of(core * branch, branch), branch)
        theirs = pl.ds(pl.multiple_of((1 - core) * branch, branch), branch)
        narrow, wide = slice(chunk, pack), slice(0, chunk)

        def part(which, columns):
            box, slot = which
            return reads[box][:, slot * rows : (slot + 1) * rows, columns].reshape(chips * rows, -1)

        for layer, slot in ((0, half), (1, 1 - half)):
            hat, up = pick[layer]
            whole_in[...] = transposed_matmul(part(hat, wide), part(up, narrow))
            whole_out[...] = transposed_matmul(part(hat, narrow), part(up, wide))
            keep[slot, 0] = whole_in[mine, :]
            keep[slot, 1] = whole_out[:, mine]
            send[slot, 0] = whole_in[theirs, :].astype(bf16)
            send[slot, 1] = whole_out[:, theirs].astype(bf16)

    def finish(name, pick, *boxes):
        return call(
            functools.partial(products, pick),
            name,
            in_vmem(*boxes),
            new=(pltpu.VMEM((2, 2, branch, branch), f32), pltpu.VMEM((2, 2, branch, branch), bf16)),
            scratch=[pltpu.VMEM((2 * branch, branch), f32), pltpu.VMEM((branch, 2 * branch), f32)],
        )

    def last(*pick):
        def branch(now, *before):
            arrived = exchange(now, keep_in_vmem=True)
            return finish("products", pick, arrived, *before)

        return branch

    end_0 = last(((1, 0), (0, 0)), ((2, 0), (2, 1)))
    end_1 = last(((1, 0), (0, 1)), ((2, 0), (0, 0)))
    end_2 = last(((1, 0), (0, 1)), ((0, 2), (0, 0)))
    end_3 = last(((1, 0), (0, 1)), ((1, 1), (0, 0)))
    keep, send = lax.switch(
        fold_here,
        (
            lambda end, late, late_two, early, near, one, two, far: end_0(end, early, near),
            lambda end, late, late_two, early, near, one, two, far: end_1(late, early, one),
            lambda end, late, late_two, early, near, one, two, far: end_2(late_two, two),
            lambda end, late, late_two, early, near, one, two, far: end_3(late, far),
        ),
        box_end,
        box_late,
        box_late_two,
        got_early,
        got_near,
        got_one,
        got_two,
        got_far,
    )
    total = keep + lax.ppermute(send, "dp", [(i, i ^ 1) for i in range(parts)]).astype(f32)
    mirror = [(s, sections - 1 - s) for s in range(sections)]
    total = total[0] + lax.ppermute(total[1].astype(bf16), "section", mirror).astype(f32)
    start = lax.axis_index("dp") * branch
    own_gain = lax.dynamic_slice_in_dim(gain[0], start, branch, 0)
    own_in = lax.dynamic_slice_in_dim(raw_in[0], start, branch, 0).astype(f32)
    grad_in = total[0] * own_gain[:, None]
    grad_gain = jnp.sum(total[0] * own_in, axis=1)
    return (grad_in[None], total[1][None], grad_gain[None])


def solution(mesh):
    return jax.shard_map(
        on_device,
        mesh=mesh,
        in_specs=(
            P(None, "dp", None),
            P(None, "dp", None),
            P("section", None, None),
            P("section", None, None),
            P("section", None),
        ),
        out_specs=(P("section", "dp", None), P("section", None, "dp"), P("section", "dp")),
        check_vma=False,
    )
```

time: 188 us -> 194 us (1.032); the launches traced: 184 us -> 193 us
  waiting for transfers between devices: 51.9 us -> 74.3 us
  blocking collectives: 49.3 us -> 38.3 us
  Pallas kernels: 37.4 us -> 31.3 us
  local copies, waits for them, and re-layouts: 5.22 us -> 9.85 us
    ppermute x24, waiting for transfers between devices: 39.3 us -> 51 us  [send_on(): return lax.ppermute(sent, 'section', pairs)]
    all_to_all x3 -> x1, blocking collectives: 49.3 us -> 38.3 us  [exchange(): lax.all_to_all(array, 'dp', 0, 0, axis_index_groups=same_core, tiled=False)]
    all_to_all x0 -> x1, waiting for transfers between devices: none -> 10.7 us  [exchange(): lax.all_to_all(array, 'dp', 0, 0, axis_index_groups=same_core, tiled=False)]
    ppermute x24, starting transfers between devices: 37.4 us -> 29.9 us  [send_on(): return lax.ppermute(sent, 'section', pairs)]
    unnamed x20 -> x24, local copies, waits for them, and re-layouts: 2.78 us -> 9.79 us
    pallas_call x30 -> x37, Pallas kernels: 37.4 us -> 31.3 us  [call(): pl.pallas_call(kernel, out_shape=tuple(shapes), in_specs=[spec for _, spe...]
    all_to_all x0 -> x1, starting transfers between devices: none -> 6.04 us  [exchange(): lax.all_to_all(array, 'dp', 0, 0, axis_index_groups=same_core, tiled=False)]
    cond x2, local copies, waits for them, and re-layouts: 2.38 us -> 0.01 us
  transfers between devices with their start and end apart: 26 -> 27, of which waited for: 13 -> 15; matrix products, arithmetic and copies ran while one was open for 1% -> 0% of each run, Pallas kernels for 17% -> 16%
where the time goes in v1:
time: 194 us; the launch traced here: 193 us
  waiting for transfers between devices  74.3 us (38%)
  blocking collectives  38.3 us (20%)
  starting transfers between devices  36.1 us (19%)
  Pallas kernels  31.3 us (16%)
  local copies, waits for them, and re-layouts  9.85 us (5%)
    ppermute x24, waiting for transfers between devices, send_on(): return lax.ppermute(sent, 'section', pairs)  51 us
    all_to_all x1, blocking collectives, exchange(): lax.all_to_all(array, 'dp', 0, 0, axis_index_groups=same_core, tiled=False)  38.3 us
    pallas_call x37, Pallas kernels, call(): pl.pallas_call(kernel, out_shape=tuple(shapes), in_specs=[spec for _, spe...  31.3 us
    ppermute x24, starting transfers between devices, send_on(): return lax.ppermute(sent, 'section', pairs)  29.9 us
    ppermute x1, waiting for transfers between devices, on_device(): lax.ppermute(total[1].astype(bf16), 'section', mirror).astype(f32)  10.7 us
    all_to_all x1, waiting for transfers between devices, exchange(): lax.all_to_all(array, 'dp', 0, 0, axis_index_groups=same_core, tiled=False)  10.7 us
    unnamed x24, local copies, waits for them, and re-layouts  9.79 us
    all_to_all x1, starting transfers between devices, exchange(): lax.all_to_all(array, 'dp', 0, 0, axis_index_groups=same_core, tiled=False)  6.04 us
  transfers between devices with their start and end apart: 27, of which 15 were waited for; matrix products, arithmetic and copies ran while one was open for 0% of the time, Pallas kernels for 16%

profile of v1, /device:TPU:18, one launch (start us, length us, event | category | flops | bytes accessed | tf_op | source)
XLA Modules:
  0.0 193.0 jit_solution(12217321155857924931)
XLA Ops:
  0.7 0.7 copy-done.8
  1.5 0.7 collective-permute-start.1
  2.8 0.7 collective-permute-start
  3.5 1.6 copy-done.7
  5.2 1.3 collective-permute-start.3
  6.5 1.3 collective-permute-start.2
  7.9 0.7 copy-done.9
  8.6 3.5 %load_far.1 = (f32[1,4096]{1,0:T(1,128)S(1)}, bf16[4096,256]{1,0:T(8,128)(2,1)S(1)}, bf16[256,4096]{1,0:T(8,128)(2,1)S(1)}, f32[1,4096]{1,0:T(1,128)S(1)}, bf16[...) custom-call(bf16[2,4096,256]{2,1,0:T(8,128)(2,1)} %refs_0_.8, bf16[2,256,4096]{2,1,0:T(8,128)(2,1)} %refs_1_.10, ...), custom_call_target="tpu_custom_call" | custom-call | flops 1000000000 | bytes 4194304 | tf_op jit(solution)/shard_map/load_far/pallas_call | solution.py:51
  12.1 15.3 %collective-permute-done.3.refs_0_ = bf16[32,4096]{1,0:T(8,128)(2,1)S(1)} collective-permute-done((bf16[32,4096]{1,0:T(8,128)(2,1)S(1)}, bf16[32,4096]{1,0:T(8,128)(2,1)S(1)}, u32[]{:S(2)}, u32[]{:S(2)}) %collective-permute-start.3) | collective-permute-done | bytes 262176 | tf_op jit(solution)/shard_map/ppermute | solution.py:171
  27.4 1.7 forward_2_0.1
  29.1 1.3 collective-permute-start.5
  30.4 1.1 collective-permute-done.2.refs_0_
  31.5 1.6 forward_2_1.1
  33.2 1.3 collective-permute-start.4
  34.5 0.7 collective-permute-done.5.refs_0_
  35.2 1.3 collective-permute-start.7
  36.5 3.4 %collective-permute-done.4.refs_0_ = bf16[32,4096]{1,0:T(8,128)(2,1)S(1)} collective-permute-done((bf16[32,4096]{1,0:T(8,128)(2,1)S(1)}, bf16[32,4096]{1,0:T(8,128)(2,1)S(1)}, u32[]{:S(2)}, u32[]{:S(2)}) %collective-permute-start.4) | collective-permute-done | bytes 262176 | tf_op jit(solution)/shard_map/ppermute | solution.py:171
  40.0 1.3 collective-permute-start.6
  41.3 5.1 %collective-permute-done.7.refs_0_ = bf16[32,4096]{1,0:T(8,128)(2,1)S(1)} collective-permute-done((bf16[32,4096]{1,0:T(8,128)(2,1)S(1)}, bf16[32,4096]{1,0:T(8,128)(2,1)S(1)}, u32[]{:S(2)}, u32[]{:S(2)}) %collective-permute-start.7) | collective-permute-done | bytes 262176 | tf_op jit(solution)/shard_map/ppermute | solution.py:171
  46.4 1.6 copy-done.5
  48.0 1.7 forward_4_0.1
  49.6 1.3 collective-permute-start.9
  50.9 1.1 collective-permute-done.6.refs_0_
  52.0 1.6 forward_4_1.1
  53.7 1.3 collective-permute-start.8
  55.0 17.7 %conditional.5 = (bf16[8,64,768]{2,1,0:T(8,128)(2,1)}, bf16[8,128,768]{2,1,0:T(8,128)(2,1)}) conditional(s32[]{:T(128)} %clamp.10, () %tuple.61, bf16[8,64,768]{2,1,0:T(8,128)(2,1)} %get-tuple-element.262, bf16[8,128,768]{2,1,0:T(8,128)(2,1)} %get-tuple-element.263), branch_computations={%region_2.3_spmd, %region_3.4_spmd, %region_4.5_spmd} | conditional | flops 1000000000 | bytes 8912944 | solution.py:399
  55.1 6.0 %all-to-all-start.1 = ((bf16[8,64,768]{2,1,0:T(8,128)(2,1)}), bf16[8,64,768]{2,1,0:T(8,128)(2,1)S(1)}, u32[]{:S(2)}, u32[]{:S(2)}) async-start(bf16[8,64,768]{2,1,0:T(8,128)(2,1)} %param.3), calls=%async_computation.1 | async-start | bytes 1572864 | tf_op jit(solution)/shard_map/cond/branch_1_fun/all_to_all | solution.py:183
  61.1 10.7 %all-to-all-done.1.refs_0_ = bf16[8,64,768]{2,1,0:T(8,128)(2,1)S(1)} async-done(((bf16[8,64,768]{2,1,0:T(8,128)(2,1)}), bf16[8,64,768]{2,1,0:T(8,128)(2,1)S(1)}, u32[]{:S(2)}, u32[]{:S(2)}) %all-to-all-start.1) | async-done | bytes 786464 | tf_op jit(solution)/shard_map/cond/branch_1_fun/all_to_all | solution.py:183
  71.8 0.9 unstage.6
  72.9 0.7 collective-permute-start.11
  73.7 0.7 collective-permute-start.10
  74.4 0.7 collective-permute-start.13
  75.2 0.7 collective-permute-start.12
  76.1 1.5 copy-done.3
  77.6 1.3 collective-permute-start.15
  79.0 1.3 collective-permute-start.14
  80.3 1.3 saved_far_2.1
  81.5 4.2 %turn_far_2.1 = (f32[1,4096]{1,0:T(1,128)S(1)}, bf16[256,4096]{1,0:T(8,128)(2,1)S(1)}, bf16[4096,256]{1,0:T(8,128)(2,1)S(1)}) custom-call(bf16[2,4096,256]{2,1,0:T(8,128)(2,1)} %refs_0_.8, bf16[2,256,4096]{2,1,0:T(8,128)(2,1)} %refs_1_.10, f32[2,4096]{1,0:T(2,128)S(1)} %copy-done.9), custom_call_target="tpu_custom_call" | custom-call | flops 1000000000 | bytes 4194304 | tf_op jit(solution)/shard_map/turn_far_2/pallas_call | solution.py:51
  85.8 1.5 backward_8_0.1
  87.3 5.0 %collective-permute-start.17 = (bf16[32,4096]{1,0:T(8,128)(2,1)S(1)}, bf16[32,4096]{1,0:T(8,128)(2,1)S(1)}, u32[]{:S(2)}, u32[]{:S(2)}) collective-permute-start(bf16[32,4096]{1,0:T(8,128)(2,1)S(1)} %get-tuple-element.333), channel_id=1, source_target_pairs={{32,48},{80,64},{33,49},{81,65},{34,50},{82,66},{35,51},{83,67},{3... | collective-permute-start | bytes 786440 | tf_op jit(solution)/shard_map/ppermute | solution.py:171
  92.3 15.0 %collective-permute-done.14.refs_0_ = bf16[32,4096]{1,0:T(8,128)(2,1)S(1)} collective-permute-done((bf16[32,4096]{1,0:T(8,128)(2,1)S(1)}, bf16[32,4096]{1,0:T(8,128)(2,1)S(1)}, u32[]{:S(2)}, u32[]{:S(2)}) %collective-permute-start.14) | collective-permute-done | bytes 262176 | tf_op jit(solution)/shard_map/ppermute | solution.py:171
  107.3 1.5 backward_8_1.1
  108.8 1.3 collective-permute-start.16
  110.1 1.3 saved_far_1.1
  111.4 4.2 %turn_far_1.1 = (f32[1,4096]{1,0:T(1,128)S(1)}, bf16[256,4096]{1,0:T(8,128)(2,1)S(1)}, bf16[4096,256]{1,0:T(8,128)(2,1)S(1)}) custom-call(bf16[2,4096,256]{2,1,0:T(8,128)(2,1)} %refs_0_.8, bf16[2,256,4096]{2,1,0:T(8,128)(2,1)} %refs_1_.10, f32[2,4096]{1,0:T(2,128)S(1)} %copy-done.9), custom_call_target="tpu_custom_call" | custom-call | flops 1000000000 | bytes 4194304 | tf_op jit(solution)/shard_map/turn_far_1/pallas_call | solution.py:51
  115.9 1.3 collective-permute-start.19
  117.3 1.3 collective-permute-start.18
  118.6 5.7 %collective-permute-done.19.refs_0_ = bf16[32,4096]{1,0:T(8,128)(2,1)S(1)} collective-permute-done((bf16[32,4096]{1,0:T(8,128)(2,1)S(1)}, bf16[32,4096]{1,0:T(8,128)(2,1)S(1)}, u32[]{:S(2)}, u32[]{:S(2)}) %collective-permute-start.19) | collective-permute-done | bytes 262176 | tf_op jit(solution)/shard_map/ppermute | solution.py:171
  124.3 1.5 backward_10_0.1
  125.8 1.3 collective-permute-start.21
  127.8 1.4 backward_10_1.1
  129.2 1.3 collective-permute-start.20
  131.0 0.7 collective-permute-start.23
  131.7 2.7 %collective-permute-done.20.refs_0_ = bf16[32,4096]{1,0:T(8,128)(2,1)S(1)} collective-permute-done((bf16[32,4096]{1,0:T(8,128)(2,1)S(1)}, bf16[32,4096]{1,0:T(8,128)(2,1)S(1)}, u32[]{:S(2)}, u32[]{:S(2)}) %collective-permute-start.20) | collective-permute-done | bytes 262176 | tf_op jit(solution)/shard_map/ppermute | solution.py:171
  134.4 0.7 backward_11_1.1
  135.1 0.7 collective-permute-start.22
  135.9 1.6 copy-done.1
  137.6 1.3 copy-done.10
  139.1 39.4 %conditional.7 = ((f32[2,2,256,256]{3,2,1,0:T(8,128)S(1)}, bf16[2,2,256,256]{3,2,1,0:T(8,128)(2,1)S(1)})) conditional(s32[]{:T(128)} %clamp.9, (bf16[8,64,768]{2,1,0:T(8,128)(2,1)}, bf16[8,64,768]{2,1,0:T(8,128)(2,1)S(1)}, bf16[8,128,768]{2,1,0:T(8,128)(2,1)S(1)}) %tuple.93, (bf16[8,128,768]{2,1,0:T(8,128)(2,1)}, ...), branch_computations={%region_8.9_spmd, %region_9.10_spmd, %region_10.11_spmd, %region_1... | conditional | flops 1000000000 | bytes 13631524 | solution.py:587
  139.1 38.3 %all_to_all.38.refs_0_ = bf16[8,192,768]{2,1,0:T(8,128)(2,1)S(1)} all-to-all(bf16[8,192,768]{2,1,0:T(8,128)(2,1)} %get-tuple-element.34), channel_id=1, replica_groups={{0,2,4,6,8,10,12,14},{1,3,5,7,9,11,13,15},{16,18,20,22,24,26,28,30},{17..., dimensions={0} | all-to-all | bytes 4718592 | tf_op jit(solution)/shard_map/cond/branch_2_fun/all_to_all | solution.py:183
  177.4 1.1 products.6
  178.6 1.9 collective-permute-done.24
  180.8 10.7 %collective-permute-done.25 = bf16[2,256,256]{2,1,0:T(8,128)(2,1)S(1)} collective-permute-done((bf16[2,256,256]{2,1,0:T(8,128)(2,1)S(1)}, bf16[2,256,256]{2,1,0:T(8,128)(2,1)S(1)}, u32[]{:S(2)}, u32[]{:S(2)}) %collective-permute-start.25) | collective-permute-done | bytes 262176 | tf_op jit(solution)/shard_map/ppermute | solution.py:606
  191.6 1.5 multiply_reduce_fusion
  (78 shorter events, 3.8 us)
Async XLA Ops:
  0.6 0.8 copy-start.8
  1.5 1.3 copy-start.6
  1.5 2.0 %collective-permute-start.1 = (bf16[32,4096]{1,0:T(8,128)(2,1)S(1)}, bf16[32,4096]{1,0:T(8,128)(2,1)S(1)}, u32[]{:S(2)}, u32[]{:S(2)}) collective-permute-start(bf16[32,4096]{1,0:T(8,128)(2,1)S(1)} %get-tuple-element.213), channel_id=1, source_target_pairs={{0,16},{112,96},{1,17},{113,97},{2,18},{114,98},{3,19},{115,99},{4... | collective-permute-start | bytes 786440 | tf_op jit(solution)/shard_map/ppermute | solution.py:171
  2.8 3.6 %collective-permute-start = (bf16[32,4096]{1,0:T(8,128)(2,1)S(1)}, bf16[32,4096]{1,0:T(8,128)(2,1)S(1)}, u32[]{:S(2)}, u32[]{:S(2)}) collective-permute-start(bf16[32,4096]{1,0:T(8,128)(2,1)S(1)} %get-tuple-element.212), channel_id=1, source_target_pairs={{0,16},{112,96},{1,17},{113,97},{2,18},{114,98},{3,19},{115,99},{4... | collective-permute-start | bytes 786440 | tf_op jit(solution)/shard_map/ppermute | solution.py:171
  3.5 1.6 copy-start.7
  5.2 22.3 %collective-permute-start.3 = (bf16[32,4096]{1,0:T(8,128)(2,1)S(1)}, bf16[32,4096]{1,0:T(8,128)(2,1)S(1)}, u32[]{:S(2)}, u32[]{:S(2)}) collective-permute-start(bf16[32,4096]{1,0:T(8,128)(2,1)S(1)} %get-tuple-element.232), channel_id=1, source_target_pairs={{16,32},{96,80},{17,33},{97,81},{18,34},{98,82},{19,35},{99,83},{2... | collective-permute-start | bytes 786440 | tf_op jit(solution)/shard_map/ppermute | solution.py:171
  6.5 25.0 %collective-permute-start.2 = (bf16[32,4096]{1,0:T(8,128)(2,1)S(1)}, bf16[32,4096]{1,0:T(8,128)(2,1)S(1)}, u32[]{:S(2)}, u32[]{:S(2)}) collective-permute-start(bf16[32,4096]{1,0:T(8,128)(2,1)S(1)} %get-tuple-element.219), channel_id=1, source_target_pairs={{16,32},{96,80},{17,33},{97,81},{18,34},{98,82},{19,35},{99,83},{2... | collective-permute-start | bytes 786440 | tf_op jit(solution)/shard_map/ppermute | solution.py:171
  7.9 0.8 copy-start.9
  12.1 27.8 %copy-start.4 = (bf16[256,4096]{1,0:T(8,128)(2,1)}, bf16[256,4096]{1,0:T(8,128)(2,1)S(1)}, u32[]{:S(2)}) copy-start(bf16[256,4096]{1,0:T(8,128)(2,1)S(1)} %get-tuple-element.242.refs_6_.refs_3_) | copy-start | bytes 6291460
  29.1 6.0 %collective-permute-start.5 = (bf16[32,4096]{1,0:T(8,128)(2,1)S(1)}, bf16[32,4096]{1,0:T(8,128)(2,1)S(1)}, u32[]{:S(2)}, u32[]{:S(2)}) collective-permute-start(bf16[32,4096]{1,0:T(8,128)(2,1)S(1)} %get-tuple-element.243), channel_id=1, source_target_pairs={{32,48},{80,64},{33,49},{81,65},{34,50},{82,66},{35,51},{83,67},{3... | collective-permute-start | bytes 786440 | tf_op jit(solution)/shard_map/ppermute | solution.py:171
  33.2 6.8 %collective-permute-start.4 = (bf16[32,4096]{1,0:T(8,128)(2,1)S(1)}, bf16[32,4096]{1,0:T(8,128)(2,1)S(1)}, u32[]{:S(2)}, u32[]{:S(2)}) collective-permute-start(bf16[32,4096]{1,0:T(8,128)(2,1)S(1)} %get-tuple-element.239), channel_id=1, source_target_pairs={{32,48},{80,64},{33,49},{81,65},{34,50},{82,66},{35,51},{83,67},{3... | collective-permute-start | bytes 786440 | tf_op jit(solution)/shard_map/ppermute | solution.py:171
  35.2 11.1 %collective-permute-start.7 = (bf16[32,4096]{1,0:T(8,128)(2,1)S(1)}, bf16[32,4096]{1,0:T(8,128)(2,1)S(1)}, u32[]{:S(2)}, u32[]{:S(2)}) collective-permute-start(bf16[32,4096]{1,0:T(8,128)(2,1)S(1)} %get-tuple-element.251), channel_id=1, source_target_pairs={{48,32},{64,80},{49,33},{65,81},{50,34},{66,82},{51,35},{67,83},{5... | collective-permute-start | bytes 786440 | tf_op jit(solution)/shard_map/ppermute | solution.py:171
  40.0 12.1 %collective-permute-start.6 = (bf16[32,4096]{1,0:T(8,128)(2,1)S(1)}, bf16[32,4096]{1,0:T(8,128)(2,1)S(1)}, u32[]{:S(2)}, u32[]{:S(2)}) collective-permute-start(bf16[32,4096]{1,0:T(8,128)(2,1)S(1)} %get-tuple-element.250), channel_id=1, source_target_pairs={{48,32},{64,80},{49,33},{65,81},{50,34},{66,82},{51,35},{67,83},{5... | collective-permute-start | bytes 786440 | tf_op jit(solution)/shard_map/ppermute | solution.py:171
  46.4 1.6 copy-start.5
  49.6 23.2 %collective-permute-start.9 = (bf16[32,4096]{1,0:T(8,128)(2,1)S(1)}, bf16[32,4096]{1,0:T(8,128)(2,1)S(1)}, u32[]{:S(2)}, u32[]{:S(2)}) collective-permute-start(bf16[32,4096]{1,0:T(8,128)(2,1)S(1)} %get-tuple-element.275), channel_id=1, source_target_pairs={{32,16},{80,96},{33,17},{81,97},{34,18},{82,98},{35,19},{83,99},{3... | collective-permute-start | bytes 786440 | tf_op jit(solution)/shard_map/ppermute | solution.py:171
  53.7 19.9 %collective-permute-start.8 = (bf16[32,4096]{1,0:T(8,128)(2,1)S(1)}, bf16[32,4096]{1,0:T(8,128)(2,1)S(1)}, u32[]{:S(2)}, u32[]{:S(2)}) collective-permute-start(bf16[32,4096]{1,0:T(8,128)(2,1)S(1)} %get-tuple-element.258), channel_id=1, source_target_pairs={{32,16},{80,96},{33,17},{81,97},{34,18},{82,98},{35,19},{83,99},{3... | collective-permute-start | bytes 786440 | tf_op jit(solution)/shard_map/ppermute | solution.py:171
  55.1 16.7 %all-to-all-start.1 = ((bf16[8,64,768]{2,1,0:T(8,128)(2,1)}), bf16[8,64,768]{2,1,0:T(8,128)(2,1)S(1)}, u32[]{:S(2)}, u32[]{:S(2)}) async-start(bf16[8,64,768]{2,1,0:T(8,128)(2,1)} %param.3), calls=%async_computation.1 | async-start | bytes 1572864 | tf_op jit(solution)/shard_map/cond/branch_1_fun/all_to_all | solution.py:183
  72.8 2.3 %copy-start.2 = (bf16[4096,256]{1,0:T(8,128)(2,1)}, bf16[4096,256]{1,0:T(8,128)(2,1)S(1)}, u32[]{:S(2)}) copy-start(bf16[4096,256]{1,0:T(8,128)(2,1)S(1)} %get-tuple-element.284.refs_5_.refs_3_) | copy-start | bytes 6291460
  72.9 1.4 collective-permute-start.11
  73.7 1.5 collective-permute-start.10
  74.4 1.6 collective-permute-start.13
  75.2 3.6 %collective-permute-start.12 = (bf16[32,4096]{1,0:T(8,128)(2,1)S(1)}, bf16[32,4096]{1,0:T(8,128)(2,1)S(1)}, u32[]{:S(2)}, u32[]{:S(2)}) collective-permute-start(bf16[32,4096]{1,0:T(8,128)(2,1)S(1)} %get-tuple-element.290), channel_id=1, source_target_pairs={{0,16},{112,96},{1,17},{113,97},{2,18},{114,98},{3,19},{115,99},{4... | collective-permute-start | bytes 786440 | tf_op jit(solution)/shard_map/ppermute | solution.py:171
  75.9 1.6 copy-start.3
  77.6 8.3 %collective-permute-start.15 = (bf16[32,4096]{1,0:T(8,128)(2,1)S(1)}, bf16[32,4096]{1,0:T(8,128)(2,1)S(1)}, u32[]{:S(2)}, u32[]{:S(2)}) collective-permute-start(bf16[32,4096]{1,0:T(8,128)(2,1)S(1)} %get-tuple-element.319), channel_id=1, source_target_pairs={{16,32},{96,80},{17,33},{97,81},{18,34},{98,82},{19,35},{99,83},{2... | collective-permute-start | bytes 786440 | tf_op jit(solution)/shard_map/ppermute | solution.py:171
  79.0 28.3 %collective-permute-start.14 = (bf16[32,4096]{1,0:T(8,128)(2,1)S(1)}, bf16[32,4096]{1,0:T(8,128)(2,1)S(1)}, u32[]{:S(2)}, u32[]{:S(2)}) collective-permute-start(bf16[32,4096]{1,0:T(8,128)(2,1)S(1)} %get-tuple-element.299), channel_id=1, source_target_pairs={{16,32},{96,80},{17,33},{97,81},{18,34},{98,82},{19,35},{99,83},{2... | collective-permute-start | bytes 786440 | tf_op jit(solution)/shard_map/ppermute | solution.py:171
  87.3 28.3 %collective-permute-start.17 = (bf16[32,4096]{1,0:T(8,128)(2,1)S(1)}, bf16[32,4096]{1,0:T(8,128)(2,1)S(1)}, u32[]{:S(2)}, u32[]{:S(2)}) collective-permute-start(bf16[32,4096]{1,0:T(8,128)(2,1)S(1)} %get-tuple-element.333), channel_id=1, source_target_pairs={{32,48},{80,64},{33,49},{81,65},{34,50},{82,66},{35,51},{83,67},{3... | collective-permute-start | bytes 786440 | tf_op jit(solution)/shard_map/ppermute | solution.py:171
  108.8 8.4 %collective-permute-start.16 = (bf16[32,4096]{1,0:T(8,128)(2,1)S(1)}, bf16[32,4096]{1,0:T(8,128)(2,1)S(1)}, u32[]{:S(2)}, u32[]{:S(2)}) collective-permute-start(bf16[32,4096]{1,0:T(8,128)(2,1)S(1)} %get-tuple-element.323), channel_id=1, source_target_pairs={{32,48},{80,64},{33,49},{81,65},{34,50},{82,66},{35,51},{83,67},{3... | collective-permute-start | bytes 786440 | tf_op jit(solution)/shard_map/ppermute | solution.py:171
  115.9 8.4 %collective-permute-start.19 = (bf16[32,4096]{1,0:T(8,128)(2,1)S(1)}, bf16[32,4096]{1,0:T(8,128)(2,1)S(1)}, u32[]{:S(2)}, u32[]{:S(2)}) collective-permute-start(bf16[32,4096]{1,0:T(8,128)(2,1)S(1)} %get-tuple-element.338), channel_id=1, source_target_pairs={{48,32},{64,80},{49,33},{65,81},{50,34},{66,82},{51,35},{67,83},{5... | collective-permute-start | bytes 786440 | tf_op jit(solution)/shard_map/ppermute | solution.py:171
  117.3 10.5 %collective-permute-start.18 = (bf16[32,4096]{1,0:T(8,128)(2,1)S(1)}, bf16[32,4096]{1,0:T(8,128)(2,1)S(1)}, u32[]{:S(2)}, u32[]{:S(2)}) collective-permute-start(bf16[32,4096]{1,0:T(8,128)(2,1)S(1)} %get-tuple-element.337), channel_id=1, source_target_pairs={{48,32},{64,80},{49,33},{65,81},{50,34},{66,82},{51,35},{67,83},{5... | collective-permute-start | bytes 786440 | tf_op jit(solution)/shard_map/ppermute | solution.py:171
  125.8 5.2 %collective-permute-start.21 = (bf16[32,4096]{1,0:T(8,128)(2,1)S(1)}, bf16[32,4096]{1,0:T(8,128)(2,1)S(1)}, u32[]{:S(2)}, u32[]{:S(2)}) collective-permute-start(bf16[32,4096]{1,0:T(8,128)(2,1)S(1)} %get-tuple-element.353), channel_id=1, source_target_pairs={{32,16},{80,96},{33,17},{81,97},{34,18},{82,98},{35,19},{83,99},{3... | collective-permute-start | bytes 786440 | tf_op jit(solution)/shard_map/ppermute | solution.py:171
  129.2 5.2 %collective-permute-start.20 = (bf16[32,4096]{1,0:T(8,128)(2,1)S(1)}, bf16[32,4096]{1,0:T(8,128)(2,1)S(1)}, u32[]{:S(2)}, u32[]{:S(2)}) collective-permute-start(bf16[32,4096]{1,0:T(8,128)(2,1)S(1)} %get-tuple-element.343), channel_id=1, source_target_pairs={{32,16},{80,96},{33,17},{81,97},{34,18},{82,98},{35,19},{83,99},{3... | collective-permute-start | bytes 786440 | tf_op jit(solution)/shard_map/ppermute | solution.py:171
  130.8 3.6 %copy-start = (bf16[4096,256]{1,0:T(8,128)(2,1)}, bf16[4096,256]{1,0:T(8,128)(2,1)S(1)}, u32[]{:S(2)}) copy-start(bf16[4096,256]{1,0:T(8,128)(2,1)S(1)} %get-tuple-element.349.refs_3_) | copy-start | bytes 6291460
  131.0 4.8 %collective-permute-start.23 = (bf16[32,4096]{1,0:T(8,128)(2,1)S(1)}, bf16[32,4096]{1,0:T(8,128)(2,1)S(1)}, u32[]{:S(2)}, u32[]{:S(2)}) collective-permute-start(bf16[32,4096]{1,0:T(8,128)(2,1)S(1)} %get-tuple-element.358), channel_id=1, source_target_pairs={{16,0},{96,112},{17,1},{97,113},{18,2},{98,114},{19,3},{99,115},{2... | collective-permute-start | bytes 786440 | tf_op jit(solution)/shard_map/ppermute | solution.py:171
  135.1 2.3 %collective-permute-start.22 = (bf16[32,4096]{1,0:T(8,128)(2,1)}, bf16[32,4096]{1,0:T(8,128)(2,1)S(1)}, u32[]{:S(2)}, u32[]{:S(2)}) collective-permute-start(bf16[32,4096]{1,0:T(8,128)(2,1)} %get-tuple-element.357), channel_id=1, source_target_pairs={{16,0},{96,112},{17,1},{97,113},{18,2},{98,114},{19,3},{99,115},{2... | collective-permute-start | bytes 786440 | tf_op jit(solution)/shard_map/ppermute | solution.py:171
  135.8 1.6 copy-start.1
  137.5 1.4 copy-start.10
  137.5 1.6 copy-start.13
  139.1 38.3 %copy-start.12 = (bf16[8,64,768]{2,1,0:T(8,128)(2,1)S(1)}, bf16[8,64,768]{2,1,0:T(8,128)(2,1)}, u32[]{:S(2)}) copy-start(bf16[8,64,768]{2,1,0:T(8,128)(2,1)} %get-tuple-element.35.refs_1_) | copy-start | bytes 2359300 | tf_op jit(solution)/shard_map/cond
  178.5 2.3 %slice-start = ((f32[2,4096]{1,0:T(2,128)}), f32[1,4096]{1,0:T(1,128)S(1)}, s32[]{:S(2)}) async-start(f32[2,4096]{1,0:T(2,128)} %refs_2_.11), calls=%async_computation.9 | async-start | bytes 32768 | tf_op jit(solution)/shard_map/slice | solution.py:608
  178.5 2.0 %collective-permute-start.24 = (bf16[2,2,256,256]{3,2,1,0:T(8,128)(2,1)S(1)}, bf16[2,2,256,256]{3,2,1,0:T(8,128)(2,1)S(1)}, u32[]{:S(2)}, u32[]{:S(2)}) collective-permute-start(bf16[2,2,256,256]{3,2,1,0:T(8,128)(2,1)S(1)} %get-tuple-element.372), channel_id=1, source_target_pairs={{0,1},{1,0},{2,3},{3,2},{4,5},{5,4},{6,7},{7,6},{8,9},{9,8},{10,11... | collective-permute-start | bytes 1572872 | tf_op jit(solution)/shard_map/ppermute | solution.py:604
  180.7 10.8 %collective-permute-start.25 = (bf16[2,256,256]{2,1,0:T(8,128)(2,1)S(1)}, bf16[2,256,256]{2,1,0:T(8,128)(2,1)S(1)}, u32[]{:S(2)}, u32[]{:S(2)}) collective-permute-start(bf16[2,256,256]{2,1,0:T(8,128)(2,1)S(1)} %fusion.1), channel_id=1, source_target_pairs={{0,112},{16,96},{32,80},{48,64},{64,48},{80,32},{96,16},{112,0},{1... | collective-permute-start | bytes 786440 | tf_op jit(solution)/shard_map/ppermute | solution.py:606
  180.8 10.8 %slice-start.1 = ((bf16[2,4096,256]{2,1,0:T(8,128)(2,1)}), bf16[1,4096,256]{2,1,0:T(8,128)(2,1)S(1)}, s32[]{:S(2)}) async-start(bf16[2,4096,256]{2,1,0:T(8,128)(2,1)} %refs_0_.8), calls=%async_computation.10 | async-start | bytes 4194304 | tf_op jit(solution)/shard_map/slice | solution.py:609

commit v2 on v1

--- a/solution.py
+++ b/solution.py
@@ -56,7 +56,7 @@
         input_output_aliases={n_read + i: i for i in range(n_update + n_place)},
         scratch_shapes=list(scratch),
         compiler_params=pltpu.CompilerParams(vmem_limit_bytes=limit * MIB),
-        cost_estimate=pl.CostEstimate(flops=10**9, bytes_accessed=4 * MIB, transcendentals=0),
+        cost_estimate=pl.CostEstimate(flops=1, bytes_accessed=1, transcendentals=0),
         name=name,
     )(*[a for a, _ in reads], *updates, *places)
 
@@ -209,23 +209,16 @@
         inputs, source_in, source_out, source_gain = reads
         fold, half = place()
 
-        @pl.when(fold <= 1)
+        @pl.when(fold == STAGES[0])
         def _():
+            copy = pltpu.make_async_copy(inputs.at[half, of_micro(0)], staged, sem)
+            copy.start()
             ready = load(half, (source_in, source_out), (weight_in, weight_out), load_sems)
             gain[...] = source_gain[pl.ds(half, 1), :]
-
-            @pl.when(fold == STAGES[0])
-            def _():
-                copy = pltpu.make_async_copy(inputs.at[half, of_micro(0)], staged, sem)
-                copy.start()
-                copy.wait()
-                out = Keeper(0, scratch, box, layer=0, kept=kept)
-                sent[...] = forward(staged[...], gain, weight_in, weight_out, out, ready)
-                out.wait()
-
-            @pl.when(fold != STAGES[0])
-            def _():
-                wait_all(ready[0] + ready[1])
+            copy.wait()
+            out = Keeper(0, scratch, box, layer=0, kept=kept)
+            sent[...] = forward(staged[...], gain, weight_in, weight_out, out, ready)
+            out.wait()
 
     class Keeper:
         def __init__(self, m, scratch, box, slot=0, layer=0, hats=None, kept=None):
@@ -380,7 +373,8 @@
             moved[m] = send_on(sent, stage)
         return box
 
-    box_early = forward_stage(1, {0: 0}, box_early, [weights_1])
+    weights = fresh_weights("load_1", lambda fold: fold == 1, (0,), 1, 0)
+    box_early = forward_stage(1, {0: 0}, box_early, weights)
 
     def none(name, array):
         return new_boxes(name, [array.shape])[0]
@@ -390,10 +384,14 @@
     got_early, box_two, box_far, kept, hats, raw_in, raw_out = lax.optimization_barrier(
         (got_early, box_two, box_far, kept, hats, raw_in, raw_out)
     )
-    weights = fresh_weights("load_far", lambda fold: fold >= 2, (0, 1), 1, 0)
+    weights = fresh_weights("load_2", lambda fold: fold == 2, (0,), 1, 0)
     box_two = forward_stage(2, {0: 0}, box_two, weights)
+    raw_in, raw_out, kept = lax.optimization_barrier((raw_in, raw_out, kept))
+    weights = fresh_weights("load_3", lambda fold: fold == 3, (0, 1), 1, 0)
     box_far = forward_stage(3, {0: 0, 1: 1}, box_far, weights)
-    box_late_two = forward_stage(4, {1: 2}, box_late_two, weights)
+    raw_in, raw_out, kept = lax.optimization_barrier((raw_in, raw_out, kept))
+    weights = fresh_weights("load_4", lambda fold: fold == 2, (1,), 1, 0)
+    box_late_two = forward_stage(4, {1: 2}, box_late_two, [None, *weights])
 
     box_two, box_far, kept = lax.optimization_barrier((box_two, box_far, kept))
     got_two, got_far = lax.switch(
@@ -539,9 +537,12 @@
     box_late = backward_stage(9, {1: 0, 0: 1}, box_late, [far_1, far_2])
     box_late_two = backward_stage(10, {0: 1}, box_late_two, [far_1])
     kept, raw_in, raw_out = lax.optimization_barrier((kept, raw_in, raw_out))
-    (near_1,) = fresh_weights("turn_near_1", lambda fold: fold <= 1, (0,), 0, 1)
-    near_1 = (*near_1, *saved_rows("saved_near_1", lambda fold: fold <= 1, 0))
+    (near_1,) = fresh_weights("turn_11", lambda fold: fold == 1, (0,), 0, 1)
+    near_1 = (*near_1, *saved_rows("saved_11", lambda fold: fold == 1, 0))
     box_late = backward_stage(11, {0: 1}, box_late, [near_1])
+    kept, raw_in, raw_out = lax.optimization_barrier((kept, raw_in, raw_out))
+    (near_1,) = fresh_weights("turn_12", lambda fold: fold == 0, (0,), 0, 1)
+    near_1 = (*near_1, *saved_rows("saved_12", lambda fold: fold == 0, 0))
     box_end = backward_stage(LAST, {0: 0}, box_end, [near_1])
 
     def products(pick, reads, keep, send, whole_in, whole_out):

time: 194 us -> 175 us (0.902)
  waiting for transfers between devices: 74.3 us -> 65.6 us
  blocking collectives: 38.3 us -> 32.5 us
  local copies, waits for them, and re-layouts: 9.85 us -> 5.24 us
    ppermute x24, waiting for transfers between devices: 51 us -> 42.3 us  [send_on(): return lax.ppermute(sent, 'section', pairs)]
    all_to_all x1, blocking collectives: 38.3 us -> 32.5 us  [exchange(): lax.all_to_all(array, 'dp', 0, 0, axis_index_groups=same_core, tiled=False)]
    unnamed x24 -> x12, local copies, waits for them, and re-layouts: 9.79 us -> 5.19 us
    pallas_call x37 -> x42, Pallas kernels: 31.3 us -> 32.1 us  [call(): pl.pallas_call(kernel, out_shape=tuple(shapes), in_specs=[spec for _, spe...]
  transfers between devices with their start and end apart: 27 -> 27, of which waited for: 15 -> 15; matrix products, arithmetic and copies ran while one was open for 0% -> 0% of each run, Pallas kernels for 16% -> 18%
where the time goes in v2:
time: 175 us; the launch traced here: 173 us
  waiting for transfers between devices  65.6 us (37%)
  starting transfers between devices  34.6 us (20%)
  blocking collectives  32.5 us (19%)
  Pallas kernels  32.1 us (18%)
  local copies, waits for them, and re-layouts  5.24 us (3%)
    ppermute x24, waiting for transfers between devices, send_on(): return lax.ppermute(sent, 'section', pairs)  42.3 us
    all_to_all x1, blocking collectives, exchange(): lax.all_to_all(array, 'dp', 0, 0, axis_index_groups=same_core, tiled=False)  32.5 us
    pallas_call x42, Pallas kernels, call(): pl.pallas_call(kernel, out_shape=tuple(shapes), in_specs=[spec for _, spe...  32.1 us
    ppermute x24, starting transfers between devices, send_on(): return lax.ppermute(sent, 'section', pairs)  28.4 us
    ppermute x1, waiting for transfers between devices, on_device(): lax.ppermute(total[1].astype(bf16), 'section', mirror).astype(f32)  10.7 us
    all_to_all x1, waiting for transfers between devices, exchange(): lax.all_to_all(array, 'dp', 0, 0, axis_index_groups=same_core, tiled=False)  10.6 us
    all_to_all x1, starting transfers between devices, exchange(): lax.all_to_all(array, 'dp', 0, 0, axis_index_groups=same_core, tiled=False)  6.04 us
    unnamed x12, local copies, waits for them, and re-layouts  5.19 us
  transfers between devices with their start and end apart: 27, of which 15 were waited for; matrix products, arithmetic and copies ran while one was open for 0% of the time, Pallas kernels for 18%

profile of v2, /device:TPU:18, one launch (start us, length us, event | category | flops | bytes accessed | tf_op | source)
XLA Modules:
  0.0 173.2 jit_solution(4274740702893768804)
XLA Ops:
  0.7 0.7 copy-done.2
  1.5 0.7 collective-permute-start.1
  2.3 0.7 collective-permute-start
  3.1 1.3 copy-done
  4.4 1.6 copy-done.1
  6.0 1.3 collective-permute-start.3
  7.4 1.3 collective-permute-start.2
  8.8 2.2 %load_2.1 = (f32[1,4096]{1,0:T(1,128)S(1)}, bf16[4096,256]{1,0:T(8,128)(2,1)S(1)}, bf16[256,4096]{1,0:T(8,128)(2,1)S(1)}) custom-call(bf16[2,4096,256]{2,1,0:T(8,128)(2,1)} %refs_0_.13, bf16[2,256,4096]{2,1,0:T(8,128)(2,1)} %refs_1_.15, f32[2,4096]{1,0:T(2,128)S(1)} %copy-done.3), custom_call_target="tpu_custom_call" | custom-call | flops 1 | bytes 1 | tf_op jit(solution)/shard_map/load_2/pallas_call | solution.py:51
  11.0 16.4 %collective-permute-done.3.refs_0_ = bf16[32,4096]{1,0:T(8,128)(2,1)S(1)} collective-permute-done((bf16[32,4096]{1,0:T(8,128)(2,1)S(1)}, bf16[32,4096]{1,0:T(8,128)(2,1)S(1)}, u32[]{:S(2)}, u32[]{:S(2)}) %collective-permute-start.3) | collective-permute-done | bytes 262176 | tf_op jit(solution)/shard_map/ppermute | solution.py:171
  27.4 1.7 forward_2_0.1
  29.0 1.3 collective-permute-start.5
  30.4 1.1 collective-permute-done.2.refs_0_
  31.4 1.7 forward_2_1.1
  33.1 1.3 collective-permute-start.4
  34.6 0.5 collective-permute-done.5.refs_0_
  35.1 1.3 collective-permute-start.7
  36.4 3.4 %collective-permute-done.4.refs_0_ = bf16[32,4096]{1,0:T(8,128)(2,1)S(1)} collective-permute-done((bf16[32,4096]{1,0:T(8,128)(2,1)S(1)}, bf16[32,4096]{1,0:T(8,128)(2,1)S(1)}, u32[]{:S(2)}, u32[]{:S(2)}) %collective-permute-start.4) | collective-permute-done | bytes 262176 | tf_op jit(solution)/shard_map/ppermute | solution.py:171
  39.9 1.3 collective-permute-start.6
  41.2 2.2 %load_4.1 = (f32[1,4096]{1,0:T(1,128)S(1)}, bf16[4096,256]{1,0:T(8,128)(2,1)S(1)}, bf16[256,4096]{1,0:T(8,128)(2,1)S(1)}) custom-call(bf16[2,4096,256]{2,1,0:T(8,128)(2,1)} %refs_0_.13, bf16[2,256,4096]{2,1,0:T(8,128)(2,1)} %refs_1_.15, f32[2,4096]{1,0:T(2,128)S(1)} %copy-done.3), custom_call_target="tpu_custom_call" | custom-call | flops 1 | bytes 1 | tf_op jit(solution)/shard_map/load_4/pallas_call | solution.py:51
  43.4 2.8 %collective-permute-done.7.refs_0_ = bf16[32,4096]{1,0:T(8,128)(2,1)S(1)} collective-permute-done((bf16[32,4096]{1,0:T(8,128)(2,1)S(1)}, bf16[32,4096]{1,0:T(8,128)(2,1)S(1)}, u32[]{:S(2)}, u32[]{:S(2)}) %collective-permute-start.7) | collective-permute-done | bytes 262176 | tf_op jit(solution)/shard_map/ppermute | solution.py:171
  46.3 1.7 forward_4_0.1
  47.9 1.3 collective-permute-start.9
  49.2 2.7 %collective-permute-done.6.refs_0_ = bf16[32,4096]{1,0:T(8,128)(2,1)S(1)} collective-permute-done((bf16[32,4096]{1,0:T(8,128)(2,1)S(1)}, bf16[32,4096]{1,0:T(8,128)(2,1)S(1)}, u32[]{:S(2)}, u32[]{:S(2)}) %collective-permute-start.6) | collective-permute-done | bytes 262176 | tf_op jit(solution)/shard_map/ppermute | solution.py:171
  51.9 1.7 forward_4_1.1
  53.6 1.3 collective-permute-start.8
  55.0 17.7 %conditional.5 = (bf16[8,64,768]{2,1,0:T(8,128)(2,1)}, bf16[8,128,768]{2,1,0:T(8,128)(2,1)}) conditional(s32[]{:T(128)} %clamp.10, () %tuple.66, bf16[8,64,768]{2,1,0:T(8,128)(2,1)} %get-tuple-element.300, bf16[8,128,768]{2,1,0:T(8,128)(2,1)} %get-tuple-element.301), branch_computations={%region_2.3_spmd, %region_3.4_spmd, %region_4.5_spmd} | conditional | flops 1 | bytes 4718641 | solution.py:397
  55.0 6.0 %all-to-all-start.1 = ((bf16[8,64,768]{2,1,0:T(8,128)(2,1)}), bf16[8,64,768]{2,1,0:T(8,128)(2,1)S(1)}, u32[]{:S(2)}, u32[]{:S(2)}) async-start(bf16[8,64,768]{2,1,0:T(8,128)(2,1)} %param.3), calls=%async_computation.1 | async-start | bytes 1572864 | tf_op jit(solution)/shard_map/cond/branch_1_fun/all_to_all | solution.py:183
  61.0 10.6 %all-to-all-done.1.refs_0_ = bf16[8,64,768]{2,1,0:T(8,128)(2,1)S(1)} async-done(((bf16[8,64,768]{2,1,0:T(8,128)(2,1)}), bf16[8,64,768]{2,1,0:T(8,128)(2,1)S(1)}, u32[]{:S(2)}, u32[]{:S(2)}) %all-to-all-start.1) | async-done | bytes 786464 | tf_op jit(solution)/shard_map/cond/branch_1_fun/all_to_all | solution.py:183
  71.7 1.0 unstage.6
  72.8 0.7 collective-permute-start.11
  73.6 0.7 collective-permute-start.10
  74.4 0.7 collective-permute-start.13
  75.2 0.7 collective-permute-start.12
  76.0 1.3 collective-permute-start.15
  77.4 1.3 collective-permute-start.14
  78.8 1.3 saved_far_2.1
  80.0 4.2 %turn_far_2.1 = (f32[1,4096]{1,0:T(1,128)S(1)}, bf16[256,4096]{1,0:T(8,128)(2,1)S(1)}, bf16[4096,256]{1,0:T(8,128)(2,1)S(1)}) custom-call(bf16[2,4096,256]{2,1,0:T(8,128)(2,1)} %refs_0_.13, bf16[2,256,4096]{2,1,0:T(8,128)(2,1)} %refs_1_.15, f32[2,4096]{1,0:T(2,128)S(1)} %copy-done.3), custom_call_target="tpu_custom_call" | custom-call | flops 1 | bytes 1 | tf_op jit(solution)/shard_map/turn_far_2/pallas_call | solution.py:51
  84.3 1.5 collective-permute-done.15.refs_0_
  85.7 1.5 backward_8_0.1
  87.2 3.5 %collective-permute-start.17 = (bf16[32,4096]{1,0:T(8,128)(2,1)S(1)}, bf16[32,4096]{1,0:T(8,128)(2,1)S(1)}, u32[]{:S(2)}, u32[]{:S(2)}) collective-permute-start(bf16[32,4096]{1,0:T(8,128)(2,1)S(1)} %get-tuple-element.371), channel_id=1, source_target_pairs={{32,48},{80,64},{33,49},{81,65},{34,50},{82,66},{35,51},{83,67},{3... | collective-permute-start | bytes 786440 | tf_op jit(solution)/shard_map/ppermute | solution.py:171
  90.7 1.5 backward_8_1.1
  92.2 1.3 collective-permute-start.16
  93.5 1.3 saved_far_1.1
  94.8 4.2 %turn_far_1.1 = (f32[1,4096]{1,0:T(1,128)S(1)}, bf16[256,4096]{1,0:T(8,128)(2,1)S(1)}, bf16[4096,256]{1,0:T(8,128)(2,1)S(1)}) custom-call(bf16[2,4096,256]{2,1,0:T(8,128)(2,1)} %refs_0_.13, bf16[2,256,4096]{2,1,0:T(8,128)(2,1)} %refs_1_.15, f32[2,4096]{1,0:T(2,128)S(1)} %copy-done.3), custom_call_target="tpu_custom_call" | custom-call | flops 1 | bytes 1 | tf_op jit(solution)/shard_map/turn_far_1/pallas_call | solution.py:51
  99.3 1.3 collective-permute-start.19
  100.6 0.5 collective-permute-done.16.refs_0_
  101.1 1.3 collective-permute-start.18
  102.4 7.8 %collective-permute-done.19.refs_0_ = bf16[32,4096]{1,0:T(8,128)(2,1)S(1)} collective-permute-done((bf16[32,4096]{1,0:T(8,128)(2,1)S(1)}, bf16[32,4096]{1,0:T(8,128)(2,1)S(1)}, u32[]{:S(2)}, u32[]{:S(2)}) %collective-permute-start.19) | collective-permute-done | bytes 262176 | tf_op jit(solution)/shard_map/ppermute | solution.py:171
  110.2 1.5 backward_10_0.1
  111.7 1.3 collective-permute-start.21
  113.0 0.8 collective-permute-done.18.refs_0_
  113.8 1.4 backward_10_1.1
  115.3 1.3 collective-permute-start.20
  116.8 1.8 %collective-permute-done.21.refs_0_ = bf16[32,4096]{1,0:T(8,128)(2,1)S(1)} collective-permute-done((bf16[32,4096]{1,0:T(8,128)(2,1)S(1)}, bf16[32,4096]{1,0:T(8,128)(2,1)S(1)}, u32[]{:S(2)}, u32[]{:S(2)}) %collective-permute-start.21) | collective-permute-done | bytes 262176 | tf_op jit(solution)/shard_map/ppermute | solution.py:171
  118.6 0.7 collective-permute-start.23
  119.3 3.1 %collective-permute-done.20.refs_0_ = bf16[32,4096]{1,0:T(8,128)(2,1)S(1)} collective-permute-done((bf16[32,4096]{1,0:T(8,128)(2,1)S(1)}, bf16[32,4096]{1,0:T(8,128)(2,1)S(1)}, u32[]{:S(2)}, u32[]{:S(2)}) %collective-permute-start.20) | collective-permute-done | bytes 262176 | tf_op jit(solution)/shard_map/ppermute | solution.py:171
  122.5 0.7 collective-permute-start.22
  123.6 1.3 copy-done.4
  125.1 33.6 %conditional.7 = ((f32[2,2,256,256]{3,2,1,0:T(8,128)S(1)}, bf16[2,2,256,256]{3,2,1,0:T(8,128)(2,1)S(1)})) conditional(s32[]{:T(128)} %clamp.9, (bf16[8,64,768]{2,1,0:T(8,128)(2,1)}, bf16[8,64,768]{2,1,0:T(8,128)(2,1)S(1)}, bf16[8,128,768]{2,1,0:T(8,128)(2,1)S(1)}) %tuple.99, (bf16[8,128,768]{2,1,0:T(8,128)(2,1)}, ...), branch_computations={%region_8.9_spmd, %region_9.10_spmd, %region_10.11_spmd, %region_1... | conditional | flops 1 | bytes 9437221 | solution.py:588
  125.1 32.5 %all_to_all.38.refs_0_ = bf16[8,192,768]{2,1,0:T(8,128)(2,1)S(1)} all-to-all(bf16[8,192,768]{2,1,0:T(8,128)(2,1)} %get-tuple-element.34), channel_id=1, replica_groups={{0,2,4,6,8,10,12,14},{1,3,5,7,9,11,13,15},{16,18,20,22,24,26,28,30},{17..., dimensions={0} | all-to-all | bytes 4718592 | tf_op jit(solution)/shard_map/cond/branch_2_fun/all_to_all | solution.py:183
  157.6 1.1 products.6
  158.8 1.9 %collective-permute-done.24 = bf16[2,2,256,256]{3,2,1,0:T(8,128)(2,1)S(1)} collective-permute-done((bf16[2,2,256,256]{3,2,1,0:T(8,128)(2,1)S(1)}, bf16[2,2,256,256]{3,2,1,0:T(8,128)(2,1)S(1)}, u32[]{:S(2)}, u32[]{:S(2)}) %collective-permute-start.24) | collective-permute-done | bytes 524320 | tf_op jit(solution)/shard_map/ppermute | solution.py:605
  161.0 10.7 %collective-permute-done.25 = bf16[2,256,256]{2,1,0:T(8,128)(2,1)S(1)} collective-permute-done((bf16[2,256,256]{2,1,0:T(8,128)(2,1)S(1)}, bf16[2,256,256]{2,1,0:T(8,128)(2,1)S(1)}, u32[]{:S(2)}, u32[]{:S(2)}) %collective-permute-start.25) | collective-permute-done | bytes 262176 | tf_op jit(solution)/shard_map/ppermute | solution.py:607
  171.7 1.5 multiply_reduce_fusion
  (71 shorter events, 2.8 us)
Async XLA Ops:
  0.6 0.8 copy-start.2
  1.5 2.9 %collective-permute-start.1 = (bf16[32,4096]{1,0:T(8,128)(2,1)S(1)}, bf16[32,4096]{1,0:T(8,128)(2,1)S(1)}, u32[]{:S(2)}, u32[]{:S(2)}) collective-permute-start(bf16[32,4096]{1,0:T(8,128)(2,1)S(1)} %get-tuple-element.239), channel_id=1, source_target_pairs={{0,16},{112,96},{1,17},{113,97},{2,18},{114,98},{3,19},{115,99},{4... | collective-permute-start | bytes 786440 | tf_op jit(solution)/shard_map/ppermute | solution.py:171
  2.2 0.8 copy-start.3
  2.3 5.0 %collective-permute-start = (bf16[32,4096]{1,0:T(8,128)(2,1)S(1)}, bf16[32,4096]{1,0:T(8,128)(2,1)S(1)}, u32[]{:S(2)}, u32[]{:S(2)}) collective-permute-start(bf16[32,4096]{1,0:T(8,128)(2,1)S(1)} %get-tuple-element.235), channel_id=1, source_target_pairs={{0,16},{112,96},{1,17},{113,97},{2,18},{114,98},{3,19},{115,99},{4... | collective-permute-start | bytes 786440 | tf_op jit(solution)/shard_map/ppermute | solution.py:171
  3.1 1.3 copy-start
  4.4 1.6 copy-start.1
  6.0 21.3 %collective-permute-start.3 = (bf16[32,4096]{1,0:T(8,128)(2,1)S(1)}, bf16[32,4096]{1,0:T(8,128)(2,1)S(1)}, u32[]{:S(2)}, u32[]{:S(2)}) collective-permute-start(bf16[32,4096]{1,0:T(8,128)(2,1)S(1)} %get-tuple-element.258), channel_id=1, source_target_pairs={{16,32},{96,80},{17,33},{97,81},{18,34},{98,82},{19,35},{99,83},{2... | collective-permute-start | bytes 786440 | tf_op jit(solution)/shard_map/ppermute | solution.py:171
  7.4 24.0 %collective-permute-start.2 = (bf16[32,4096]{1,0:T(8,128)(2,1)S(1)}, bf16[32,4096]{1,0:T(8,128)(2,1)S(1)}, u32[]{:S(2)}, u32[]{:S(2)}) collective-permute-start(bf16[32,4096]{1,0:T(8,128)(2,1)S(1)} %get-tuple-element.245), channel_id=1, source_target_pairs={{16,32},{96,80},{17,33},{97,81},{18,34},{98,82},{19,35},{99,83},{2... | collective-permute-start | bytes 786440 | tf_op jit(solution)/shard_map/ppermute | solution.py:171
  29.0 6.0 %collective-permute-start.5 = (bf16[32,4096]{1,0:T(8,128)(2,1)S(1)}, bf16[32,4096]{1,0:T(8,128)(2,1)S(1)}, u32[]{:S(2)}, u32[]{:S(2)}) collective-permute-start(bf16[32,4096]{1,0:T(8,128)(2,1)S(1)} %get-tuple-element.275), channel_id=1, source_target_pairs={{32,48},{80,64},{33,49},{81,65},{34,50},{82,66},{35,51},{83,67},{3... | collective-permute-start | bytes 786440 | tf_op jit(solution)/shard_map/ppermute | solution.py:171
  33.1 6.7 %collective-permute-start.4 = (bf16[32,4096]{1,0:T(8,128)(2,1)S(1)}, bf16[32,4096]{1,0:T(8,128)(2,1)S(1)}, u32[]{:S(2)}, u32[]{:S(2)}) collective-permute-start(bf16[32,4096]{1,0:T(8,128)(2,1)S(1)} %get-tuple-element.265), channel_id=1, source_target_pairs={{32,48},{80,64},{33,49},{81,65},{34,50},{82,66},{35,51},{83,67},{3... | collective-permute-start | bytes 786440 | tf_op jit(solution)/shard_map/ppermute | solution.py:171
  35.1 11.1 %collective-permute-start.7 = (bf16[32,4096]{1,0:T(8,128)(2,1)S(1)}, bf16[32,4096]{1,0:T(8,128)(2,1)S(1)}, u32[]{:S(2)}, u32[]{:S(2)}) collective-permute-start(bf16[32,4096]{1,0:T(8,128)(2,1)S(1)} %get-tuple-element.289), channel_id=1, source_target_pairs={{48,32},{64,80},{49,33},{65,81},{50,34},{66,82},{51,35},{67,83},{5... | collective-permute-start | bytes 786440 | tf_op jit(solution)/shard_map/ppermute | solution.py:171
  39.9 12.1 %collective-permute-start.6 = (bf16[32,4096]{1,0:T(8,128)(2,1)S(1)}, bf16[32,4096]{1,0:T(8,128)(2,1)S(1)}, u32[]{:S(2)}, u32[]{:S(2)}) collective-permute-start(bf16[32,4096]{1,0:T(8,128)(2,1)S(1)} %get-tuple-element.282), channel_id=1, source_target_pairs={{48,32},{64,80},{49,33},{65,81},{50,34},{66,82},{51,35},{67,83},{5... | collective-permute-start | bytes 786440 | tf_op jit(solution)/shard_map/ppermute | solution.py:171
  47.9 24.8 %collective-permute-start.9 = (bf16[32,4096]{1,0:T(8,128)(2,1)S(1)}, bf16[32,4096]{1,0:T(8,128)(2,1)S(1)}, u32[]{:S(2)}, u32[]{:S(2)}) collective-permute-start(bf16[32,4096]{1,0:T(8,128)(2,1)S(1)} %get-tuple-element.313), channel_id=1, source_target_pairs={{32,16},{80,96},{33,17},{81,97},{34,18},{82,98},{35,19},{83,99},{3... | collective-permute-start | bytes 786440 | tf_op jit(solution)/shard_map/ppermute | solution.py:171
  53.6 19.9 %collective-permute-start.8 = (bf16[32,4096]{1,0:T(8,128)(2,1)S(1)}, bf16[32,4096]{1,0:T(8,128)(2,1)S(1)}, u32[]{:S(2)}, u32[]{:S(2)}) collective-permute-start(bf16[32,4096]{1,0:T(8,128)(2,1)S(1)} %get-tuple-element.296), channel_id=1, source_target_pairs={{32,16},{80,96},{33,17},{81,97},{34,18},{82,98},{35,19},{83,99},{3... | collective-permute-start | bytes 786440 | tf_op jit(solution)/shard_map/ppermute | solution.py:171
  55.0 16.7 %all-to-all-start.1 = ((bf16[8,64,768]{2,1,0:T(8,128)(2,1)}), bf16[8,64,768]{2,1,0:T(8,128)(2,1)S(1)}, u32[]{:S(2)}, u32[]{:S(2)}) async-start(bf16[8,64,768]{2,1,0:T(8,128)(2,1)} %param.3), calls=%async_computation.1 | async-start | bytes 1572864 | tf_op jit(solution)/shard_map/cond/branch_1_fun/all_to_all | solution.py:183
  72.8 1.4 collective-permute-start.11
  73.6 1.5 collective-permute-start.10
  74.4 1.6 collective-permute-start.13
  75.2 2.2 %collective-permute-start.12 = (bf16[32,4096]{1,0:T(8,128)(2,1)S(1)}, bf16[32,4096]{1,0:T(8,128)(2,1)S(1)}, u32[]{:S(2)}, u32[]{:S(2)}) collective-permute-start(bf16[32,4096]{1,0:T(8,128)(2,1)S(1)} %get-tuple-element.328), channel_id=1, source_target_pairs={{0,16},{112,96},{1,17},{113,97},{2,18},{114,98},{3,19},{115,99},{4... | collective-permute-start | bytes 786440 | tf_op jit(solution)/shard_map/ppermute | solution.py:171
  76.0 9.7 %collective-permute-start.15 = (bf16[32,4096]{1,0:T(8,128)(2,1)S(1)}, bf16[32,4096]{1,0:T(8,128)(2,1)S(1)}, u32[]{:S(2)}, u32[]{:S(2)}) collective-permute-start(bf16[32,4096]{1,0:T(8,128)(2,1)S(1)} %get-tuple-element.357), channel_id=1, source_target_pairs={{16,32},{96,80},{17,33},{97,81},{18,34},{98,82},{19,35},{99,83},{2... | collective-permute-start | bytes 786440 | tf_op jit(solution)/shard_map/ppermute | solution.py:171
  77.4 13.3 %collective-permute-start.14 = (bf16[32,4096]{1,0:T(8,128)(2,1)S(1)}, bf16[32,4096]{1,0:T(8,128)(2,1)S(1)}, u32[]{:S(2)}, u32[]{:S(2)}) collective-permute-start(bf16[32,4096]{1,0:T(8,128)(2,1)S(1)} %get-tuple-element.337), channel_id=1, source_target_pairs={{16,32},{96,80},{17,33},{97,81},{18,34},{98,82},{19,35},{99,83},{2... | collective-permute-start | bytes 786440 | tf_op jit(solution)/shard_map/ppermute | solution.py:171
  87.2 11.8 %collective-permute-start.17 = (bf16[32,4096]{1,0:T(8,128)(2,1)S(1)}, bf16[32,4096]{1,0:T(8,128)(2,1)S(1)}, u32[]{:S(2)}, u32[]{:S(2)}) collective-permute-start(bf16[32,4096]{1,0:T(8,128)(2,1)S(1)} %get-tuple-element.371), channel_id=1, source_target_pairs={{32,48},{80,64},{33,49},{81,65},{34,50},{82,66},{35,51},{83,67},{3... | collective-permute-start | bytes 786440 | tf_op jit(solution)/shard_map/ppermute | solution.py:171
  92.2 8.9 %collective-permute-start.16 = (bf16[32,4096]{1,0:T(8,128)(2,1)S(1)}, bf16[32,4096]{1,0:T(8,128)(2,1)S(1)}, u32[]{:S(2)}, u32[]{:S(2)}) collective-permute-start(bf16[32,4096]{1,0:T(8,128)(2,1)S(1)} %get-tuple-element.361), channel_id=1, source_target_pairs={{32,48},{80,64},{33,49},{81,65},{34,50},{82,66},{35,51},{83,67},{3... | collective-permute-start | bytes 786440 | tf_op jit(solution)/shard_map/ppermute | solution.py:171
  99.3 10.9 %collective-permute-start.19 = (bf16[32,4096]{1,0:T(8,128)(2,1)S(1)}, bf16[32,4096]{1,0:T(8,128)(2,1)S(1)}, u32[]{:S(2)}, u32[]{:S(2)}) collective-permute-start(bf16[32,4096]{1,0:T(8,128)(2,1)S(1)} %get-tuple-element.376), channel_id=1, source_target_pairs={{48,32},{64,80},{49,33},{65,81},{50,34},{66,82},{51,35},{67,83},{5... | collective-permute-start | bytes 786440 | tf_op jit(solution)/shard_map/ppermute | solution.py:171
  101.1 12.7 %collective-permute-start.18 = (bf16[32,4096]{1,0:T(8,128)(2,1)S(1)}, bf16[32,4096]{1,0:T(8,128)(2,1)S(1)}, u32[]{:S(2)}, u32[]{:S(2)}) collective-permute-start(bf16[32,4096]{1,0:T(8,128)(2,1)S(1)} %get-tuple-element.375), channel_id=1, source_target_pairs={{48,32},{64,80},{49,33},{65,81},{50,34},{66,82},{51,35},{67,83},{5... | collective-permute-start | bytes 786440 | tf_op jit(solution)/shard_map/ppermute | solution.py:171
  111.7 6.9 %collective-permute-start.21 = (bf16[32,4096]{1,0:T(8,128)(2,1)S(1)}, bf16[32,4096]{1,0:T(8,128)(2,1)S(1)}, u32[]{:S(2)}, u32[]{:S(2)}) collective-permute-start(bf16[32,4096]{1,0:T(8,128)(2,1)S(1)} %get-tuple-element.391), channel_id=1, source_target_pairs={{32,16},{80,96},{33,17},{81,97},{34,18},{82,98},{35,19},{83,99},{3... | collective-permute-start | bytes 786440 | tf_op jit(solution)/shard_map/ppermute | solution.py:171
  115.3 7.2 %collective-permute-start.20 = (bf16[32,4096]{1,0:T(8,128)(2,1)S(1)}, bf16[32,4096]{1,0:T(8,128)(2,1)S(1)}, u32[]{:S(2)}, u32[]{:S(2)}) collective-permute-start(bf16[32,4096]{1,0:T(8,128)(2,1)S(1)} %get-tuple-element.381), channel_id=1, source_target_pairs={{32,16},{80,96},{33,17},{81,97},{34,18},{82,98},{35,19},{83,99},{3... | collective-permute-start | bytes 786440 | tf_op jit(solution)/shard_map/ppermute | solution.py:171
  118.6 4.8 %collective-permute-start.23 = (bf16[32,4096]{1,0:T(8,128)(2,1)S(1)}, bf16[32,4096]{1,0:T(8,128)(2,1)S(1)}, u32[]{:S(2)}, u32[]{:S(2)}) collective-permute-start(bf16[32,4096]{1,0:T(8,128)(2,1)S(1)} %get-tuple-element.405), channel_id=1, source_target_pairs={{16,0},{96,112},{17,1},{97,113},{18,2},{98,114},{19,3},{99,115},{2... | collective-permute-start | bytes 786440 | tf_op jit(solution)/shard_map/ppermute | solution.py:171
  122.5 1.0 collective-permute-start.22
  123.5 1.4 copy-start.4
  123.5 1.6 copy-start.6
  125.1 32.5 %copy-start.7 = (bf16[8,64,768]{2,1,0:T(8,128)(2,1)S(1)}, bf16[8,64,768]{2,1,0:T(8,128)(2,1)}, u32[]{:S(2)}) copy-start(bf16[8,64,768]{2,1,0:T(8,128)(2,1)} %get-tuple-element.35.refs_1_) | copy-start | bytes 2359300 | tf_op jit(solution)/shard_map/cond
  158.7 2.3 %slice-start = ((f32[2,4096]{1,0:T(2,128)}), f32[1,4096]{1,0:T(1,128)S(1)}, s32[]{:S(2)}) async-start(f32[2,4096]{1,0:T(2,128)} %refs_2_.19), calls=%async_computation.9 | async-start | bytes 32768 | tf_op jit(solution)/shard_map/slice | solution.py:609
  158.7 2.0 %collective-permute-start.24 = (bf16[2,2,256,256]{3,2,1,0:T(8,128)(2,1)S(1)}, bf16[2,2,256,256]{3,2,1,0:T(8,128)(2,1)S(1)}, u32[]{:S(2)}, u32[]{:S(2)}) collective-permute-start(bf16[2,2,256,256]{3,2,1,0:T(8,128)(2,1)S(1)} %get-tuple-element.418), channel_id=1, source_target_pairs={{0,1},{1,0},{2,3},{3,2},{4,5},{5,4},{6,7},{7,6},{8,9},{9,8},{10,11... | collective-permute-start | bytes 1572872 | tf_op jit(solution)/shard_map/ppermute | solution.py:605
  160.8 10.8 %collective-permute-start.25 = (bf16[2,256,256]{2,1,0:T(8,128)(2,1)S(1)}, bf16[2,256,256]{2,1,0:T(8,128)(2,1)S(1)}, u32[]{:S(2)}, u32[]{:S(2)}) collective-permute-start(bf16[2,256,256]{2,1,0:T(8,128)(2,1)S(1)} %fusion.1), channel_id=1, source_target_pairs={{0,112},{16,96},{32,80},{48,64},{64,48},{80,32},{96,16},{112,0},{1... | collective-permute-start | bytes 786440 | tf_op jit(solution)/shard_map/ppermute | solution.py:607
  161.0 10.8 %slice-start.1 = ((bf16[2,4096,256]{2,1,0:T(8,128)(2,1)}), bf16[1,4096,256]{2,1,0:T(8,128)(2,1)S(1)}, s32[]{:S(2)}) async-start(bf16[2,4096,256]{2,1,0:T(8,128)(2,1)} %refs_0_.13), calls=%async_computation.10 | async-start | bytes 4194304 | tf_op jit(solution)/shard_map/slice | solution.py:610

commit v3 on v2

--- a/solution.py
+++ b/solution.py
@@ -179,9 +179,9 @@
             copy.start()
         wait_all(copies)
 
-    def exchange(array, keep_in_vmem=False):
+    def exchange(array, raw=False):
         array = lax.all_to_all(array, "dp", 0, 0, axis_index_groups=same_core, tiled=False)
-        if keep_in_vmem:
+        if raw:
             return array
         array = pltpu.with_memory_space_constraint(array, pltpu.VMEM)
         (target,) = new_boxes("unstage_box", [array.shape])
@@ -198,7 +198,7 @@
         return [(a, VMEM) for a in arrays]
 
     (box_early,) = new_boxes("box_early", [(chips, rows, pack)])
-    box_two, box_far = new_boxes("box_far", [(chips, rows, pack), (chips, 2 * rows, pack)])
+    (box_two,) = new_boxes("box_two", [(chips, rows, pack)])
     box_near, box_one = new_boxes("box_near", [(chips, 2 * rows, pack), (chips, rows, pack)])
     box_late, box_late_two, box_end = new_boxes(
         "box_late", [(chips, n * rows, pack) for n in (2, 3, 1)]
@@ -333,8 +333,9 @@
         )
         return [outs[i * len(shapes) : (i + 1) * len(shapes)] for i in range(len(layers))]
 
-    def forward_kernel(stage, slots, m, reads, box, hats, kept, sent, stash, stash_kept, sems):
+    def forward_kernel(stage, slots, m, reads, *refs):
         moved = reads[0]
+        boxes, (hats, kept, sent, stash, stash_kept, sems) = refs[:-6], refs[-6:]
         layers = list(slots)
         weights = [reads[1 + 3 * i : 4 + 3 * i] for i in range(len(layers))]
         fold, _ = place()
@@ -345,7 +346,7 @@
                 Keeper(
                     m,
                     (stash.at[i], stash_kept.at[i], sems.at[i]),
-                    box,
+                    boxes[min(i, len(boxes) - 1)],
                     slot=slots[layer],
                     layer=layer,
                     hats=hats,
@@ -359,56 +360,47 @@
             for out in outs:
                 out.wait()
 
-    def forward_stage(stage, slots, box, weights):
+    def forward_stage(stage, slots, boxes, weights):
         nonlocal hats, kept
         for m in range(MICROS):
-            box, hats, kept, sent = call(
+            *boxes, hats, kept, sent = call(
                 functools.partial(forward_kernel, stage, slots, m),
                 "forward_%d_%d" % (stage, m),
                 in_vmem(moved[m], *[a for layer in slots for a in weights[layer]]),
-                places=(box, hats, kept),
+                places=(*boxes, hats, kept),
                 new=(block,),
                 scratch=keeping(len(slots)),
             )
             moved[m] = send_on(sent, stage)
-        return box
+        return boxes
 
     weights = fresh_weights("load_1", lambda fold: fold == 1, (0,), 1, 0)
-    box_early = forward_stage(1, {0: 0}, box_early, weights)
+    (box_early,) = forward_stage(1, {0: 0}, [box_early], weights)
 
     def none(name, array):
         return new_boxes(name, [array.shape])[0]
 
     box_early, kept = lax.optimization_barrier((box_early, kept))
     got_early = lax.cond(fold_here <= 1, exchange, functools.partial(none, "none_early"), box_early)
-    got_early, box_two, box_far, kept, hats, raw_in, raw_out = lax.optimization_barrier(
-        (got_early, box_two, box_far, kept, hats, raw_in, raw_out)
+    got_early, box_two, kept, hats, raw_in, raw_out = lax.optimization_barrier(
+        (got_early, box_two, kept, hats, raw_in, raw_out)
     )
     weights = fresh_weights("load_2", lambda fold: fold == 2, (0,), 1, 0)
-    box_two = forward_stage(2, {0: 0}, box_two, weights)
+    (box_two,) = forward_stage(2, {0: 0}, [box_two], weights)
     raw_in, raw_out, kept = lax.optimization_barrier((raw_in, raw_out, kept))
     weights = fresh_weights("load_3", lambda fold: fold == 3, (0, 1), 1, 0)
-    box_far = forward_stage(3, {0: 0, 1: 1}, box_far, weights)
+    box_two, box_late_two = forward_stage(3, {0: 0, 1: 2}, [box_two, box_late_two], weights)
     raw_in, raw_out, kept = lax.optimization_barrier((raw_in, raw_out, kept))
     weights = fresh_weights("load_4", lambda fold: fold == 2, (1,), 1, 0)
-    box_late_two = forward_stage(4, {1: 2}, box_late_two, [None, *weights])
-
-    box_two, box_far, kept = lax.optimization_barrier((box_two, box_far, kept))
-    got_two, got_far = lax.switch(
-        jnp.maximum(fold_here - 1, 0),
-        (
-            lambda two, far: (none("none_two", two), none("none_far", far)),
-            lambda two, far: (exchange(two), none("none_far", far)),
-            lambda two, far: (none("none_two", two), exchange(far)),
-        ),
-        box_two,
-        box_far,
-    )
-    got_two, got_far, box_near, box_one, kept, hats, raw_in, raw_out = lax.optimization_barrier(
-        (got_two, got_far, box_near, box_one, kept, hats, raw_in, raw_out)
+    (box_late_two,) = forward_stage(4, {1: 2}, [box_late_two], [None, *weights])
+
+    box_two, kept = lax.optimization_barrier((box_two, kept))
+    got_two = lax.cond(fold_here >= 2, exchange, functools.partial(none, "none_two"), box_two)
+    got_two, box_near, box_one, kept, hats, raw_in, raw_out = lax.optimization_barrier(
+        (got_two, box_near, box_one, kept, hats, raw_in, raw_out)
     )
     (near,) = fresh_weights("load_near", lambda fold: fold <= 1, (1,), 1, 1)
-    box_one = forward_stage(5, {1: 0}, box_one, [None, near[:3]])
+    (box_one,) = forward_stage(5, {1: 0}, [box_one], [None, near[:3]])
 
     def middle_kernel(m, reads, box, kept, sent, staged, sem, stash, stash_kept, sems):
         moved, cotangent, gain, weight_in, weight_in_t, weight_out_t = reads
@@ -534,13 +526,27 @@
     kept, raw_in, raw_out = lax.optimization_barrier((kept, raw_in, raw_out))
     (far_1,) = fresh_weights("turn_far_1", lambda fold: fold >= 2, (0,), 0, 1)
     far_1 = (*far_1, *saved_rows("saved_far_1", lambda fold: fold >= 2, 0))
-    box_late = backward_stage(9, {1: 0, 0: 1}, box_late, [far_1, far_2])
+    box_late_two = backward_stage(9, {1: 0, 0: 1}, box_late_two, [far_1, far_2])
     box_late_two = backward_stage(10, {0: 1}, box_late_two, [far_1])
     kept, raw_in, raw_out = lax.optimization_barrier((kept, raw_in, raw_out))
     (near_1,) = fresh_weights("turn_11", lambda fold: fold == 1, (0,), 0, 1)
     near_1 = (*near_1, *saved_rows("saved_11", lambda fold: fold == 1, 0))
     box_late = backward_stage(11, {0: 1}, box_late, [near_1])
-    kept, raw_in, raw_out = lax.optimization_barrier((kept, raw_in, raw_out))
+
+    box_late, box_late_two, kept = lax.optimization_barrier((box_late, box_late_two, kept))
+    got_late, got_late_two = lax.switch(
+        jnp.minimum(fold_here, 2),
+        (
+            lambda late, late_two: (none("none_late", late), none("none_late_two", late_two)),
+            lambda late, late_two: (exchange(late, raw=True), none("none_late_two", late_two)),
+            lambda late, late_two: (none("none_late", late), exchange(late_two, raw=True)),
+        ),
+        box_late,
+        box_late_two,
+    )
+    got_late, got_late_two, box_end, kept, raw_in, raw_out = lax.optimization_barrier(
+        (got_late, got_late_two, box_end, kept, raw_in, raw_out)
+    )
     (near_1,) = fresh_weights("turn_12", lambda fold: fold == 0, (0,), 0, 1)
     near_1 = (*near_1, *saved_rows("saved_12", lambda fold: fold == 0, 0))
     box_end = backward_stage(LAST, {0: 0}, box_end, [near_1])
@@ -574,33 +580,28 @@
             scratch=[pltpu.VMEM((2 * branch, branch), f32), pltpu.VMEM((branch, 2 * branch), f32)],
         )
 
-    def last(*pick):
-        def branch(now, *before):
-            arrived = exchange(now, keep_in_vmem=True)
-            return finish("products", pick, arrived, *before)
-
-        return branch
-
-    end_0 = last(((1, 0), (0, 0)), ((2, 0), (2, 1)))
-    end_1 = last(((1, 0), (0, 1)), ((2, 0), (0, 0)))
-    end_2 = last(((1, 0), (0, 1)), ((0, 2), (0, 0)))
-    end_3 = last(((1, 0), (0, 1)), ((1, 1), (0, 0)))
+    near_pick = (((0, 0), (1, 1)), ((2, 0), (1, 0)))
+    far_pick = (((0, 0), (1, 1)), ((1, 2), (1, 0)))
     keep, send = lax.switch(
-        fold_here,
+        jnp.minimum(fold_here, 2),
         (
-            lambda end, late, late_two, early, near, one, two, far: end_0(end, early, near),
-            lambda end, late, late_two, early, near, one, two, far: end_1(late, early, one),
-            lambda end, late, late_two, early, near, one, two, far: end_2(late_two, two),
-            lambda end, late, late_two, early, near, one, two, far: end_3(late, far),
+            lambda end, late, late_two, early, near, one, two: finish(
+                "products_0", (((0, 0), (1, 0)), ((2, 0), (2, 1))), early, exchange(end, raw=True), near
+            ),
+            lambda end, late, late_two, early, near, one, two: finish(
+                "products_1", near_pick, early, late, one
+            ),
+            lambda end, late, late_two, early, near, one, two: finish(
+                "products_2", far_pick, two, late_two
+            ),
         ),
         box_end,
-        box_late,
-        box_late_two,
+        got_late,
+        got_late_two,
         got_early,
         got_near,
         got_one,
         got_two,
-        got_far,
     )
     total = keep + lax.ppermute(send, "dp", [(i, i ^ 1) for i in range(parts)]).astype(f32)
     mirror = [(s, sections - 1 - s) for s in range(sections)]

time: 175 us -> 175 us (level)
  blocking collectives: 32.5 us -> 0 us
  waiting for transfers between devices: 65.6 us -> 91.5 us
  starting transfers between devices: 34.6 us -> 40.5 us
    all_to_all x1 -> x0, blocking collectives: 32.5 us -> none  [exchange(): lax.all_to_all(array, 'dp', 0, 0, axis_index_groups=same_core, tiled=False)]
    all_to_all x1 -> x2, waiting for transfers between devices: 10.6 us -> 39.8 us  [exchange(): lax.all_to_all(array, 'dp', 0, 0, axis_index_groups=same_core, tiled=False)]
    all_to_all x1 -> x2, starting transfers between devices: 6.04 us -> 13.9 us  [exchange(): lax.all_to_all(array, 'dp', 0, 0, axis_index_groups=same_core, tiled=False)]
    ppermute x24, waiting for transfers between devices: 42.3 us -> 39.1 us  [send_on(): return lax.ppermute(sent, 'section', pairs)]
    ppermute x24, starting transfers between devices: 28.4 us -> 26.4 us  [send_on(): return lax.ppermute(sent, 'section', pairs)]
  transfers between devices with their start and end apart: 27 -> 28, of which waited for: 15 -> 14; matrix products, arithmetic and copies ran while one was open for 0% -> 0% of each run, Pallas kernels for 18% -> 18%
where the time goes in v3:
time: 175 us; the launch traced here: 174 us
  waiting for transfers between devices  91.5 us (52%)
  starting transfers between devices  40.5 us (23%)
  Pallas kernels  33.7 us (19%)
  local copies, waits for them, and re-layouts  5.23 us (3%)
    all_to_all x2, waiting for transfers between devices, exchange(): lax.all_to_all(array, 'dp', 0, 0, axis_index_groups=same_core, tiled=False)  39.8 us
    ppermute x24, waiting for transfers between devices, send_on(): return lax.ppermute(sent, 'section', pairs)  39.1 us
    pallas_call x42, Pallas kernels, call(): pl.pallas_call(kernel, out_shape=tuple(shapes), in_specs=[spec for _, spe...  33.7 us
    ppermute x24, starting transfers between devices, send_on(): return lax.ppermute(sent, 'section', pairs)  26.4 us
    all_to_all x2, starting transfers between devices, exchange(): lax.all_to_all(array, 'dp', 0, 0, axis_index_groups=same_core, tiled=False)  13.9 us
    ppermute x1, waiting for transfers between devices, on_device(): lax.ppermute(total[1].astype(bf16), 'section', mirror).astype(f32)  10.7 us
    unnamed x12, local copies, waits for them, and re-layouts  5.17 us
  transfers between devices with their start and end apart: 28, of which 14 were waited for; matrix products, arithmetic and copies ran while one was open for 0% of the time, Pallas kernels for 18%

profile of v3, /device:TPU:18, one launch (start us, length us, event | category | flops | bytes accessed | tf_op | source)
XLA Modules:
  0.0 174.2 jit_solution(3717386475901225049)
XLA Ops:
  0.7 0.7 copy-done.2
  1.5 0.7 collective-permute-start.1
  2.3 0.7 collective-permute-start
  3.1 1.3 copy-done
  4.4 1.6 copy-done.1
  6.0 1.3 collective-permute-start.3
  7.4 1.3 collective-permute-start.2
  8.7 2.2 %load_2.1 = (f32[1,4096]{1,0:T(1,128)S(1)}, bf16[4096,256]{1,0:T(8,128)(2,1)S(1)}, bf16[256,4096]{1,0:T(8,128)(2,1)S(1)}) custom-call(bf16[2,4096,256]{2,1,0:T(8,128)(2,1)} %refs_0_.13, bf16[2,256,4096]{2,1,0:T(8,128)(2,1)} %refs_1_.15, f32[2,4096]{1,0:T(2,128)S(1)} %copy-done.3), custom_call_target="tpu_custom_call" | custom-call | flops 1 | bytes 1 | tf_op jit(solution)/shard_map/load_2/pallas_call | solution.py:51
  11.0 16.3 %collective-permute-done.3.refs_0_ = bf16[32,4096]{1,0:T(8,128)(2,1)S(1)} collective-permute-done((bf16[32,4096]{1,0:T(8,128)(2,1)S(1)}, bf16[32,4096]{1,0:T(8,128)(2,1)S(1)}, u32[]{:S(2)}, u32[]{:S(2)}) %collective-permute-start.3) | collective-permute-done | bytes 262176 | tf_op jit(solution)/shard_map/ppermute | solution.py:171
  27.3 1.6 forward_2_0.1
  28.9 1.3 collective-permute-start.5
  30.2 1.1 collective-permute-done.2.refs_0_
  31.4 1.7 forward_2_1.1
  33.0 1.3 collective-permute-start.4
  34.5 0.3 collective-permute-done.5.refs_0_
  34.9 1.3 collective-permute-start.7
  36.2 3.5 %collective-permute-done.4.refs_0_ = bf16[32,4096]{1,0:T(8,128)(2,1)S(1)} collective-permute-done((bf16[32,4096]{1,0:T(8,128)(2,1)S(1)}, bf16[32,4096]{1,0:T(8,128)(2,1)S(1)}, u32[]{:S(2)}, u32[]{:S(2)}) %collective-permute-start.4) | collective-permute-done | bytes 262176 | tf_op jit(solution)/shard_map/ppermute | solution.py:171
  39.8 1.3 collective-permute-start.6
  41.1 2.2 %load_4.1 = (f32[1,4096]{1,0:T(1,128)S(1)}, bf16[4096,256]{1,0:T(8,128)(2,1)S(1)}, bf16[256,4096]{1,0:T(8,128)(2,1)S(1)}) custom-call(bf16[2,4096,256]{2,1,0:T(8,128)(2,1)} %refs_0_.13, bf16[2,256,4096]{2,1,0:T(8,128)(2,1)} %refs_1_.15, f32[2,4096]{1,0:T(2,128)S(1)} %copy-done.3), custom_call_target="tpu_custom_call" | custom-call | flops 1 | bytes 1 | tf_op jit(solution)/shard_map/load_4/pallas_call | solution.py:51
  43.3 2.7 %collective-permute-done.7.refs_0_ = bf16[32,4096]{1,0:T(8,128)(2,1)S(1)} collective-permute-done((bf16[32,4096]{1,0:T(8,128)(2,1)S(1)}, bf16[32,4096]{1,0:T(8,128)(2,1)S(1)}, u32[]{:S(2)}, u32[]{:S(2)}) %collective-permute-start.7) | collective-permute-done | bytes 262176 | tf_op jit(solution)/shard_map/ppermute | solution.py:171
  46.0 1.7 forward_4_0.1
  47.7 1.3 collective-permute-start.9
  49.0 2.8 %collective-permute-done.6.refs_0_ = bf16[32,4096]{1,0:T(8,128)(2,1)S(1)} collective-permute-done((bf16[32,4096]{1,0:T(8,128)(2,1)S(1)}, bf16[32,4096]{1,0:T(8,128)(2,1)S(1)}, u32[]{:S(2)}, u32[]{:S(2)}) %collective-permute-start.6) | collective-permute-done | bytes 262176 | tf_op jit(solution)/shard_map/ppermute | solution.py:171
  51.8 1.6 forward_4_1.1
  53.4 1.3 collective-permute-start.8
  54.8 17.7 %conditional.6 = (bf16[8,64,768]{2,1,0:T(8,128)(2,1)}) conditional(s32[]{:T(128)} %convert_element_type.25, () %tuple.70, bf16[8,64,768]{2,1,0:T(8,128)(2,1)} %get-tuple-element.300), branch_computations={%region_2.3_spmd, %region_3.4_spmd} | conditional | flops 1 | bytes 2359337 | solution.py:398
  54.8 6.0 %all-to-all-start.1 = ((bf16[8,64,768]{2,1,0:T(8,128)(2,1)}), bf16[8,64,768]{2,1,0:T(8,128)(2,1)S(1)}, u32[]{:S(2)}, u32[]{:S(2)}) async-start(bf16[8,64,768]{2,1,0:T(8,128)(2,1)} %param.3), calls=%async_computation.1 | async-start | bytes 1572864 | tf_op jit(solution)/shard_map/cond/branch_1_fun/all_to_all | solution.py:183
  60.8 10.6 %all-to-all-done.1.refs_0_ = bf16[8,64,768]{2,1,0:T(8,128)(2,1)S(1)} async-done(((bf16[8,64,768]{2,1,0:T(8,128)(2,1)}), bf16[8,64,768]{2,1,0:T(8,128)(2,1)S(1)}, u32[]{:S(2)}, u32[]{:S(2)}) %all-to-all-start.1) | async-done | bytes 786464 | tf_op jit(solution)/shard_map/cond/branch_1_fun/all_to_all | solution.py:183
  71.4 1.0 unstage.5
  72.6 0.7 collective-permute-start.11
  73.3 0.7 collective-permute-start.10
  74.1 0.7 collective-permute-start.13
  74.9 0.7 collective-permute-start.12
  75.8 1.3 collective-permute-start.15
  77.2 1.3 collective-permute-start.14
  78.5 1.3 saved_far_2.1
  79.8 4.2 %turn_far_2.1 = (f32[1,4096]{1,0:T(1,128)S(1)}, bf16[256,4096]{1,0:T(8,128)(2,1)S(1)}, bf16[4096,256]{1,0:T(8,128)(2,1)S(1)}) custom-call(bf16[2,4096,256]{2,1,0:T(8,128)(2,1)} %refs_0_.13, bf16[2,256,4096]{2,1,0:T(8,128)(2,1)} %refs_1_.15, f32[2,4096]{1,0:T(2,128)S(1)} %copy-done.3), custom_call_target="tpu_custom_call" | custom-call | flops 1 | bytes 1 | tf_op jit(solution)/shard_map/turn_far_2/pallas_call | solution.py:51
  84.0 1.5 collective-permute-done.15.refs_0_
  85.5 1.5 backward_8_0.1
  87.0 1.3 collective-permute-start.17
  88.4 1.5 backward_8_1.1
  89.8 1.3 collective-permute-start.16
  91.1 1.3 saved_far_1.1
  92.4 4.2 %turn_far_1.1 = (f32[1,4096]{1,0:T(1,128)S(1)}, bf16[256,4096]{1,0:T(8,128)(2,1)S(1)}, bf16[4096,256]{1,0:T(8,128)(2,1)S(1)}) custom-call(bf16[2,4096,256]{2,1,0:T(8,128)(2,1)} %refs_0_.13, bf16[2,256,4096]{2,1,0:T(8,128)(2,1)} %refs_1_.15, f32[2,4096]{1,0:T(2,128)S(1)} %copy-done.3), custom_call_target="tpu_custom_call" | custom-call | flops 1 | bytes 1 | tf_op jit(solution)/shard_map/turn_far_1/pallas_call | solution.py:51
  96.7 1.5 collective-permute-start.19
  98.3 1.3 collective-permute-start.18
  99.6 6.9 %collective-permute-done.19.refs_0_ = bf16[32,4096]{1,0:T(8,128)(2,1)S(1)} collective-permute-done((bf16[32,4096]{1,0:T(8,128)(2,1)S(1)}, bf16[32,4096]{1,0:T(8,128)(2,1)S(1)}, u32[]{:S(2)}, u32[]{:S(2)}) %collective-permute-start.19) | collective-permute-done | bytes 262176 | tf_op jit(solution)/shard_map/ppermute | solution.py:171
  106.5 1.5 backward_10_0.1
  108.0 1.3 collective-permute-start.21
  109.4 1.5 backward_10_1.1
  110.8 1.3 collective-permute-start.20
  112.4 1.8 %collective-permute-done.21.refs_0_ = bf16[32,4096]{1,0:T(8,128)(2,1)S(1)} collective-permute-done((bf16[32,4096]{1,0:T(8,128)(2,1)S(1)}, bf16[32,4096]{1,0:T(8,128)(2,1)S(1)}, u32[]{:S(2)}, u32[]{:S(2)}) %collective-permute-start.21) | collective-permute-done | bytes 262176 | tf_op jit(solution)/shard_map/ppermute | solution.py:171
  114.2 0.7 collective-permute-start.23
  114.9 2.1 %collective-permute-done.20.refs_0_ = bf16[32,4096]{1,0:T(8,128)(2,1)S(1)} collective-permute-done((bf16[32,4096]{1,0:T(8,128)(2,1)S(1)}, bf16[32,4096]{1,0:T(8,128)(2,1)S(1)}, u32[]{:S(2)}, u32[]{:S(2)}) %collective-permute-start.20) | collective-permute-done | bytes 262176 | tf_op jit(solution)/shard_map/ppermute | solution.py:171
  117.0 0.7 collective-permute-start.22
  117.7 37.1 %conditional.8 = (bf16[8,128,768]{2,1,0:T(8,128)(2,1)}, bf16[8,192,768]{2,1,0:T(8,128)(2,1)}) conditional(s32[]{:T(128)} %clamp.2, () %tuple.78, bf16[8,128,768]{2,1,0:T(8,128)(2,1)} %get-tuple-element.396, bf16[8,192,768]{2,1,0:T(8,128)(2,1)} %get-tuple-element.397), branch_computations={%region_7.8_spmd, %region_8.9_spmd, %region_9.10_spmd} | conditional | bytes 7077936 | solution.py:537
  117.7 7.9 %all-to-all-start.5 = ((bf16[8,192,768]{2,1,0:T(8,128)(2,1)}), bf16[8,192,768]{2,1,0:T(8,128)(2,1)}, u32[]{:S(2)}, u32[]{:S(2)}) async-start(bf16[8,192,768]{2,1,0:T(8,128)(2,1)} %param.9), calls=%async_computation.5 | async-start | bytes 4718592 | tf_op jit(solution)/shard_map/cond/branch_2_fun/all_to_all | solution.py:183
  125.6 29.2 %all-to-all-done.5 = bf16[8,192,768]{2,1,0:T(8,128)(2,1)} async-done(((bf16[8,192,768]{2,1,0:T(8,128)(2,1)}), bf16[8,192,768]{2,1,0:T(8,128)(2,1)}, u32[]{:S(2)}, u32[]{:S(2)}) %all-to-all-start.5) | async-done | bytes 2359328 | tf_op jit(solution)/shard_map/cond/branch_2_fun/all_to_all | solution.py:183
  155.1 1.3 copy-done.4
  156.6 3.0 %conditional.9 = ((f32[2,2,256,256]{3,2,1,0:T(8,128)S(1)}, bf16[2,2,256,256]{3,2,1,0:T(8,128)(2,1)S(1)})) conditional(s32[]{:T(128)} %clamp.2, (bf16[8,64,768]{2,1,0:T(8,128)(2,1)}, bf16[8,64,768]{2,1,0:T(8,128)(2,1)S(1)}, bf16[8,128,768]{2,1,0:T(8,128)(2,1)S(1)}) %tuple.104, (bf16[8,64,768]{2,1,0:T(8,128)(2,1)S(1)}, ...), branch_computations={%region_10.11_spmd, %region_11.12_spmd, %region_12.13_spmd} | conditional | flops 1 | bytes 1572873 | solution.py:585
  156.6 3.0 %products_2.1 = (f32[2,2,256,256]{3,2,1,0:T(8,128)S(1)}, bf16[2,2,256,256]{3,2,1,0:T(8,128)(2,1)S(1)}) custom-call(bf16[8,64,768]{2,1,0:T(8,128)(2,1)} %get-tuple-element.34.refs_0_, bf16[8,192,768]{2,1,0:T(8,128)(2,1)} %get-tuple-element.35.refs_1_), custom_call_target="tpu_custom_call" | custom-call | flops 1 | bytes 1 | tf_op jit(solution)/shard_map/cond/branch_2_fun/products_2/pallas_call | solution.py:51
  159.7 1.9 %collective-permute-done.24 = bf16[2,2,256,256]{3,2,1,0:T(8,128)(2,1)S(1)} collective-permute-done((bf16[2,2,256,256]{3,2,1,0:T(8,128)(2,1)S(1)}, bf16[2,2,256,256]{3,2,1,0:T(8,128)(2,1)S(1)}, u32[]{:S(2)}, u32[]{:S(2)}) %collective-permute-start.24) | collective-permute-done | bytes 524320 | tf_op jit(solution)/shard_map/ppermute | solution.py:606
  161.9 10.7 %collective-permute-done.25 = bf16[2,256,256]{2,1,0:T(8,128)(2,1)S(1)} collective-permute-done((bf16[2,256,256]{2,1,0:T(8,128)(2,1)S(1)}, bf16[2,256,256]{2,1,0:T(8,128)(2,1)S(1)}, u32[]{:S(2)}, u32[]{:S(2)}) %collective-permute-start.25) | collective-permute-done | bytes 262176 | tf_op jit(solution)/shard_map/ppermute | solution.py:608
  172.7 1.5 multiply_reduce_fusion
  (71 shorter events, 2.6 us)
Async XLA Ops:
  0.6 0.8 copy-start.2
  1.5 2.9 %collective-permute-start.1 = (bf16[32,4096]{1,0:T(8,128)(2,1)S(1)}, bf16[32,4096]{1,0:T(8,128)(2,1)S(1)}, u32[]{:S(2)}, u32[]{:S(2)}) collective-permute-start(bf16[32,4096]{1,0:T(8,128)(2,1)S(1)} %get-tuple-element.240), channel_id=1, source_target_pairs={{0,16},{112,96},{1,17},{113,97},{2,18},{114,98},{3,19},{115,99},{4... | collective-permute-start | bytes 786440 | tf_op jit(solution)/shard_map/ppermute | solution.py:171
  2.2 0.8 copy-start.3
  2.3 5.0 %collective-permute-start = (bf16[32,4096]{1,0:T(8,128)(2,1)S(1)}, bf16[32,4096]{1,0:T(8,128)(2,1)S(1)}, u32[]{:S(2)}, u32[]{:S(2)}) collective-permute-start(bf16[32,4096]{1,0:T(8,128)(2,1)S(1)} %get-tuple-element.236), channel_id=1, source_target_pairs={{0,16},{112,96},{1,17},{113,97},{2,18},{114,98},{3,19},{115,99},{4... | collective-permute-start | bytes 786440 | tf_op jit(solution)/shard_map/ppermute | solution.py:171
  3.1 1.3 copy-start
  4.4 1.6 copy-start.1
  6.0 21.3 %collective-permute-start.3 = (bf16[32,4096]{1,0:T(8,128)(2,1)S(1)}, bf16[32,4096]{1,0:T(8,128)(2,1)S(1)}, u32[]{:S(2)}, u32[]{:S(2)}) collective-permute-start(bf16[32,4096]{1,0:T(8,128)(2,1)S(1)} %get-tuple-element.257), channel_id=1, source_target_pairs={{16,32},{96,80},{17,33},{97,81},{18,34},{98,82},{19,35},{99,83},{2... | collective-permute-start | bytes 786440 | tf_op jit(solution)/shard_map/ppermute | solution.py:171
  7.4 24.0 %collective-permute-start.2 = (bf16[32,4096]{1,0:T(8,128)(2,1)S(1)}, bf16[32,4096]{1,0:T(8,128)(2,1)S(1)}, u32[]{:S(2)}, u32[]{:S(2)}) collective-permute-start(bf16[32,4096]{1,0:T(8,128)(2,1)S(1)} %get-tuple-element.246), channel_id=1, source_target_pairs={{16,32},{96,80},{17,33},{97,81},{18,34},{98,82},{19,35},{99,83},{2... | collective-permute-start | bytes 786440 | tf_op jit(solution)/shard_map/ppermute | solution.py:171
  28.9 5.9 %collective-permute-start.5 = (bf16[32,4096]{1,0:T(8,128)(2,1)S(1)}, bf16[32,4096]{1,0:T(8,128)(2,1)S(1)}, u32[]{:S(2)}, u32[]{:S(2)}) collective-permute-start(bf16[32,4096]{1,0:T(8,128)(2,1)S(1)} %get-tuple-element.274), channel_id=1, source_target_pairs={{32,48},{80,64},{33,49},{81,65},{34,50},{82,66},{35,51},{83,67},{3... | collective-permute-start | bytes 786440 | tf_op jit(solution)/shard_map/ppermute | solution.py:171
  33.0 6.7 %collective-permute-start.4 = (bf16[32,4096]{1,0:T(8,128)(2,1)S(1)}, bf16[32,4096]{1,0:T(8,128)(2,1)S(1)}, u32[]{:S(2)}, u32[]{:S(2)}) collective-permute-start(bf16[32,4096]{1,0:T(8,128)(2,1)S(1)} %get-tuple-element.264), channel_id=1, source_target_pairs={{32,48},{80,64},{33,49},{81,65},{34,50},{82,66},{35,51},{83,67},{3... | collective-permute-start | bytes 786440 | tf_op jit(solution)/shard_map/ppermute | solution.py:171
  34.9 11.1 %collective-permute-start.7 = (bf16[32,4096]{1,0:T(8,128)(2,1)S(1)}, bf16[32,4096]{1,0:T(8,128)(2,1)S(1)}, u32[]{:S(2)}, u32[]{:S(2)}) collective-permute-start(bf16[32,4096]{1,0:T(8,128)(2,1)S(1)} %get-tuple-element.290), channel_id=1, source_target_pairs={{48,32},{64,80},{49,33},{65,81},{50,34},{66,82},{51,35},{67,83},{5... | collective-permute-start | bytes 786440 | tf_op jit(solution)/shard_map/ppermute | solution.py:171
  39.8 12.0 %collective-permute-start.6 = (bf16[32,4096]{1,0:T(8,128)(2,1)S(1)}, bf16[32,4096]{1,0:T(8,128)(2,1)S(1)}, u32[]{:S(2)}, u32[]{:S(2)}) collective-permute-start(bf16[32,4096]{1,0:T(8,128)(2,1)S(1)} %get-tuple-element.283), channel_id=1, source_target_pairs={{48,32},{64,80},{49,33},{65,81},{50,34},{66,82},{51,35},{67,83},{5... | collective-permute-start | bytes 786440 | tf_op jit(solution)/shard_map/ppermute | solution.py:171
  47.7 24.8 %collective-permute-start.9 = (bf16[32,4096]{1,0:T(8,128)(2,1)S(1)}, bf16[32,4096]{1,0:T(8,128)(2,1)S(1)}, u32[]{:S(2)}, u32[]{:S(2)}) collective-permute-start(bf16[32,4096]{1,0:T(8,128)(2,1)S(1)} %get-tuple-element.310), channel_id=1, source_target_pairs={{32,16},{80,96},{33,17},{81,97},{34,18},{82,98},{35,19},{83,99},{3... | collective-permute-start | bytes 786440 | tf_op jit(solution)/shard_map/ppermute | solution.py:171
  53.4 19.8 %collective-permute-start.8 = (bf16[32,4096]{1,0:T(8,128)(2,1)S(1)}, bf16[32,4096]{1,0:T(8,128)(2,1)S(1)}, u32[]{:S(2)}, u32[]{:S(2)}) collective-permute-start(bf16[32,4096]{1,0:T(8,128)(2,1)S(1)} %get-tuple-element.297), channel_id=1, source_target_pairs={{32,16},{80,96},{33,17},{81,97},{34,18},{82,98},{35,19},{83,99},{3... | collective-permute-start | bytes 786440 | tf_op jit(solution)/shard_map/ppermute | solution.py:171
  54.8 16.7 %all-to-all-start.1 = ((bf16[8,64,768]{2,1,0:T(8,128)(2,1)}), bf16[8,64,768]{2,1,0:T(8,128)(2,1)S(1)}, u32[]{:S(2)}, u32[]{:S(2)}) async-start(bf16[8,64,768]{2,1,0:T(8,128)(2,1)} %param.3), calls=%async_computation.1 | async-start | bytes 1572864 | tf_op jit(solution)/shard_map/cond/branch_1_fun/all_to_all | solution.py:183
  72.6 1.4 collective-permute-start.11
  73.3 1.5 collective-permute-start.10
  74.1 1.6 collective-permute-start.13
  74.9 2.2 %collective-permute-start.12 = (bf16[32,4096]{1,0:T(8,128)(2,1)S(1)}, bf16[32,4096]{1,0:T(8,128)(2,1)S(1)}, u32[]{:S(2)}, u32[]{:S(2)}) collective-permute-start(bf16[32,4096]{1,0:T(8,128)(2,1)S(1)} %get-tuple-element.325), channel_id=1, source_target_pairs={{0,16},{112,96},{1,17},{113,97},{2,18},{114,98},{3,19},{115,99},{4... | collective-permute-start | bytes 786440 | tf_op jit(solution)/shard_map/ppermute | solution.py:171
  75.8 9.7 %collective-permute-start.15 = (bf16[32,4096]{1,0:T(8,128)(2,1)S(1)}, bf16[32,4096]{1,0:T(8,128)(2,1)S(1)}, u32[]{:S(2)}, u32[]{:S(2)}) collective-permute-start(bf16[32,4096]{1,0:T(8,128)(2,1)S(1)} %get-tuple-element.354), channel_id=1, source_target_pairs={{16,32},{96,80},{17,33},{97,81},{18,34},{98,82},{19,35},{99,83},{2... | collective-permute-start | bytes 786440 | tf_op jit(solution)/shard_map/ppermute | solution.py:171
  77.2 11.2 %collective-permute-start.14 = (bf16[32,4096]{1,0:T(8,128)(2,1)S(1)}, bf16[32,4096]{1,0:T(8,128)(2,1)S(1)}, u32[]{:S(2)}, u32[]{:S(2)}) collective-permute-start(bf16[32,4096]{1,0:T(8,128)(2,1)S(1)} %get-tuple-element.334), channel_id=1, source_target_pairs={{16,32},{96,80},{17,33},{97,81},{18,34},{98,82},{19,35},{99,83},{2... | collective-permute-start | bytes 786440 | tf_op jit(solution)/shard_map/ppermute | solution.py:171
  87.0 9.6 %collective-permute-start.17 = (bf16[32,4096]{1,0:T(8,128)(2,1)S(1)}, bf16[32,4096]{1,0:T(8,128)(2,1)S(1)}, u32[]{:S(2)}, u32[]{:S(2)}) collective-permute-start(bf16[32,4096]{1,0:T(8,128)(2,1)S(1)} %get-tuple-element.368), channel_id=1, source_target_pairs={{32,48},{80,64},{33,49},{81,65},{34,50},{82,66},{35,51},{83,67},{3... | collective-permute-start | bytes 786440 | tf_op jit(solution)/shard_map/ppermute | solution.py:171
  89.8 8.4 %collective-permute-start.16 = (bf16[32,4096]{1,0:T(8,128)(2,1)S(1)}, bf16[32,4096]{1,0:T(8,128)(2,1)S(1)}, u32[]{:S(2)}, u32[]{:S(2)}) collective-permute-start(bf16[32,4096]{1,0:T(8,128)(2,1)S(1)} %get-tuple-element.358), channel_id=1, source_target_pairs={{32,48},{80,64},{33,49},{81,65},{34,50},{82,66},{35,51},{83,67},{3... | collective-permute-start | bytes 786440 | tf_op jit(solution)/shard_map/ppermute | solution.py:171
  96.7 9.8 %collective-permute-start.19 = (bf16[32,4096]{1,0:T(8,128)(2,1)S(1)}, bf16[32,4096]{1,0:T(8,128)(2,1)S(1)}, u32[]{:S(2)}, u32[]{:S(2)}) collective-permute-start(bf16[32,4096]{1,0:T(8,128)(2,1)S(1)} %get-tuple-element.373), channel_id=1, source_target_pairs={{48,32},{64,80},{49,33},{65,81},{50,34},{66,82},{51,35},{67,83},{5... | collective-permute-start | bytes 786440 | tf_op jit(solution)/shard_map/ppermute | solution.py:171
  98.3 11.0 %collective-permute-start.18 = (bf16[32,4096]{1,0:T(8,128)(2,1)S(1)}, bf16[32,4096]{1,0:T(8,128)(2,1)S(1)}, u32[]{:S(2)}, u32[]{:S(2)}) collective-permute-start(bf16[32,4096]{1,0:T(8,128)(2,1)S(1)} %get-tuple-element.372), channel_id=1, source_target_pairs={{48,32},{64,80},{49,33},{65,81},{50,34},{66,82},{51,35},{67,83},{5... | collective-permute-start | bytes 786440 | tf_op jit(solution)/shard_map/ppermute | solution.py:171
  108.0 6.1 %collective-permute-start.21 = (bf16[32,4096]{1,0:T(8,128)(2,1)S(1)}, bf16[32,4096]{1,0:T(8,128)(2,1)S(1)}, u32[]{:S(2)}, u32[]{:S(2)}) collective-permute-start(bf16[32,4096]{1,0:T(8,128)(2,1)S(1)} %get-tuple-element.388), channel_id=1, source_target_pairs={{32,16},{80,96},{33,17},{81,97},{34,18},{82,98},{35,19},{83,99},{3... | collective-permute-start | bytes 786440 | tf_op jit(solution)/shard_map/ppermute | solution.py:171
  110.8 6.1 %collective-permute-start.20 = (bf16[32,4096]{1,0:T(8,128)(2,1)S(1)}, bf16[32,4096]{1,0:T(8,128)(2,1)S(1)}, u32[]{:S(2)}, u32[]{:S(2)}) collective-permute-start(bf16[32,4096]{1,0:T(8,128)(2,1)S(1)} %get-tuple-element.378), channel_id=1, source_target_pairs={{32,16},{80,96},{33,17},{81,97},{34,18},{82,98},{35,19},{83,99},{3... | collective-permute-start | bytes 786440 | tf_op jit(solution)/shard_map/ppermute | solution.py:171
  114.2 40.8 %collective-permute-start.23 = (bf16[32,4096]{1,0:T(8,128)(2,1)S(1)}, bf16[32,4096]{1,0:T(8,128)(2,1)S(1)}, u32[]{:S(2)}, u32[]{:S(2)}) collective-permute-start(bf16[32,4096]{1,0:T(8,128)(2,1)S(1)} %get-tuple-element.410), channel_id=1, source_target_pairs={{16,0},{96,112},{17,1},{97,113},{18,2},{98,114},{19,3},{99,115},{2... | collective-permute-start | bytes 786440 | tf_op jit(solution)/shard_map/ppermute | solution.py:171
  117.0 38.0 %collective-permute-start.22 = (bf16[32,4096]{1,0:T(8,128)(2,1)S(1)}, bf16[32,4096]{1,0:T(8,128)(2,1)S(1)}, u32[]{:S(2)}, u32[]{:S(2)}) collective-permute-start(bf16[32,4096]{1,0:T(8,128)(2,1)S(1)} %get-tuple-element.392), channel_id=1, source_target_pairs={{16,0},{96,112},{17,1},{97,113},{18,2},{98,114},{19,3},{99,115},{2... | collective-permute-start | bytes 786440 | tf_op jit(solution)/shard_map/ppermute | solution.py:171
  117.7 37.1 %all-to-all-start.5 = ((bf16[8,192,768]{2,1,0:T(8,128)(2,1)}), bf16[8,192,768]{2,1,0:T(8,128)(2,1)}, u32[]{:S(2)}, u32[]{:S(2)}) async-start(bf16[8,192,768]{2,1,0:T(8,128)(2,1)} %param.9), calls=%async_computation.5 | async-start | bytes 4718592 | tf_op jit(solution)/shard_map/cond/branch_2_fun/all_to_all | solution.py:183
  155.0 1.4 copy-start.4
  155.0 1.6 copy-start.5
  159.6 2.3 %slice-start = ((f32[2,4096]{1,0:T(2,128)}), f32[1,4096]{1,0:T(1,128)S(1)}, s32[]{:S(2)}) async-start(f32[2,4096]{1,0:T(2,128)} %refs_2_.19), calls=%async_computation.7 | async-start | bytes 32768 | tf_op jit(solution)/shard_map/slice | solution.py:610
  159.6 2.0 %collective-permute-start.24 = (bf16[2,2,256,256]{3,2,1,0:T(8,128)(2,1)S(1)}, bf16[2,2,256,256]{3,2,1,0:T(8,128)(2,1)S(1)}, u32[]{:S(2)}, u32[]{:S(2)}) collective-permute-start(bf16[2,2,256,256]{3,2,1,0:T(8,128)(2,1)S(1)} %get-tuple-element.422), channel_id=1, source_target_pairs={{0,1},{1,0},{2,3},{3,2},{4,5},{5,4},{6,7},{7,6},{8,9},{9,8},{10,11... | collective-permute-start | bytes 1572872 | tf_op jit(solution)/shard_map/ppermute | solution.py:606
  161.8 10.8 %collective-permute-start.25 = (bf16[2,256,256]{2,1,0:T(8,128)(2,1)S(1)}, bf16[2,256,256]{2,1,0:T(8,128)(2,1)S(1)}, u32[]{:S(2)}, u32[]{:S(2)}) collective-permute-start(bf16[2,256,256]{2,1,0:T(8,128)(2,1)S(1)} %fusion.1), channel_id=1, source_target_pairs={{0,112},{16,96},{32,80},{48,64},{64,48},{80,32},{96,16},{112,0},{1... | collective-permute-start | bytes 786440 | tf_op jit(solution)/shard_map/ppermute | solution.py:608
  161.9 10.8 %slice-start.1 = ((bf16[2,4096,256]{2,1,0:T(8,128)(2,1)}), bf16[1,4096,256]{2,1,0:T(8,128)(2,1)S(1)}, s32[]{:S(2)}) async-start(bf16[2,4096,256]{2,1,0:T(8,128)(2,1)} %refs_0_.13), calls=%async_computation.8 | async-start | bytes 4194304 | tf_op jit(solution)/shard_map/slice | solution.py:611

commit v4 on v3

--- a/solution.py
+++ b/solution.py
@@ -15,7 +15,7 @@
 f32 = jnp.float32
 VMEM = pl.BlockSpec(memory_space=pltpu.VMEM)
 HBM = pl.BlockSpec(memory_space=pltpu.HBM)
-LOADS = 4
+LOADS = 8
 MIB = 2**20
 
 
@@ -524,28 +524,37 @@
     far_2 = (*far_2, *saved_rows("saved_far_2", lambda fold: fold >= 2, 1))
     box_late_two = backward_stage(8, {1: 0}, box_late_two, [None, far_2])
     kept, raw_in, raw_out = lax.optimization_barrier((kept, raw_in, raw_out))
-    (far_1,) = fresh_weights("turn_far_1", lambda fold: fold >= 2, (0,), 0, 1)
-    far_1 = (*far_1, *saved_rows("saved_far_1", lambda fold: fold >= 2, 0))
+    (far_1,) = fresh_weights("turn_9", lambda fold: fold == 3, (0,), 0, 1)
+    far_1 = (*far_1, *saved_rows("saved_9", lambda fold: fold == 3, 0))
     box_late_two = backward_stage(9, {1: 0, 0: 1}, box_late_two, [far_1, far_2])
+    kept, raw_in, raw_out = lax.optimization_barrier((kept, raw_in, raw_out))
+    (far_1,) = fresh_weights("turn_10", lambda fold: fold == 2, (0,), 0, 1)
+    far_1 = (*far_1, *saved_rows("saved_10", lambda fold: fold == 2, 0))
     box_late_two = backward_stage(10, {0: 1}, box_late_two, [far_1])
-    kept, raw_in, raw_out = lax.optimization_barrier((kept, raw_in, raw_out))
+
+    box_late_two, kept = lax.optimization_barrier((box_late_two, kept))
+    got_late_two = lax.cond(
+        fold_here >= 2,
+        functools.partial(exchange, raw=True),
+        functools.partial(none, "none_late_two"),
+        box_late_two,
+    )
+    got_late_two, box_late, kept, hats, raw_in, raw_out = lax.optimization_barrier(
+        (got_late_two, box_late, kept, hats, raw_in, raw_out)
+    )
     (near_1,) = fresh_weights("turn_11", lambda fold: fold == 1, (0,), 0, 1)
     near_1 = (*near_1, *saved_rows("saved_11", lambda fold: fold == 1, 0))
     box_late = backward_stage(11, {0: 1}, box_late, [near_1])
 
-    box_late, box_late_two, kept = lax.optimization_barrier((box_late, box_late_two, kept))
-    got_late, got_late_two = lax.switch(
-        jnp.minimum(fold_here, 2),
-        (
-            lambda late, late_two: (none("none_late", late), none("none_late_two", late_two)),
-            lambda late, late_two: (exchange(late, raw=True), none("none_late_two", late_two)),
-            lambda late, late_two: (none("none_late", late), exchange(late_two, raw=True)),
-        ),
+    box_late, kept = lax.optimization_barrier((box_late, kept))
+    got_late = lax.cond(
+        fold_here == 1,
+        functools.partial(exchange, raw=True),
+        functools.partial(none, "none_late"),
         box_late,
-        box_late_two,
-    )
-    got_late, got_late_two, box_end, kept, raw_in, raw_out = lax.optimization_barrier(
-        (got_late, got_late_two, box_end, kept, raw_in, raw_out)
+    )
+    got_late, box_end, kept, raw_in, raw_out = lax.optimization_barrier(
+        (got_late, box_end, kept, raw_in, raw_out)
     )
     (near_1,) = fresh_weights("turn_12", lambda fold: fold == 0, (0,), 0, 1)
     near_1 = (*near_1, *saved_rows("saved_12", lambda fold: fold == 0, 0))

time: 175 us -> 169 us (0.966)
  blocking collectives: 0 us -> 36.6 us
  waiting for transfers between devices: 91.5 us -> 56 us
  starting transfers between devices: 40.5 us -> 32.4 us
    all_to_all x0 -> x1, blocking collectives: none -> 36.6 us  [exchange(): lax.all_to_all(array, 'dp', 0, 0, axis_index_groups=same_core, tiled=False)]
    all_to_all x2 -> x1, waiting for transfers between devices: 39.8 us -> 10.7 us  [exchange(): lax.all_to_all(array, 'dp', 0, 0, axis_index_groups=same_core, tiled=False)]
    all_to_all x2 -> x1, starting transfers between devices: 13.9 us -> 6.04 us  [exchange(): lax.all_to_all(array, 'dp', 0, 0, axis_index_groups=same_core, tiled=False)]
    ppermute x24, waiting for transfers between devices: 39.1 us -> 32.8 us  [send_on(): return lax.ppermute(sent, 'section', pairs)]
    pallas_call x42 -> x44, Pallas kernels: 33.7 us -> 34.8 us  [call(): pl.pallas_call(kernel, out_shape=tuple(shapes), in_specs=[spec for _, spe...]
  transfers between devices with their start and end apart: 28 -> 27, of which waited for: 14 -> 14; matrix products, arithmetic and copies ran while one was open for 0% -> 0% of each run, Pallas kernels for 18% -> 19%
where the time goes in v4:
time: 169 us; the launch traced here: 168 us
  waiting for transfers between devices  56 us (33%)
  blocking collectives  36.6 us (22%)
  Pallas kernels  34.9 us (21%)
  starting transfers between devices  32.4 us (19%)
  local copies, waits for them, and re-layouts  5.23 us (3%)
    all_to_all x1, blocking collectives, exchange(): lax.all_to_all(array, 'dp', 0, 0, axis_index_groups=same_core, tiled=False)  36.6 us
    pallas_call x44, Pallas kernels, call(): pl.pallas_call(kernel, out_shape=tuple(shapes), in_specs=[spec for _, spe...  34.8 us
    ppermute x24, waiting for transfers between devices, send_on(): return lax.ppermute(sent, 'section', pairs)  32.8 us
    ppermute x24, starting transfers between devices, send_on(): return lax.ppermute(sent, 'section', pairs)  26.2 us
    ppermute x1, waiting for transfers between devices, on_device(): lax.ppermute(total[1].astype(bf16), 'section', mirror).astype(f32)  10.7 us
    all_to_all x1, waiting for transfers between devices, exchange(): lax.all_to_all(array, 'dp', 0, 0, axis_index_groups=same_core, tiled=False)  10.7 us
    all_to_all x1, starting transfers between devices, exchange(): lax.all_to_all(array, 'dp', 0, 0, axis_index_groups=same_core, tiled=False)  6.04 us
    unnamed x12, local copies, waits for them, and re-layouts  5.18 us
  transfers between devices with their start and end apart: 27, of which 14 were waited for; matrix products, arithmetic and copies ran while one was open for 0% of the time, Pallas kernels for 19%

profile of v4, /device:TPU:18, one launch (start us, length us, event | category | flops | bytes accessed | tf_op | source)
XLA Modules:
  0.0 168.3 jit_solution(17854207324940527751)
XLA Ops:
  0.7 0.7 copy-done.2
  1.6 0.7 collective-permute-start.1
  2.4 0.7 collective-permute-start
  3.2 1.3 copy-done
  4.5 1.6 copy-done.1
  6.2 1.3 collective-permute-start.3
  7.5 1.3 collective-permute-start.2
  8.9 2.3 %load_2.1 = (f32[1,4096]{1,0:T(1,128)S(1)}, bf16[4096,256]{1,0:T(8,128)(2,1)S(1)}, bf16[256,4096]{1,0:T(8,128)(2,1)S(1)}) custom-call(bf16[2,4096,256]{2,1,0:T(8,128)(2,1)} %refs_0_.14, bf16[2,256,4096]{2,1,0:T(8,128)(2,1)} %refs_1_.16, f32[2,4096]{1,0:T(2,128)S(1)} %copy-done.3), custom_call_target="tpu_custom_call" | custom-call | flops 1 | bytes 1 | tf_op jit(solution)/shard_map/load_2/pallas_call | solution.py:51
  11.2 16.4 %collective-permute-done.3.refs_0_ = bf16[32,4096]{1,0:T(8,128)(2,1)S(1)} collective-permute-done((bf16[32,4096]{1,0:T(8,128)(2,1)S(1)}, bf16[32,4096]{1,0:T(8,128)(2,1)S(1)}, u32[]{:S(2)}, u32[]{:S(2)}) %collective-permute-start.3) | collective-permute-done | bytes 262176 | tf_op jit(solution)/shard_map/ppermute | solution.py:171
  27.6 1.6 forward_2_0.1
  29.2 1.3 collective-permute-start.5
  30.6 1.1 collective-permute-done.2.refs_0_
  31.6 1.7 forward_2_1.1
  33.3 1.3 collective-permute-start.4
  34.9 0.3 collective-permute-done.5.refs_0_
  35.3 1.3 collective-permute-start.7
  36.6 3.4 %collective-permute-done.4.refs_0_ = bf16[32,4096]{1,0:T(8,128)(2,1)S(1)} collective-permute-done((bf16[32,4096]{1,0:T(8,128)(2,1)S(1)}, bf16[32,4096]{1,0:T(8,128)(2,1)S(1)}, u32[]{:S(2)}, u32[]{:S(2)}) %collective-permute-start.4) | collective-permute-done | bytes 262176 | tf_op jit(solution)/shard_map/ppermute | solution.py:171
  40.1 1.3 collective-permute-start.6
  41.4 2.3 %load_4.1 = (f32[1,4096]{1,0:T(1,128)S(1)}, bf16[4096,256]{1,0:T(8,128)(2,1)S(1)}, bf16[256,4096]{1,0:T(8,128)(2,1)S(1)}) custom-call(bf16[2,4096,256]{2,1,0:T(8,128)(2,1)} %refs_0_.14, bf16[2,256,4096]{2,1,0:T(8,128)(2,1)} %refs_1_.16, f32[2,4096]{1,0:T(2,128)S(1)} %copy-done.3), custom_call_target="tpu_custom_call" | custom-call | flops 1 | bytes 1 | tf_op jit(solution)/shard_map/load_4/pallas_call | solution.py:51
  43.7 2.8 %collective-permute-done.7.refs_0_ = bf16[32,4096]{1,0:T(8,128)(2,1)S(1)} collective-permute-done((bf16[32,4096]{1,0:T(8,128)(2,1)S(1)}, bf16[32,4096]{1,0:T(8,128)(2,1)S(1)}, u32[]{:S(2)}, u32[]{:S(2)}) %collective-permute-start.7) | collective-permute-done | bytes 262176 | tf_op jit(solution)/shard_map/ppermute | solution.py:171
  46.5 1.7 %forward_4_0.1 = (bf16[8,192,768]{2,1,0:T(8,128)(2,1)}, bf16[8,128,512]{2,1,0:T(8,128)(2,1)}, f32[128,384]{1,0:T(8,128)}, bf16[32,4096]{1,0:T(8,128)(2,1)S(1)}) custom-call(bf16[32,4096]{1,0:T(8,128)(2,1)S(1)} %collective-permute-done.7.refs_0_, ...), custom_call_target="tpu_custom_call", output_to_operand_aliasing={{0}: (4, {}), {1}: (5, {}), {2}: (6, {})} | custom-call | flops 1 | bytes 1 | tf_op jit(solution)/shard_map/forward_4_0/pallas_call | solution.py:51
  48.2 1.3 collective-permute-start.9
  49.5 2.6 %collective-permute-done.6.refs_0_ = bf16[32,4096]{1,0:T(8,128)(2,1)S(1)} collective-permute-done((bf16[32,4096]{1,0:T(8,128)(2,1)S(1)}, bf16[32,4096]{1,0:T(8,128)(2,1)S(1)}, u32[]{:S(2)}, u32[]{:S(2)}) %collective-permute-start.6) | collective-permute-done | bytes 262176 | tf_op jit(solution)/shard_map/ppermute | solution.py:171
  52.1 1.7 forward_4_1.1
  53.8 1.3 collective-permute-start.8
  55.1 17.7 %conditional.7 = (bf16[8,64,768]{2,1,0:T(8,128)(2,1)}) conditional(s32[]{:T(128)} %convert_element_type.29, () %tuple.72, bf16[8,64,768]{2,1,0:T(8,128)(2,1)} %get-tuple-element.315), branch_computations={%region_2.3_spmd, %region_3.4_spmd} | conditional | flops 1 | bytes 2359337 | solution.py:398
  55.2 6.0 %all-to-all-start.1 = ((bf16[8,64,768]{2,1,0:T(8,128)(2,1)}), bf16[8,64,768]{2,1,0:T(8,128)(2,1)S(1)}, u32[]{:S(2)}, u32[]{:S(2)}) async-start(bf16[8,64,768]{2,1,0:T(8,128)(2,1)} %param.3), calls=%async_computation.1 | async-start | bytes 1572864 | tf_op jit(solution)/shard_map/cond/branch_1_fun/all_to_all | solution.py:183
  61.2 10.7 %all-to-all-done.1.refs_0_ = bf16[8,64,768]{2,1,0:T(8,128)(2,1)S(1)} async-done(((bf16[8,64,768]{2,1,0:T(8,128)(2,1)}), bf16[8,64,768]{2,1,0:T(8,128)(2,1)S(1)}, u32[]{:S(2)}, u32[]{:S(2)}) %all-to-all-start.1) | async-done | bytes 786464 | tf_op jit(solution)/shard_map/cond/branch_1_fun/all_to_all | solution.py:183
  71.8 1.0 unstage.5
  73.1 0.7 collective-permute-start.11
  73.9 0.7 collective-permute-start.10
  74.7 0.7 collective-permute-start.13
  75.4 0.7 collective-permute-start.12
  76.3 1.3 collective-permute-start.15
  77.7 1.3 collective-permute-start.14
  79.0 1.3 saved_far_2.1
  80.3 4.3 %turn_far_2.1 = (f32[1,4096]{1,0:T(1,128)S(1)}, bf16[256,4096]{1,0:T(8,128)(2,1)S(1)}, bf16[4096,256]{1,0:T(8,128)(2,1)S(1)}) custom-call(bf16[2,4096,256]{2,1,0:T(8,128)(2,1)} %refs_0_.14, bf16[2,256,4096]{2,1,0:T(8,128)(2,1)} %refs_1_.16, f32[2,4096]{1,0:T(2,128)S(1)} %copy-done.3), custom_call_target="tpu_custom_call" | custom-call | flops 1 | bytes 1 | tf_op jit(solution)/shard_map/turn_far_2/pallas_call | solution.py:51
  84.6 1.5 collective-permute-done.15.refs_0_
  86.1 1.5 backward_8_0.1
  87.6 1.3 collective-permute-start.17
  89.0 1.5 backward_8_1.1
  90.4 1.3 collective-permute-start.16
  92.0 1.7 collective-permute-done.17.refs_0_
  93.8 1.3 collective-permute-start.19
  95.1 1.4 collective-permute-done.16.refs_0_
  96.6 1.3 collective-permute-start.18
  97.9 1.3 saved_10.1
  99.1 4.3 %turn_10.1 = (f32[1,4096]{1,0:T(1,128)S(1)}, bf16[256,4096]{1,0:T(8,128)(2,1)S(1)}, bf16[4096,256]{1,0:T(8,128)(2,1)S(1)}) custom-call(bf16[2,4096,256]{2,1,0:T(8,128)(2,1)} %refs_0_.14, bf16[2,256,4096]{2,1,0:T(8,128)(2,1)} %refs_1_.16, f32[2,4096]{1,0:T(2,128)S(1)} %copy-done.3), custom_call_target="tpu_custom_call" | custom-call | flops 1 | bytes 1 | tf_op jit(solution)/shard_map/turn_10/pallas_call | solution.py:51
  103.4 0.9 collective-permute-done.19.refs_0_
  104.3 1.5 backward_10_0.1
  105.8 1.3 collective-permute-start.21
  107.1 0.6 collective-permute-done.18.refs_0_
  107.7 1.5 backward_10_1.1
  109.1 1.3 collective-permute-start.20
  110.4 36.6 %conditional.9 = (bf16[8,192,768]{2,1,0:T(8,128)(2,1)}) conditional(s32[]{:T(128)} %convert_element_type.29, () %tuple.80, bf16[8,192,768]{2,1,0:T(8,128)(2,1)} %get-tuple-element.404), branch_computations={%region_7.8_spmd, %region_8.9_spmd} | conditional | bytes 4718600 | solution.py:536
  110.5 36.6 %all_to_all.28 = bf16[8,192,768]{2,1,0:T(8,128)(2,1)} all-to-all(bf16[8,192,768]{2,1,0:T(8,128)(2,1)} %param.8), channel_id=1, replica_groups={{0,2,4,6,8,10,12,14},{1,3,5,7,9,11,13,15},{16,18,20,22,24,26,28,30},{17..., dimensions={0} | all-to-all | bytes 4718592 | tf_op jit(solution)/shard_map/cond/branch_1_fun/all_to_all | solution.py:183
  147.3 0.7 collective-permute-start.23
  148.1 0.7 collective-permute-start.22
  149.3 1.3 copy-done.4
  150.8 3.0 %conditional.11 = ((f32[2,2,256,256]{3,2,1,0:T(8,128)S(1)}, bf16[2,2,256,256]{3,2,1,0:T(8,128)(2,1)S(1)})) conditional(s32[]{:T(128)} %clamp.4, (bf16[8,64,768]{2,1,0:T(8,128)(2,1)}, bf16[8,64,768]{2,1,0:T(8,128)(2,1)S(1)}, bf16[8,128,768]{2,1,0:T(8,128)(2,1)S(1)}) %tuple.110, (bf16[8,64,768]{2,1,0:T(8,128)(2,1)S(1)}, ...), branch_computations={%region_11.12_spmd, %region_12.13_spmd, %region_13.14_spmd} | conditional | flops 1 | bytes 1572873 | solution.py:594
  150.8 3.0 %products_2.1 = (f32[2,2,256,256]{3,2,1,0:T(8,128)S(1)}, bf16[2,2,256,256]{3,2,1,0:T(8,128)(2,1)S(1)}) custom-call(bf16[8,64,768]{2,1,0:T(8,128)(2,1)} %get-tuple-element.40.refs_0_, bf16[8,192,768]{2,1,0:T(8,128)(2,1)} %get-tuple-element.41.refs_1_), custom_call_target="tpu_custom_call" | custom-call | flops 1 | bytes 1 | tf_op jit(solution)/shard_map/cond/branch_2_fun/products_2/pallas_call | solution.py:51
  153.9 1.9 %collective-permute-done.24 = bf16[2,2,256,256]{3,2,1,0:T(8,128)(2,1)S(1)} collective-permute-done((bf16[2,2,256,256]{3,2,1,0:T(8,128)(2,1)S(1)}, bf16[2,2,256,256]{3,2,1,0:T(8,128)(2,1)S(1)}, u32[]{:S(2)}, u32[]{:S(2)}) %collective-permute-start.24) | collective-permute-done | bytes 524320 | tf_op jit(solution)/shard_map/ppermute | solution.py:615
  156.1 10.7 %collective-permute-done.25 = bf16[2,256,256]{2,1,0:T(8,128)(2,1)S(1)} collective-permute-done((bf16[2,256,256]{2,1,0:T(8,128)(2,1)S(1)}, bf16[2,256,256]{2,1,0:T(8,128)(2,1)S(1)}, u32[]{:S(2)}, u32[]{:S(2)}) %collective-permute-start.25) | collective-permute-done | bytes 262176 | tf_op jit(solution)/shard_map/ppermute | solution.py:617
  166.8 1.5 multiply_reduce_fusion
  (73 shorter events, 3.4 us)
Async XLA Ops:
  0.6 0.8 copy-start.2
  1.6 2.9 %collective-permute-start.1 = (bf16[32,4096]{1,0:T(8,128)(2,1)S(1)}, bf16[32,4096]{1,0:T(8,128)(2,1)S(1)}, u32[]{:S(2)}, u32[]{:S(2)}) collective-permute-start(bf16[32,4096]{1,0:T(8,128)(2,1)S(1)} %get-tuple-element.255), channel_id=1, source_target_pairs={{0,16},{112,96},{1,17},{113,97},{2,18},{114,98},{3,19},{115,99},{4... | collective-permute-start | bytes 786440 | tf_op jit(solution)/shard_map/ppermute | solution.py:171
  2.3 0.8 copy-start.3
  2.4 5.1 %collective-permute-start = (bf16[32,4096]{1,0:T(8,128)(2,1)S(1)}, bf16[32,4096]{1,0:T(8,128)(2,1)S(1)}, u32[]{:S(2)}, u32[]{:S(2)}) collective-permute-start(bf16[32,4096]{1,0:T(8,128)(2,1)S(1)} %get-tuple-element.251), channel_id=1, source_target_pairs={{0,16},{112,96},{1,17},{113,97},{2,18},{114,98},{3,19},{115,99},{4... | collective-permute-start | bytes 786440 | tf_op jit(solution)/shard_map/ppermute | solution.py:171
  3.2 1.3 copy-start
  4.5 1.6 copy-start.1
  6.2 21.4 %collective-permute-start.3 = (bf16[32,4096]{1,0:T(8,128)(2,1)S(1)}, bf16[32,4096]{1,0:T(8,128)(2,1)S(1)}, u32[]{:S(2)}, u32[]{:S(2)}) collective-permute-start(bf16[32,4096]{1,0:T(8,128)(2,1)S(1)} %get-tuple-element.272), channel_id=1, source_target_pairs={{16,32},{96,80},{17,33},{97,81},{18,34},{98,82},{19,35},{99,83},{2... | collective-permute-start | bytes 786440 | tf_op jit(solution)/shard_map/ppermute | solution.py:171
  7.5 24.1 %collective-permute-start.2 = (bf16[32,4096]{1,0:T(8,128)(2,1)S(1)}, bf16[32,4096]{1,0:T(8,128)(2,1)S(1)}, u32[]{:S(2)}, u32[]{:S(2)}) collective-permute-start(bf16[32,4096]{1,0:T(8,128)(2,1)S(1)} %get-tuple-element.261), channel_id=1, source_target_pairs={{16,32},{96,80},{17,33},{97,81},{18,34},{98,82},{19,35},{99,83},{2... | collective-permute-start | bytes 786440 | tf_op jit(solution)/shard_map/ppermute | solution.py:171
  29.2 6.0 %collective-permute-start.5 = (bf16[32,4096]{1,0:T(8,128)(2,1)S(1)}, bf16[32,4096]{1,0:T(8,128)(2,1)S(1)}, u32[]{:S(2)}, u32[]{:S(2)}) collective-permute-start(bf16[32,4096]{1,0:T(8,128)(2,1)S(1)} %get-tuple-element.289), channel_id=1, source_target_pairs={{32,48},{80,64},{33,49},{81,65},{34,50},{82,66},{35,51},{83,67},{3... | collective-permute-start | bytes 786440 | tf_op jit(solution)/shard_map/ppermute | solution.py:171
  33.3 6.7 %collective-permute-start.4 = (bf16[32,4096]{1,0:T(8,128)(2,1)S(1)}, bf16[32,4096]{1,0:T(8,128)(2,1)S(1)}, u32[]{:S(2)}, u32[]{:S(2)}) collective-permute-start(bf16[32,4096]{1,0:T(8,128)(2,1)S(1)} %get-tuple-element.279), channel_id=1, source_target_pairs={{32,48},{80,64},{33,49},{81,65},{34,50},{82,66},{35,51},{83,67},{3... | collective-permute-start | bytes 786440 | tf_op jit(solution)/shard_map/ppermute | solution.py:171
  35.3 11.2 %collective-permute-start.7 = (bf16[32,4096]{1,0:T(8,128)(2,1)S(1)}, bf16[32,4096]{1,0:T(8,128)(2,1)S(1)}, u32[]{:S(2)}, u32[]{:S(2)}) collective-permute-start(bf16[32,4096]{1,0:T(8,128)(2,1)S(1)} %get-tuple-element.305), channel_id=1, source_target_pairs={{48,32},{64,80},{49,33},{65,81},{50,34},{66,82},{51,35},{67,83},{5... | collective-permute-start | bytes 786440 | tf_op jit(solution)/shard_map/ppermute | solution.py:171
  40.1 12.0 %collective-permute-start.6 = (bf16[32,4096]{1,0:T(8,128)(2,1)S(1)}, bf16[32,4096]{1,0:T(8,128)(2,1)S(1)}, u32[]{:S(2)}, u32[]{:S(2)}) collective-permute-start(bf16[32,4096]{1,0:T(8,128)(2,1)S(1)} %get-tuple-element.298), channel_id=1, source_target_pairs={{48,32},{64,80},{49,33},{65,81},{50,34},{66,82},{51,35},{67,83},{5... | collective-permute-start | bytes 786440 | tf_op jit(solution)/shard_map/ppermute | solution.py:171
  48.2 24.8 %collective-permute-start.9 = (bf16[32,4096]{1,0:T(8,128)(2,1)S(1)}, bf16[32,4096]{1,0:T(8,128)(2,1)S(1)}, u32[]{:S(2)}, u32[]{:S(2)}) collective-permute-start(bf16[32,4096]{1,0:T(8,128)(2,1)S(1)} %get-tuple-element.325), channel_id=1, source_target_pairs={{32,16},{80,96},{33,17},{81,97},{34,18},{82,98},{35,19},{83,99},{3... | collective-permute-start | bytes 786440 | tf_op jit(solution)/shard_map/ppermute | solution.py:171
  53.8 20.0 %collective-permute-start.8 = (bf16[32,4096]{1,0:T(8,128)(2,1)S(1)}, bf16[32,4096]{1,0:T(8,128)(2,1)S(1)}, u32[]{:S(2)}, u32[]{:S(2)}) collective-permute-start(bf16[32,4096]{1,0:T(8,128)(2,1)S(1)} %get-tuple-element.312), channel_id=1, source_target_pairs={{32,16},{80,96},{33,17},{81,97},{34,18},{82,98},{35,19},{83,99},{3... | collective-permute-start | bytes 786440 | tf_op jit(solution)/shard_map/ppermute | solution.py:171
  55.2 16.7 %all-to-all-start.1 = ((bf16[8,64,768]{2,1,0:T(8,128)(2,1)}), bf16[8,64,768]{2,1,0:T(8,128)(2,1)S(1)}, u32[]{:S(2)}, u32[]{:S(2)}) async-start(bf16[8,64,768]{2,1,0:T(8,128)(2,1)} %param.3), calls=%async_computation.1 | async-start | bytes 1572864 | tf_op jit(solution)/shard_map/cond/branch_1_fun/all_to_all | solution.py:183
  73.1 1.4 collective-permute-start.11
  73.9 1.5 collective-permute-start.10
  74.7 1.6 collective-permute-start.13
  75.4 2.2 %collective-permute-start.12 = (bf16[32,4096]{1,0:T(8,128)(2,1)S(1)}, bf16[32,4096]{1,0:T(8,128)(2,1)S(1)}, u32[]{:S(2)}, u32[]{:S(2)}) collective-permute-start(bf16[32,4096]{1,0:T(8,128)(2,1)S(1)} %get-tuple-element.340), channel_id=1, source_target_pairs={{0,16},{112,96},{1,17},{113,97},{2,18},{114,98},{3,19},{115,99},{4... | collective-permute-start | bytes 786440 | tf_op jit(solution)/shard_map/ppermute | solution.py:171
  76.3 9.8 %collective-permute-start.15 = (bf16[32,4096]{1,0:T(8,128)(2,1)S(1)}, bf16[32,4096]{1,0:T(8,128)(2,1)S(1)}, u32[]{:S(2)}, u32[]{:S(2)}) collective-permute-start(bf16[32,4096]{1,0:T(8,128)(2,1)S(1)} %get-tuple-element.369), channel_id=1, source_target_pairs={{16,32},{96,80},{17,33},{97,81},{18,34},{98,82},{19,35},{99,83},{2... | collective-permute-start | bytes 786440 | tf_op jit(solution)/shard_map/ppermute | solution.py:171
  77.7 11.3 %collective-permute-start.14 = (bf16[32,4096]{1,0:T(8,128)(2,1)S(1)}, bf16[32,4096]{1,0:T(8,128)(2,1)S(1)}, u32[]{:S(2)}, u32[]{:S(2)}) collective-permute-start(bf16[32,4096]{1,0:T(8,128)(2,1)S(1)} %get-tuple-element.349), channel_id=1, source_target_pairs={{16,32},{96,80},{17,33},{97,81},{18,34},{98,82},{19,35},{99,83},{2... | collective-permute-start | bytes 786440 | tf_op jit(solution)/shard_map/ppermute | solution.py:171
  87.6 6.1 %collective-permute-start.17 = (bf16[32,4096]{1,0:T(8,128)(2,1)S(1)}, bf16[32,4096]{1,0:T(8,128)(2,1)S(1)}, u32[]{:S(2)}, u32[]{:S(2)}) collective-permute-start(bf16[32,4096]{1,0:T(8,128)(2,1)S(1)} %get-tuple-element.383), channel_id=1, source_target_pairs={{32,48},{80,64},{33,49},{81,65},{34,50},{82,66},{35,51},{83,67},{3... | collective-permute-start | bytes 786440 | tf_op jit(solution)/shard_map/ppermute | solution.py:171
  90.4 6.1 %collective-permute-start.16 = (bf16[32,4096]{1,0:T(8,128)(2,1)S(1)}, bf16[32,4096]{1,0:T(8,128)(2,1)S(1)}, u32[]{:S(2)}, u32[]{:S(2)}) collective-permute-start(bf16[32,4096]{1,0:T(8,128)(2,1)S(1)} %get-tuple-element.373), channel_id=1, source_target_pairs={{32,48},{80,64},{33,49},{81,65},{34,50},{82,66},{35,51},{83,67},{3... | collective-permute-start | bytes 786440 | tf_op jit(solution)/shard_map/ppermute | solution.py:171
  93.8 10.5 %collective-permute-start.19 = (bf16[32,4096]{1,0:T(8,128)(2,1)S(1)}, bf16[32,4096]{1,0:T(8,128)(2,1)S(1)}, u32[]{:S(2)}, u32[]{:S(2)}) collective-permute-start(bf16[32,4096]{1,0:T(8,128)(2,1)S(1)} %get-tuple-element.397), channel_id=1, source_target_pairs={{48,32},{64,80},{49,33},{65,81},{50,34},{66,82},{51,35},{67,83},{5... | collective-permute-start | bytes 786440 | tf_op jit(solution)/shard_map/ppermute | solution.py:171
  96.6 11.1 %collective-permute-start.18 = (bf16[32,4096]{1,0:T(8,128)(2,1)S(1)}, bf16[32,4096]{1,0:T(8,128)(2,1)S(1)}, u32[]{:S(2)}, u32[]{:S(2)}) collective-permute-start(bf16[32,4096]{1,0:T(8,128)(2,1)S(1)} %get-tuple-element.387), channel_id=1, source_target_pairs={{48,32},{64,80},{49,33},{65,81},{50,34},{66,82},{51,35},{67,83},{5... | collective-permute-start | bytes 786440 | tf_op jit(solution)/shard_map/ppermute | solution.py:171
  105.8 41.5 %collective-permute-start.21 = (bf16[32,4096]{1,0:T(8,128)(2,1)S(1)}, bf16[32,4096]{1,0:T(8,128)(2,1)S(1)}, u32[]{:S(2)}, u32[]{:S(2)}) collective-permute-start(bf16[32,4096]{1,0:T(8,128)(2,1)S(1)} %get-tuple-element.416), channel_id=1, source_target_pairs={{32,16},{80,96},{33,17},{81,97},{34,18},{82,98},{35,19},{83,99},{3... | collective-permute-start | bytes 786440 | tf_op jit(solution)/shard_map/ppermute | solution.py:171
  109.1 38.9 %collective-permute-start.20 = (bf16[32,4096]{1,0:T(8,128)(2,1)S(1)}, bf16[32,4096]{1,0:T(8,128)(2,1)S(1)}, u32[]{:S(2)}, u32[]{:S(2)}) collective-permute-start(bf16[32,4096]{1,0:T(8,128)(2,1)S(1)} %get-tuple-element.401), channel_id=1, source_target_pairs={{32,16},{80,96},{33,17},{81,97},{34,18},{82,98},{35,19},{83,99},{3... | collective-permute-start | bytes 786440 | tf_op jit(solution)/shard_map/ppermute | solution.py:171
  147.3 1.8 %collective-permute-start.23 = (bf16[32,4096]{1,0:T(8,128)(2,1)S(1)}, bf16[32,4096]{1,0:T(8,128)(2,1)S(1)}, u32[]{:S(2)}, u32[]{:S(2)}) collective-permute-start(bf16[32,4096]{1,0:T(8,128)(2,1)S(1)} %get-tuple-element.434), channel_id=1, source_target_pairs={{16,0},{96,112},{17,1},{97,113},{18,2},{98,114},{19,3},{99,115},{2... | collective-permute-start | bytes 786440 | tf_op jit(solution)/shard_map/ppermute | solution.py:171
  148.1 1.1 collective-permute-start.22
  149.2 1.4 copy-start.4
  149.2 1.6 copy-start.5
  153.8 2.3 %slice-start = ((f32[2,4096]{1,0:T(2,128)}), f32[1,4096]{1,0:T(1,128)S(1)}, s32[]{:S(2)}) async-start(f32[2,4096]{1,0:T(2,128)} %refs_2_.21), calls=%async_computation.7 | async-start | bytes 32768 | tf_op jit(solution)/shard_map/slice | solution.py:619
  153.8 2.0 %collective-permute-start.24 = (bf16[2,2,256,256]{3,2,1,0:T(8,128)(2,1)S(1)}, bf16[2,2,256,256]{3,2,1,0:T(8,128)(2,1)S(1)}, u32[]{:S(2)}, u32[]{:S(2)}) collective-permute-start(bf16[2,2,256,256]{3,2,1,0:T(8,128)(2,1)S(1)} %get-tuple-element.446), channel_id=1, source_target_pairs={{0,1},{1,0},{2,3},{3,2},{4,5},{5,4},{6,7},{7,6},{8,9},{9,8},{10,11... | collective-permute-start | bytes 1572872 | tf_op jit(solution)/shard_map/ppermute | solution.py:615
  155.9 10.8 %collective-permute-start.25 = (bf16[2,256,256]{2,1,0:T(8,128)(2,1)S(1)}, bf16[2,256,256]{2,1,0:T(8,128)(2,1)S(1)}, u32[]{:S(2)}, u32[]{:S(2)}) collective-permute-start(bf16[2,256,256]{2,1,0:T(8,128)(2,1)S(1)} %fusion.1), channel_id=1, source_target_pairs={{0,112},{16,96},{32,80},{48,64},{64,48},{80,32},{96,16},{112,0},{1... | collective-permute-start | bytes 786440 | tf_op jit(solution)/shard_map/ppermute | solution.py:617
  156.1 10.8 %slice-start.1 = ((bf16[2,4096,256]{2,1,0:T(8,128)(2,1)}), bf16[1,4096,256]{2,1,0:T(8,128)(2,1)S(1)}, s32[]{:S(2)}) async-start(bf16[2,4096,256]{2,1,0:T(8,128)(2,1)} %refs_0_.14), calls=%async_computation.8 | async-start | bytes 4194304 | tf_op jit(solution)/shard_map/slice | solution.py:620

commit v5 on v4

--- a/solution.py
+++ b/solution.py
@@ -213,6 +213,12 @@
         def _():
             copy = pltpu.make_async_copy(inputs.at[half, of_micro(0)], staged, sem)
             copy.start()
+
+            @pl.when(lax.rem(lax.axis_index("dp"), 2) == 1)
+            def _():
+                first = load(half, (source_in, source_out), (weight_in, weight_out), load_sems)
+                wait_all(first[0] + first[1])
+
             ready = load(half, (source_in, source_out), (weight_in, weight_out), load_sems)
             gain[...] = source_gain[pl.ds(half, 1), :]
             copy.wait()

time: 169 us -> 170 us (level)
  starting transfers between devices: 32.4 us -> 36.6 us
  blocking collectives: 36.6 us -> 33.3 us
    ppermute x24, starting transfers between devices: 26.2 us -> 30.3 us  [send_on(): return lax.ppermute(sent, 'section', pairs)]
    all_to_all x1, blocking collectives: 36.6 us -> 33.3 us  [exchange(): lax.all_to_all(array, 'dp', 0, 0, axis_index_groups=same_core, tiled=False)]
    ppermute x24, waiting for transfers between devices: 32.8 us -> 31 us  [send_on(): return lax.ppermute(sent, 'section', pairs)]
  transfers between devices with their start and end apart: 27 -> 27, of which waited for: 14 -> 10; matrix products, arithmetic and copies ran while one was open for 0% -> 0% of each run, Pallas kernels for 19% -> 19%
where the time goes in v5:
time: 170 us; the launch traced here: 169 us
  waiting for transfers between devices  55.7 us (33%)
  starting transfers between devices  36.6 us (22%)
  Pallas kernels  35.2 us (21%)
  blocking collectives  33.3 us (20%)
  local copies, waits for them, and re-layouts  5.23 us (3%)
    pallas_call x44, Pallas kernels, call(): pl.pallas_call(kernel, out_shape=tuple(shapes), in_specs=[spec for _, spe...  35.1 us
    all_to_all x1, blocking collectives, exchange(): lax.all_to_all(array, 'dp', 0, 0, axis_index_groups=same_core, tiled=False)  33.3 us
    ppermute x24, waiting for transfers between devices, send_on(): return lax.ppermute(sent, 'section', pairs)  31 us
    ppermute x24, starting transfers between devices, send_on(): return lax.ppermute(sent, 'section', pairs)  30.3 us
    all_to_all x1, waiting for transfers between devices, exchange(): lax.all_to_all(array, 'dp', 0, 0, axis_index_groups=same_core, tiled=False)  12.1 us
    ppermute x1, waiting for transfers between devices, on_device(): lax.ppermute(total[1].astype(bf16), 'section', mirror).astype(f32)  10.7 us
    all_to_all x1, starting transfers between devices, exchange(): lax.all_to_all(array, 'dp', 0, 0, axis_index_groups=same_core, tiled=False)  6.04 us
    unnamed x12, local copies, waits for them, and re-layouts  5.18 us
  transfers between devices with their start and end apart: 27, of which 10 were waited for; matrix products, arithmetic and copies ran while one was open for 0% of the time, Pallas kernels for 19%

profile of v5, /device:TPU:18, one launch (start us, length us, event | category | flops | bytes accessed | tf_op | source)
XLA Modules:
  0.0 169.2 jit_solution(636298147217572378)
XLA Ops:
  0.7 0.7 copy-done.2
  1.4 0.2 forward_0_0.1
  1.6 0.7 collective-permute-start.1
  2.4 0.7 collective-permute-start
  3.2 1.3 copy-done
  4.5 1.6 copy-done.1
  6.2 1.3 collective-permute-start.3
  7.5 1.3 collective-permute-start.2
  8.9 2.3 %load_2.1 = (f32[1,4096]{1,0:T(1,128)S(1)}, bf16[4096,256]{1,0:T(8,128)(2,1)S(1)}, bf16[256,4096]{1,0:T(8,128)(2,1)S(1)}) custom-call(bf16[2,4096,256]{2,1,0:T(8,128)(2,1)} %refs_0_.14, bf16[2,256,4096]{2,1,0:T(8,128)(2,1)} %refs_1_.16, f32[2,4096]{1,0:T(2,128)S(1)} %copy-done.3), custom_call_target="tpu_custom_call" | custom-call | flops 1 | bytes 1 | tf_op jit(solution)/shard_map/load_2/pallas_call | solution.py:51
  11.2 12.9 %collective-permute-done.3.refs_0_ = bf16[32,4096]{1,0:T(8,128)(2,1)S(1)} collective-permute-done((bf16[32,4096]{1,0:T(8,128)(2,1)S(1)}, bf16[32,4096]{1,0:T(8,128)(2,1)S(1)}, u32[]{:S(2)}, u32[]{:S(2)}) %collective-permute-start.3) | collective-permute-done | bytes 262176 | tf_op jit(solution)/shard_map/ppermute | solution.py:171
  24.1 1.6 forward_2_0.1
  25.8 1.3 collective-permute-start.5
  27.1 3.2 %collective-permute-done.2.refs_0_ = bf16[32,4096]{1,0:T(8,128)(2,1)S(1)} collective-permute-done((bf16[32,4096]{1,0:T(8,128)(2,1)S(1)}, bf16[32,4096]{1,0:T(8,128)(2,1)S(1)}, u32[]{:S(2)}, u32[]{:S(2)}) %collective-permute-start.2) | collective-permute-done | bytes 262176 | tf_op jit(solution)/shard_map/ppermute | solution.py:171
  30.3 1.7 forward_2_1.1
  31.9 1.3 collective-permute-start.4
  33.3 0.3 load_3.1
  33.7 1.3 collective-permute-start.7
  35.0 4.3 %collective-permute-done.4.refs_0_ = bf16[32,4096]{1,0:T(8,128)(2,1)S(1)} collective-permute-done((bf16[32,4096]{1,0:T(8,128)(2,1)S(1)}, bf16[32,4096]{1,0:T(8,128)(2,1)S(1)}, u32[]{:S(2)}, u32[]{:S(2)}) %collective-permute-start.4) | collective-permute-done | bytes 262176 | tf_op jit(solution)/shard_map/ppermute | solution.py:171
  39.3 1.3 collective-permute-start.6
  40.6 2.3 %load_4.1 = (f32[1,4096]{1,0:T(1,128)S(1)}, bf16[4096,256]{1,0:T(8,128)(2,1)S(1)}, bf16[256,4096]{1,0:T(8,128)(2,1)S(1)}) custom-call(bf16[2,4096,256]{2,1,0:T(8,128)(2,1)} %refs_0_.14, bf16[2,256,4096]{2,1,0:T(8,128)(2,1)} %refs_1_.16, f32[2,4096]{1,0:T(2,128)S(1)} %copy-done.3), custom_call_target="tpu_custom_call" | custom-call | flops 1 | bytes 1 | tf_op jit(solution)/shard_map/load_4/pallas_call | solution.py:51
  42.9 1.7 %forward_4_0.1 = (bf16[8,192,768]{2,1,0:T(8,128)(2,1)}, bf16[8,128,512]{2,1,0:T(8,128)(2,1)}, f32[128,384]{1,0:T(8,128)}, bf16[32,4096]{1,0:T(8,128)(2,1)S(1)}) custom-call(bf16[32,4096]{1,0:T(8,128)(2,1)S(1)} %collective-permute-done.7.refs_0_, ...), custom_call_target="tpu_custom_call", output_to_operand_aliasing={{0}: (4, {}), {1}: (5, {}), {2}: (6, {})} | custom-call | flops 1 | bytes 1 | tf_op jit(solution)/shard_map/forward_4_0/pallas_call | solution.py:51
  44.6 4.3 %collective-permute-start.9 = (bf16[32,4096]{1,0:T(8,128)(2,1)S(1)}, bf16[32,4096]{1,0:T(8,128)(2,1)S(1)}, u32[]{:S(2)}, u32[]{:S(2)}) collective-permute-start(bf16[32,4096]{1,0:T(8,128)(2,1)S(1)} %get-tuple-element.325), channel_id=1, source_target_pairs={{32,16},{80,96},{33,17},{81,97},{34,18},{82,98},{35,19},{83,99},{3... | collective-permute-start | bytes 786440 | tf_op jit(solution)/shard_map/ppermute | solution.py:171
  48.9 4.1 %collective-permute-done.6.refs_0_ = bf16[32,4096]{1,0:T(8,128)(2,1)S(1)} collective-permute-done((bf16[32,4096]{1,0:T(8,128)(2,1)S(1)}, bf16[32,4096]{1,0:T(8,128)(2,1)S(1)}, u32[]{:S(2)}, u32[]{:S(2)}) %collective-permute-start.6) | collective-permute-done | bytes 262176 | tf_op jit(solution)/shard_map/ppermute | solution.py:171
  53.0 1.7 forward_4_1.1
  54.7 1.3 collective-permute-start.8
  56.0 19.2 %conditional.7 = (bf16[8,64,768]{2,1,0:T(8,128)(2,1)}) conditional(s32[]{:T(128)} %convert_element_type.29, () %tuple.72, bf16[8,64,768]{2,1,0:T(8,128)(2,1)} %get-tuple-element.315), branch_computations={%region_2.3_spmd, %region_3.4_spmd} | conditional | flops 1 | bytes 2359337 | solution.py:404
  56.0 6.0 %all-to-all-start.1 = ((bf16[8,64,768]{2,1,0:T(8,128)(2,1)}), bf16[8,64,768]{2,1,0:T(8,128)(2,1)S(1)}, u32[]{:S(2)}, u32[]{:S(2)}) async-start(bf16[8,64,768]{2,1,0:T(8,128)(2,1)} %param.3), calls=%async_computation.1 | async-start | bytes 1572864 | tf_op jit(solution)/shard_map/cond/branch_1_fun/all_to_all | solution.py:183
  62.1 12.1 %all-to-all-done.1.refs_0_ = bf16[8,64,768]{2,1,0:T(8,128)(2,1)S(1)} async-done(((bf16[8,64,768]{2,1,0:T(8,128)(2,1)}), bf16[8,64,768]{2,1,0:T(8,128)(2,1)S(1)}, u32[]{:S(2)}, u32[]{:S(2)}) %all-to-all-start.1) | async-done | bytes 786464 | tf_op jit(solution)/shard_map/cond/branch_1_fun/all_to_all | solution.py:183
  74.2 1.0 unstage.5
  75.4 0.7 collective-permute-start.11
  76.2 0.7 collective-permute-start.10
  77.0 0.7 collective-permute-start.13
  77.8 0.7 collective-permute-start.12
  78.7 1.3 collective-permute-start.15
  80.0 1.3 collective-permute-start.14
  81.4 1.3 saved_far_2.1
  82.6 4.3 %turn_far_2.1 = (f32[1,4096]{1,0:T(1,128)S(1)}, bf16[256,4096]{1,0:T(8,128)(2,1)S(1)}, bf16[4096,256]{1,0:T(8,128)(2,1)S(1)}) custom-call(bf16[2,4096,256]{2,1,0:T(8,128)(2,1)} %refs_0_.14, bf16[2,256,4096]{2,1,0:T(8,128)(2,1)} %refs_1_.16, f32[2,4096]{1,0:T(2,128)S(1)} %copy-done.3), custom_call_target="tpu_custom_call" | custom-call | flops 1 | bytes 1 | tf_op jit(solution)/shard_map/turn_far_2/pallas_call | solution.py:51
  86.9 1.7 %collective-permute-done.15.refs_0_ = bf16[32,4096]{1,0:T(8,128)(2,1)S(1)} collective-permute-done((bf16[32,4096]{1,0:T(8,128)(2,1)S(1)}, bf16[32,4096]{1,0:T(8,128)(2,1)S(1)}, u32[]{:S(2)}, u32[]{:S(2)}) %collective-permute-start.15) | collective-permute-done | bytes 262176 | tf_op jit(solution)/shard_map/ppermute | solution.py:171
  88.7 1.5 backward_8_0.1
  90.2 1.3 collective-permute-start.17
  91.5 2.0 %collective-permute-done.14.refs_0_ = bf16[32,4096]{1,0:T(8,128)(2,1)S(1)} collective-permute-done((bf16[32,4096]{1,0:T(8,128)(2,1)S(1)}, bf16[32,4096]{1,0:T(8,128)(2,1)S(1)}, u32[]{:S(2)}, u32[]{:S(2)}) %collective-permute-start.14) | collective-permute-done | bytes 262176 | tf_op jit(solution)/shard_map/ppermute | solution.py:171
  93.5 1.5 backward_8_1.1
  94.9 1.3 collective-permute-start.16
  96.5 0.3 backward_9_0.1
  96.8 1.3 collective-permute-start.19
  98.1 2.8 %collective-permute-done.16.refs_0_ = bf16[32,4096]{1,0:T(8,128)(2,1)S(1)} collective-permute-done((bf16[32,4096]{1,0:T(8,128)(2,1)S(1)}, bf16[32,4096]{1,0:T(8,128)(2,1)S(1)}, u32[]{:S(2)}, u32[]{:S(2)}) %collective-permute-start.16) | collective-permute-done | bytes 262176 | tf_op jit(solution)/shard_map/ppermute | solution.py:171
  101.0 1.3 collective-permute-start.18
  102.3 1.3 saved_10.1
  103.6 4.3 %turn_10.1 = (f32[1,4096]{1,0:T(1,128)S(1)}, bf16[256,4096]{1,0:T(8,128)(2,1)S(1)}, bf16[4096,256]{1,0:T(8,128)(2,1)S(1)}) custom-call(bf16[2,4096,256]{2,1,0:T(8,128)(2,1)} %refs_0_.14, bf16[2,256,4096]{2,1,0:T(8,128)(2,1)} %refs_1_.16, f32[2,4096]{1,0:T(2,128)S(1)} %copy-done.3), custom_call_target="tpu_custom_call" | custom-call | flops 1 | bytes 1 | tf_op jit(solution)/shard_map/turn_10/pallas_call | solution.py:51
  107.9 1.5 backward_10_0.1
  109.4 2.4 %collective-permute-start.21 = (bf16[32,4096]{1,0:T(8,128)(2,1)S(1)}, bf16[32,4096]{1,0:T(8,128)(2,1)S(1)}, u32[]{:S(2)}, u32[]{:S(2)}) collective-permute-start(bf16[32,4096]{1,0:T(8,128)(2,1)S(1)} %get-tuple-element.416), channel_id=1, source_target_pairs={{32,16},{80,96},{33,17},{81,97},{34,18},{82,98},{35,19},{83,99},{3... | collective-permute-start | bytes 786440 | tf_op jit(solution)/shard_map/ppermute | solution.py:171
  111.8 1.5 backward_10_1.1
  113.3 1.3 collective-permute-start.20
  114.6 33.3 %conditional.9 = (bf16[8,192,768]{2,1,0:T(8,128)(2,1)}) conditional(s32[]{:T(128)} %convert_element_type.29, () %tuple.80, bf16[8,192,768]{2,1,0:T(8,128)(2,1)} %get-tuple-element.404), branch_computations={%region_7.8_spmd, %region_8.9_spmd} | conditional | bytes 4718600 | solution.py:542
  114.6 33.3 %all_to_all.28 = bf16[8,192,768]{2,1,0:T(8,128)(2,1)} all-to-all(bf16[8,192,768]{2,1,0:T(8,128)(2,1)} %param.8), channel_id=1, replica_groups={{0,2,4,6,8,10,12,14},{1,3,5,7,9,11,13,15},{16,18,20,22,24,26,28,30},{17..., dimensions={0} | all-to-all | bytes 4718592 | tf_op jit(solution)/shard_map/cond/branch_1_fun/all_to_all | solution.py:183
  148.2 0.7 collective-permute-start.23
  149.0 0.7 collective-permute-start.22
  150.2 1.3 copy-done.4
  151.5 0.2 copy-done.5
  151.7 3.0 %conditional.11 = ((f32[2,2,256,256]{3,2,1,0:T(8,128)S(1)}, bf16[2,2,256,256]{3,2,1,0:T(8,128)(2,1)S(1)})) conditional(s32[]{:T(128)} %clamp.4, (bf16[8,64,768]{2,1,0:T(8,128)(2,1)}, bf16[8,64,768]{2,1,0:T(8,128)(2,1)S(1)}, bf16[8,128,768]{2,1,0:T(8,128)(2,1)S(1)}) %tuple.110, (bf16[8,64,768]{2,1,0:T(8,128)(2,1)S(1)}, ...), branch_computations={%region_11.12_spmd, %region_12.13_spmd, %region_13.14_spmd} | conditional | flops 1 | bytes 1572873 | solution.py:600
  151.7 3.0 %products_2.1 = (f32[2,2,256,256]{3,2,1,0:T(8,128)S(1)}, bf16[2,2,256,256]{3,2,1,0:T(8,128)(2,1)S(1)}) custom-call(bf16[8,64,768]{2,1,0:T(8,128)(2,1)} %get-tuple-element.40.refs_0_, bf16[8,192,768]{2,1,0:T(8,128)(2,1)} %get-tuple-element.41.refs_1_), custom_call_target="tpu_custom_call" | custom-call | flops 1 | bytes 1 | tf_op jit(solution)/shard_map/cond/branch_2_fun/products_2/pallas_call | solution.py:51
  154.8 1.9 %collective-permute-done.24 = bf16[2,2,256,256]{3,2,1,0:T(8,128)(2,1)S(1)} collective-permute-done((bf16[2,2,256,256]{3,2,1,0:T(8,128)(2,1)S(1)}, bf16[2,2,256,256]{3,2,1,0:T(8,128)(2,1)S(1)}, u32[]{:S(2)}, u32[]{:S(2)}) %collective-permute-start.24) | collective-permute-done | bytes 524320 | tf_op jit(solution)/shard_map/ppermute | solution.py:621
  157.0 10.7 %collective-permute-done.25 = bf16[2,256,256]{2,1,0:T(8,128)(2,1)S(1)} collective-permute-done((bf16[2,256,256]{2,1,0:T(8,128)(2,1)S(1)}, bf16[2,256,256]{2,1,0:T(8,128)(2,1)S(1)}, u32[]{:S(2)}, u32[]{:S(2)}) %collective-permute-start.25) | collective-permute-done | bytes 262176 | tf_op jit(solution)/shard_map/ppermute | solution.py:623
  167.7 1.5 multiply_reduce_fusion
  (73 shorter events, 2.7 us)
Async XLA Ops:
  0.6 0.8 copy-start.2
  1.6 2.9 %collective-permute-start.1 = (bf16[32,4096]{1,0:T(8,128)(2,1)S(1)}, bf16[32,4096]{1,0:T(8,128)(2,1)S(1)}, u32[]{:S(2)}, u32[]{:S(2)}) collective-permute-start(bf16[32,4096]{1,0:T(8,128)(2,1)S(1)} %get-tuple-element.255), channel_id=1, source_target_pairs={{0,16},{112,96},{1,17},{113,97},{2,18},{114,98},{3,19},{115,99},{4... | collective-permute-start | bytes 786440 | tf_op jit(solution)/shard_map/ppermute | solution.py:171
  2.3 0.8 copy-start.3
  2.4 5.1 %collective-permute-start = (bf16[32,4096]{1,0:T(8,128)(2,1)S(1)}, bf16[32,4096]{1,0:T(8,128)(2,1)S(1)}, u32[]{:S(2)}, u32[]{:S(2)}) collective-permute-start(bf16[32,4096]{1,0:T(8,128)(2,1)S(1)} %get-tuple-element.251), channel_id=1, source_target_pairs={{0,16},{112,96},{1,17},{113,97},{2,18},{114,98},{3,19},{115,99},{4... | collective-permute-start | bytes 786440 | tf_op jit(solution)/shard_map/ppermute | solution.py:171
  3.2 1.3 copy-start
  4.5 1.6 copy-start.1
  6.2 18.0 %collective-permute-start.3 = (bf16[32,4096]{1,0:T(8,128)(2,1)S(1)}, bf16[32,4096]{1,0:T(8,128)(2,1)S(1)}, u32[]{:S(2)}, u32[]{:S(2)}) collective-permute-start(bf16[32,4096]{1,0:T(8,128)(2,1)S(1)} %get-tuple-element.272), channel_id=1, source_target_pairs={{16,32},{96,80},{17,33},{97,81},{18,34},{98,82},{19,35},{99,83},{2... | collective-permute-start | bytes 786440 | tf_op jit(solution)/shard_map/ppermute | solution.py:171
  7.5 22.7 %collective-permute-start.2 = (bf16[32,4096]{1,0:T(8,128)(2,1)S(1)}, bf16[32,4096]{1,0:T(8,128)(2,1)S(1)}, u32[]{:S(2)}, u32[]{:S(2)}) collective-permute-start(bf16[32,4096]{1,0:T(8,128)(2,1)S(1)} %get-tuple-element.261), channel_id=1, source_target_pairs={{16,32},{96,80},{17,33},{97,81},{18,34},{98,82},{19,35},{99,83},{2... | collective-permute-start | bytes 786440 | tf_op jit(solution)/shard_map/ppermute | solution.py:171
  25.8 7.8 %collective-permute-start.5 = (bf16[32,4096]{1,0:T(8,128)(2,1)S(1)}, bf16[32,4096]{1,0:T(8,128)(2,1)S(1)}, u32[]{:S(2)}, u32[]{:S(2)}) collective-permute-start(bf16[32,4096]{1,0:T(8,128)(2,1)S(1)} %get-tuple-element.289), channel_id=1, source_target_pairs={{32,48},{80,64},{33,49},{81,65},{34,50},{82,66},{35,51},{83,67},{3... | collective-permute-start | bytes 786440 | tf_op jit(solution)/shard_map/ppermute | solution.py:171
  31.9 7.3 %collective-permute-start.4 = (bf16[32,4096]{1,0:T(8,128)(2,1)S(1)}, bf16[32,4096]{1,0:T(8,128)(2,1)S(1)}, u32[]{:S(2)}, u32[]{:S(2)}) collective-permute-start(bf16[32,4096]{1,0:T(8,128)(2,1)S(1)} %get-tuple-element.279), channel_id=1, source_target_pairs={{32,48},{80,64},{33,49},{81,65},{34,50},{82,66},{35,51},{83,67},{3... | collective-permute-start | bytes 786440 | tf_op jit(solution)/shard_map/ppermute | solution.py:171
  33.7 9.2 %collective-permute-start.7 = (bf16[32,4096]{1,0:T(8,128)(2,1)S(1)}, bf16[32,4096]{1,0:T(8,128)(2,1)S(1)}, u32[]{:S(2)}, u32[]{:S(2)}) collective-permute-start(bf16[32,4096]{1,0:T(8,128)(2,1)S(1)} %get-tuple-element.305), channel_id=1, source_target_pairs={{48,32},{64,80},{49,33},{65,81},{50,34},{66,82},{51,35},{67,83},{5... | collective-permute-start | bytes 786440 | tf_op jit(solution)/shard_map/ppermute | solution.py:171
  39.3 13.8 %collective-permute-start.6 = (bf16[32,4096]{1,0:T(8,128)(2,1)S(1)}, bf16[32,4096]{1,0:T(8,128)(2,1)S(1)}, u32[]{:S(2)}, u32[]{:S(2)}) collective-permute-start(bf16[32,4096]{1,0:T(8,128)(2,1)S(1)} %get-tuple-element.298), channel_id=1, source_target_pairs={{48,32},{64,80},{49,33},{65,81},{50,34},{66,82},{51,35},{67,83},{5... | collective-permute-start | bytes 786440 | tf_op jit(solution)/shard_map/ppermute | solution.py:171
  44.6 30.8 %collective-permute-start.9 = (bf16[32,4096]{1,0:T(8,128)(2,1)S(1)}, bf16[32,4096]{1,0:T(8,128)(2,1)S(1)}, u32[]{:S(2)}, u32[]{:S(2)}) collective-permute-start(bf16[32,4096]{1,0:T(8,128)(2,1)S(1)} %get-tuple-element.325), channel_id=1, source_target_pairs={{32,16},{80,96},{33,17},{81,97},{34,18},{82,98},{35,19},{83,99},{3... | collective-permute-start | bytes 786440 | tf_op jit(solution)/shard_map/ppermute | solution.py:171
  54.7 21.4 %collective-permute-start.8 = (bf16[32,4096]{1,0:T(8,128)(2,1)S(1)}, bf16[32,4096]{1,0:T(8,128)(2,1)S(1)}, u32[]{:S(2)}, u32[]{:S(2)}) collective-permute-start(bf16[32,4096]{1,0:T(8,128)(2,1)S(1)} %get-tuple-element.312), channel_id=1, source_target_pairs={{32,16},{80,96},{33,17},{81,97},{34,18},{82,98},{35,19},{83,99},{3... | collective-permute-start | bytes 786440 | tf_op jit(solution)/shard_map/ppermute | solution.py:171
  56.0 18.1 %all-to-all-start.1 = ((bf16[8,64,768]{2,1,0:T(8,128)(2,1)}), bf16[8,64,768]{2,1,0:T(8,128)(2,1)S(1)}, u32[]{:S(2)}, u32[]{:S(2)}) async-start(bf16[8,64,768]{2,1,0:T(8,128)(2,1)} %param.3), calls=%async_computation.1 | async-start | bytes 1572864 | tf_op jit(solution)/shard_map/cond/branch_1_fun/all_to_all | solution.py:183
  75.4 1.4 collective-permute-start.11
  76.2 1.5 collective-permute-start.10
  77.0 1.6 collective-permute-start.13
  77.8 2.2 %collective-permute-start.12 = (bf16[32,4096]{1,0:T(8,128)(2,1)S(1)}, bf16[32,4096]{1,0:T(8,128)(2,1)S(1)}, u32[]{:S(2)}, u32[]{:S(2)}) collective-permute-start(bf16[32,4096]{1,0:T(8,128)(2,1)S(1)} %get-tuple-element.340), channel_id=1, source_target_pairs={{0,16},{112,96},{1,17},{113,97},{2,18},{114,98},{3,19},{115,99},{4... | collective-permute-start | bytes 786440 | tf_op jit(solution)/shard_map/ppermute | solution.py:171
  78.7 10.0 %collective-permute-start.15 = (bf16[32,4096]{1,0:T(8,128)(2,1)S(1)}, bf16[32,4096]{1,0:T(8,128)(2,1)S(1)}, u32[]{:S(2)}, u32[]{:S(2)}) collective-permute-start(bf16[32,4096]{1,0:T(8,128)(2,1)S(1)} %get-tuple-element.369), channel_id=1, source_target_pairs={{16,32},{96,80},{17,33},{97,81},{18,34},{98,82},{19,35},{99,83},{2... | collective-permute-start | bytes 786440 | tf_op jit(solution)/shard_map/ppermute | solution.py:171
  80.0 13.4 %collective-permute-start.14 = (bf16[32,4096]{1,0:T(8,128)(2,1)S(1)}, bf16[32,4096]{1,0:T(8,128)(2,1)S(1)}, u32[]{:S(2)}, u32[]{:S(2)}) collective-permute-start(bf16[32,4096]{1,0:T(8,128)(2,1)S(1)} %get-tuple-element.349), channel_id=1, source_target_pairs={{16,32},{96,80},{17,33},{97,81},{18,34},{98,82},{19,35},{99,83},{2... | collective-permute-start | bytes 786440 | tf_op jit(solution)/shard_map/ppermute | solution.py:171
  90.2 6.4 %collective-permute-start.17 = (bf16[32,4096]{1,0:T(8,128)(2,1)S(1)}, bf16[32,4096]{1,0:T(8,128)(2,1)S(1)}, u32[]{:S(2)}, u32[]{:S(2)}) collective-permute-start(bf16[32,4096]{1,0:T(8,128)(2,1)S(1)} %get-tuple-element.383), channel_id=1, source_target_pairs={{32,48},{80,64},{33,49},{81,65},{34,50},{82,66},{35,51},{83,67},{3... | collective-permute-start | bytes 786440 | tf_op jit(solution)/shard_map/ppermute | solution.py:171
  94.9 6.0 %collective-permute-start.16 = (bf16[32,4096]{1,0:T(8,128)(2,1)S(1)}, bf16[32,4096]{1,0:T(8,128)(2,1)S(1)}, u32[]{:S(2)}, u32[]{:S(2)}) collective-permute-start(bf16[32,4096]{1,0:T(8,128)(2,1)S(1)} %get-tuple-element.373), channel_id=1, source_target_pairs={{32,48},{80,64},{33,49},{81,65},{34,50},{82,66},{35,51},{83,67},{3... | collective-permute-start | bytes 786440 | tf_op jit(solution)/shard_map/ppermute | solution.py:171
  96.8 11.0 %collective-permute-start.19 = (bf16[32,4096]{1,0:T(8,128)(2,1)S(1)}, bf16[32,4096]{1,0:T(8,128)(2,1)S(1)}, u32[]{:S(2)}, u32[]{:S(2)}) collective-permute-start(bf16[32,4096]{1,0:T(8,128)(2,1)S(1)} %get-tuple-element.397), channel_id=1, source_target_pairs={{48,32},{64,80},{49,33},{65,81},{50,34},{66,82},{51,35},{67,83},{5... | collective-permute-start | bytes 786440 | tf_op jit(solution)/shard_map/ppermute | solution.py:171
  101.0 10.8 %collective-permute-start.18 = (bf16[32,4096]{1,0:T(8,128)(2,1)S(1)}, bf16[32,4096]{1,0:T(8,128)(2,1)S(1)}, u32[]{:S(2)}, u32[]{:S(2)}) collective-permute-start(bf16[32,4096]{1,0:T(8,128)(2,1)S(1)} %get-tuple-element.387), channel_id=1, source_target_pairs={{48,32},{64,80},{49,33},{65,81},{50,34},{66,82},{51,35},{67,83},{5... | collective-permute-start | bytes 786440 | tf_op jit(solution)/shard_map/ppermute | solution.py:171
  109.4 38.8 %collective-permute-start.21 = (bf16[32,4096]{1,0:T(8,128)(2,1)S(1)}, bf16[32,4096]{1,0:T(8,128)(2,1)S(1)}, u32[]{:S(2)}, u32[]{:S(2)}) collective-permute-start(bf16[32,4096]{1,0:T(8,128)(2,1)S(1)} %get-tuple-element.416), channel_id=1, source_target_pairs={{32,16},{80,96},{33,17},{81,97},{34,18},{82,98},{35,19},{83,99},{3... | collective-permute-start | bytes 786440 | tf_op jit(solution)/shard_map/ppermute | solution.py:171
  113.3 35.6 %collective-permute-start.20 = (bf16[32,4096]{1,0:T(8,128)(2,1)S(1)}, bf16[32,4096]{1,0:T(8,128)(2,1)S(1)}, u32[]{:S(2)}, u32[]{:S(2)}) collective-permute-start(bf16[32,4096]{1,0:T(8,128)(2,1)S(1)} %get-tuple-element.401), channel_id=1, source_target_pairs={{32,16},{80,96},{33,17},{81,97},{34,18},{82,98},{35,19},{83,99},{3... | collective-permute-start | bytes 786440 | tf_op jit(solution)/shard_map/ppermute | solution.py:171
  148.2 1.8 %collective-permute-start.23 = (bf16[32,4096]{1,0:T(8,128)(2,1)S(1)}, bf16[32,4096]{1,0:T(8,128)(2,1)S(1)}, u32[]{:S(2)}, u32[]{:S(2)}) collective-permute-start(bf16[32,4096]{1,0:T(8,128)(2,1)S(1)} %get-tuple-element.434), channel_id=1, source_target_pairs={{16,0},{96,112},{17,1},{97,113},{18,2},{98,114},{19,3},{99,115},{2... | collective-permute-start | bytes 786440 | tf_op jit(solution)/shard_map/ppermute | solution.py:171
  149.0 1.1 collective-permute-start.22
  150.1 1.4 copy-start.4
  150.1 1.6 copy-start.5
  154.7 2.3 %slice-start = ((f32[2,4096]{1,0:T(2,128)}), f32[1,4096]{1,0:T(1,128)S(1)}, s32[]{:S(2)}) async-start(f32[2,4096]{1,0:T(2,128)} %refs_2_.21), calls=%async_computation.7 | async-start | bytes 32768 | tf_op jit(solution)/shard_map/slice | solution.py:625
  154.7 2.0 %collective-permute-start.24 = (bf16[2,2,256,256]{3,2,1,0:T(8,128)(2,1)S(1)}, bf16[2,2,256,256]{3,2,1,0:T(8,128)(2,1)S(1)}, u32[]{:S(2)}, u32[]{:S(2)}) collective-permute-start(bf16[2,2,256,256]{3,2,1,0:T(8,128)(2,1)S(1)} %get-tuple-element.446), channel_id=1, source_target_pairs={{0,1},{1,0},{2,3},{3,2},{4,5},{5,4},{6,7},{7,6},{8,9},{9,8},{10,11... | collective-permute-start | bytes 1572872 | tf_op jit(solution)/shard_map/ppermute | solution.py:621
  156.8 10.8 %collective-permute-start.25 = (bf16[2,256,256]{2,1,0:T(8,128)(2,1)S(1)}, bf16[2,256,256]{2,1,0:T(8,128)(2,1)S(1)}, u32[]{:S(2)}, u32[]{:S(2)}) collective-permute-start(bf16[2,256,256]{2,1,0:T(8,128)(2,1)S(1)} %fusion.1), channel_id=1, source_target_pairs={{0,112},{16,96},{32,80},{48,64},{64,48},{80,32},{96,16},{112,0},{1... | collective-permute-start | bytes 786440 | tf_op jit(solution)/shard_map/ppermute | solution.py:623
  157.0 10.8 %slice-start.1 = ((bf16[2,4096,256]{2,1,0:T(8,128)(2,1)}), bf16[1,4096,256]{2,1,0:T(8,128)(2,1)S(1)}, s32[]{:S(2)}) async-start(bf16[2,4096,256]{2,1,0:T(8,128)(2,1)} %refs_0_.14), calls=%async_computation.8 | async-start | bytes 4194304 | tf_op jit(solution)/shard_map/slice | solution.py:626

commit v6 on v4

--- a/solution.py
+++ b/solution.py
@@ -532,34 +532,6 @@
     far_1 = (*far_1, *saved_rows("saved_10", lambda fold: fold == 2, 0))
     box_late_two = backward_stage(10, {0: 1}, box_late_two, [far_1])
 
-    box_late_two, kept = lax.optimization_barrier((box_late_two, kept))
-    got_late_two = lax.cond(
-        fold_here >= 2,
-        functools.partial(exchange, raw=True),
-        functools.partial(none, "none_late_two"),
-        box_late_two,
-    )
-    got_late_two, box_late, kept, hats, raw_in, raw_out = lax.optimization_barrier(
-        (got_late_two, box_late, kept, hats, raw_in, raw_out)
-    )
-    (near_1,) = fresh_weights("turn_11", lambda fold: fold == 1, (0,), 0, 1)
-    near_1 = (*near_1, *saved_rows("saved_11", lambda fold: fold == 1, 0))
-    box_late = backward_stage(11, {0: 1}, box_late, [near_1])
-
-    box_late, kept = lax.optimization_barrier((box_late, kept))
-    got_late = lax.cond(
-        fold_here == 1,
-        functools.partial(exchange, raw=True),
-        functools.partial(none, "none_late"),
-        box_late,
-    )
-    got_late, box_end, kept, raw_in, raw_out = lax.optimization_barrier(
-        (got_late, box_end, kept, raw_in, raw_out)
-    )
-    (near_1,) = fresh_weights("turn_12", lambda fold: fold == 0, (0,), 0, 1)
-    near_1 = (*near_1, *saved_rows("saved_12", lambda fold: fold == 0, 0))
-    box_end = backward_stage(LAST, {0: 0}, box_end, [near_1])
-
     def products(pick, reads, keep, send, whole_in, whole_out):
         _, half = place()
         core = lax.rem(lax.axis_index("dp"), 2)
@@ -589,28 +561,63 @@
             scratch=[pltpu.VMEM((2 * branch, branch), f32), pltpu.VMEM((branch, 2 * branch), f32)],
         )
 
-    near_pick = (((0, 0), (1, 1)), ((2, 0), (1, 0)))
-    far_pick = (((0, 0), (1, 1)), ((1, 2), (1, 0)))
+    def nothing(*_):
+        return call(
+            lambda reads, keep, send: None,
+            "nothing",
+            [],
+            new=(pltpu.VMEM((2, 2, branch, branch), f32), pltpu.VMEM((2, 2, branch, branch), bf16)),
+        )
+
+    box_late_two, kept = lax.optimization_barrier((box_late_two, kept))
+    done_far = lax.cond(
+        fold_here >= 2,
+        lambda late, two: finish(
+            "products_far", (((0, 0), (1, 1)), ((1, 2), (1, 0))), two, exchange(late, raw=True)
+        ),
+        nothing,
+        box_late_two,
+        got_two,
+    )
+    done_far, box_late, kept, hats, raw_in, raw_out = lax.optimization_barrier(
+        (done_far, box_late, kept, hats, raw_in, raw_out)
+    )
+    (near_1,) = fresh_weights("turn_11", lambda fold: fold == 1, (0,), 0, 1)
+    near_1 = (*near_1, *saved_rows("saved_11", lambda fold: fold == 1, 0))
+    box_late = backward_stage(11, {0: 1}, box_late, [near_1])
+
+    box_late, kept = lax.optimization_barrier((box_late, kept))
+    done_one = lax.cond(
+        fold_here == 1,
+        lambda late, early, one: finish(
+            "products_one", (((0, 0), (1, 1)), ((2, 0), (1, 0))), early, exchange(late, raw=True), one
+        ),
+        nothing,
+        box_late,
+        got_early,
+        got_one,
+    )
+    done_one, box_end, kept, raw_in, raw_out = lax.optimization_barrier(
+        (done_one, box_end, kept, raw_in, raw_out)
+    )
+    (near_1,) = fresh_weights("turn_12", lambda fold: fold == 0, (0,), 0, 1)
+    near_1 = (*near_1, *saved_rows("saved_12", lambda fold: fold == 0, 0))
+    box_end = backward_stage(LAST, {0: 0}, box_end, [near_1])
+
     keep, send = lax.switch(
         jnp.minimum(fold_here, 2),
         (
-            lambda end, late, late_two, early, near, one, two: finish(
+            lambda end, early, near, one, far: finish(
                 "products_0", (((0, 0), (1, 0)), ((2, 0), (2, 1))), early, exchange(end, raw=True), near
             ),
-            lambda end, late, late_two, early, near, one, two: finish(
-                "products_1", near_pick, early, late, one
-            ),
-            lambda end, late, late_two, early, near, one, two: finish(
-                "products_2", far_pick, two, late_two
-            ),
+            lambda end, early, near, one, far: one,
+            lambda end, early, near, one, far: far,
         ),
         box_end,
-        got_late,
-        got_late_two,
         got_early,
         got_near,
-        got_one,
-        got_two,
+        tuple(done_one),
+        tuple(done_far),
     )
     total = keep + lax.ppermute(send, "dp", [(i, i ^ 1) for i in range(parts)]).astype(f32)
     mirror = [(s, sections - 1 - s) for s in range(sections)]

time: 169 us -> 170 us (level)
    pallas_call x44 -> x45, Pallas kernels: 34.8 us -> 35.4 us  [call(): pl.pallas_call(kernel, out_shape=tuple(shapes), in_specs=[spec for _, spe...]
  transfers between devices with their start and end apart: 27 -> 27, of which waited for: 14 -> 14; matrix products, arithmetic and copies ran while one was open for 0% -> 0% of each run, Pallas kernels for 19% -> 20%
where the time goes in v6:
time: 170 us; the launch traced here: 169 us
  waiting for transfers between devices  55.7 us (33%)
  blocking collectives  36.3 us (21%)
  Pallas kernels  35.4 us (21%)
  starting transfers between devices  33 us (19%)
  local copies, waits for them, and re-layouts  5.1 us (3%)
    all_to_all x1, blocking collectives, exchange(): lax.all_to_all(array, 'dp', 0, 0, axis_index_groups=same_core, tiled=False)  36.3 us
    pallas_call x45, Pallas kernels, call(): pl.pallas_call(kernel, out_shape=tuple(shapes), in_specs=[spec for _, spe...  35.4 us
    ppermute x24, waiting for transfers between devices, send_on(): return lax.ppermute(sent, 'section', pairs)  32.3 us
    ppermute x24, starting transfers between devices, send_on(): return lax.ppermute(sent, 'section', pairs)  26.9 us
    ppermute x1, waiting for transfers between devices, on_device(): lax.ppermute(total[1].astype(bf16), 'section', mirror).astype(f32)  10.7 us
    all_to_all x1, waiting for transfers between devices, exchange(): lax.all_to_all(array, 'dp', 0, 0, axis_index_groups=same_core, tiled=False)  10.6 us
    all_to_all x1, starting transfers between devices, exchange(): lax.all_to_all(array, 'dp', 0, 0, axis_index_groups=same_core, tiled=False)  6.04 us
    unnamed x12, local copies, waits for them, and re-layouts  4.18 us
  transfers between devices with their start and end apart: 27, of which 14 were waited for; matrix products, arithmetic and copies ran while one was open for 0% of the time, Pallas kernels for 20%

profile of v6, /device:TPU:18, one launch (start us, length us, event | category | flops | bytes accessed | tf_op | source)
XLA Modules:
  0.0 168.8 jit_solution(15074955924787304854)
XLA Ops:
  0.7 0.7 copy-done.2
  1.6 0.7 collective-permute-start.1
  2.4 0.7 collective-permute-start
  3.2 1.3 copy-done
  4.5 1.6 copy-done.1
  6.2 1.3 collective-permute-start.3
  7.5 1.3 collective-permute-start.2
  8.9 2.3 %load_2.1 = (f32[1,4096]{1,0:T(1,128)S(1)}, bf16[4096,256]{1,0:T(8,128)(2,1)S(1)}, bf16[256,4096]{1,0:T(8,128)(2,1)S(1)}) custom-call(bf16[2,4096,256]{2,1,0:T(8,128)(2,1)} %refs_0_.14, bf16[2,256,4096]{2,1,0:T(8,128)(2,1)} %refs_1_.16, f32[2,4096]{1,0:T(2,128)S(1)} %copy-done.3), custom_call_target="tpu_custom_call" | custom-call | flops 1 | bytes 1 | tf_op jit(solution)/shard_map/load_2/pallas_call | solution.py:51
  11.2 16.4 %collective-permute-done.3.refs_0_ = bf16[32,4096]{1,0:T(8,128)(2,1)S(1)} collective-permute-done((bf16[32,4096]{1,0:T(8,128)(2,1)S(1)}, bf16[32,4096]{1,0:T(8,128)(2,1)S(1)}, u32[]{:S(2)}, u32[]{:S(2)}) %collective-permute-start.3) | collective-permute-done | bytes 262176 | tf_op jit(solution)/shard_map/ppermute | solution.py:171
  27.6 1.7 forward_2_0.1
  29.2 1.3 collective-permute-start.5
  30.6 1.1 collective-permute-done.2.refs_0_
  31.6 1.7 forward_2_1.1
  33.3 1.3 collective-permute-start.4
  35.2 1.3 collective-permute-start.7
  36.5 3.5 %collective-permute-done.4.refs_0_ = bf16[32,4096]{1,0:T(8,128)(2,1)S(1)} collective-permute-done((bf16[32,4096]{1,0:T(8,128)(2,1)S(1)}, bf16[32,4096]{1,0:T(8,128)(2,1)S(1)}, u32[]{:S(2)}, u32[]{:S(2)}) %collective-permute-start.4) | collective-permute-done | bytes 262176 | tf_op jit(solution)/shard_map/ppermute | solution.py:171
  40.1 1.3 collective-permute-start.6
  41.4 2.3 %load_4.1 = (f32[1,4096]{1,0:T(1,128)S(1)}, bf16[4096,256]{1,0:T(8,128)(2,1)S(1)}, bf16[256,4096]{1,0:T(8,128)(2,1)S(1)}) custom-call(bf16[2,4096,256]{2,1,0:T(8,128)(2,1)} %refs_0_.14, bf16[2,256,4096]{2,1,0:T(8,128)(2,1)} %refs_1_.16, f32[2,4096]{1,0:T(2,128)S(1)} %copy-done.3), custom_call_target="tpu_custom_call" | custom-call | flops 1 | bytes 1 | tf_op jit(solution)/shard_map/load_4/pallas_call | solution.py:51
  43.7 2.7 %collective-permute-done.7.refs_0_ = bf16[32,4096]{1,0:T(8,128)(2,1)S(1)} collective-permute-done((bf16[32,4096]{1,0:T(8,128)(2,1)S(1)}, bf16[32,4096]{1,0:T(8,128)(2,1)S(1)}, u32[]{:S(2)}, u32[]{:S(2)}) %collective-permute-start.7) | collective-permute-done | bytes 262176 | tf_op jit(solution)/shard_map/ppermute | solution.py:171
  46.4 1.7 forward_4_0.1
  48.1 1.3 collective-permute-start.9
  49.4 2.8 %collective-permute-done.6.refs_0_ = bf16[32,4096]{1,0:T(8,128)(2,1)S(1)} collective-permute-done((bf16[32,4096]{1,0:T(8,128)(2,1)S(1)}, bf16[32,4096]{1,0:T(8,128)(2,1)S(1)}, u32[]{:S(2)}, u32[]{:S(2)}) %collective-permute-start.6) | collective-permute-done | bytes 262176 | tf_op jit(solution)/shard_map/ppermute | solution.py:171
  52.2 1.7 %forward_4_1.1 = (bf16[8,192,768]{2,1,0:T(8,128)(2,1)}, bf16[8,128,512]{2,1,0:T(8,128)(2,1)}, f32[128,384]{1,0:T(8,128)}, bf16[32,4096]{1,0:T(8,128)(2,1)S(1)}) custom-call(bf16[32,4096]{1,0:T(8,128)(2,1)S(1)} %collective-permute-done.6.refs_0_, ...), custom_call_target="tpu_custom_call", output_to_operand_aliasing={{0}: (4, {}), {1}: (5, {}), {2}: (6, {})} | custom-call | flops 1 | bytes 1 | tf_op jit(solution)/shard_map/forward_4_1/pallas_call | solution.py:51
  53.9 1.3 collective-permute-start.8
  55.3 17.7 %conditional.7 = (bf16[8,64,768]{2,1,0:T(8,128)(2,1)}) conditional(s32[]{:T(128)} %convert_element_type.29, () %tuple.72, bf16[8,64,768]{2,1,0:T(8,128)(2,1)} %get-tuple-element.321), branch_computations={%region_2.3_spmd, %region_3.4_spmd} | conditional | flops 1 | bytes 2359337 | solution.py:398
  55.3 6.0 %all-to-all-start.1 = ((bf16[8,64,768]{2,1,0:T(8,128)(2,1)}), bf16[8,64,768]{2,1,0:T(8,128)(2,1)S(1)}, u32[]{:S(2)}, u32[]{:S(2)}) async-start(bf16[8,64,768]{2,1,0:T(8,128)(2,1)} %param.3), calls=%async_computation.1 | async-start | bytes 1572864 | tf_op jit(solution)/shard_map/cond/branch_1_fun/all_to_all | solution.py:183
  61.3 10.6 %all-to-all-done.1.refs_0_ = bf16[8,64,768]{2,1,0:T(8,128)(2,1)S(1)} async-done(((bf16[8,64,768]{2,1,0:T(8,128)(2,1)}), bf16[8,64,768]{2,1,0:T(8,128)(2,1)S(1)}, u32[]{:S(2)}, u32[]{:S(2)}) %all-to-all-start.1) | async-done | bytes 786464 | tf_op jit(solution)/shard_map/cond/branch_1_fun/all_to_all | solution.py:183
  71.9 1.0 unstage.5
  73.2 0.7 collective-permute-start.11
  73.9 0.7 collective-permute-start.10
  74.7 0.7 collective-permute-start.13
  76.4 1.3 collective-permute-start.15
  77.8 1.3 collective-permute-start.14
  79.1 1.3 saved_far_2.1
  80.4 4.3 %turn_far_2.1 = (f32[1,4096]{1,0:T(1,128)S(1)}, bf16[256,4096]{1,0:T(8,128)(2,1)S(1)}, bf16[4096,256]{1,0:T(8,128)(2,1)S(1)}) custom-call(bf16[2,4096,256]{2,1,0:T(8,128)(2,1)} %refs_0_.14, bf16[2,256,4096]{2,1,0:T(8,128)(2,1)} %refs_1_.16, f32[2,4096]{1,0:T(2,128)S(1)} %copy-done.3), custom_call_target="tpu_custom_call" | custom-call | flops 1 | bytes 1 | tf_op jit(solution)/shard_map/turn_far_2/pallas_call | solution.py:51
  84.7 1.3 collective-permute-done.15.refs_0_
  85.9 1.4 backward_8_0.1
  87.4 1.3 collective-permute-start.17
  88.7 1.5 backward_8_1.1
  90.2 1.3 collective-permute-start.16
  91.8 1.4 collective-permute-done.17.refs_0_
  93.3 1.3 collective-permute-start.19
  94.6 1.4 collective-permute-done.16.refs_0_
  96.1 1.3 collective-permute-start.18
  97.4 1.3 saved_10.1
  98.7 4.3 %turn_10.1 = (f32[1,4096]{1,0:T(1,128)S(1)}, bf16[256,4096]{1,0:T(8,128)(2,1)S(1)}, bf16[4096,256]{1,0:T(8,128)(2,1)S(1)}) custom-call(bf16[2,4096,256]{2,1,0:T(8,128)(2,1)} %refs_0_.14, bf16[2,256,4096]{2,1,0:T(8,128)(2,1)} %refs_1_.16, f32[2,4096]{1,0:T(2,128)S(1)} %copy-done.3), custom_call_target="tpu_custom_call" | custom-call | flops 1 | bytes 1 | tf_op jit(solution)/shard_map/turn_10/pallas_call | solution.py:51
  103.6 1.5 backward_10_0.1
  105.1 1.3 collective-permute-start.21
  106.4 0.8 collective-permute-done.18.refs_0_
  107.2 1.5 backward_10_1.1
  108.6 1.3 collective-permute-start.20
  110.0 37.4 %conditional.9 = ((f32[2,2,256,256]{3,2,1,0:T(8,128)S(1)}, bf16[2,2,256,256]{3,2,1,0:T(8,128)(2,1)S(1)})) conditional(s32[]{:T(128)} %convert_element_type.29, () %tuple.80, (bf16[8,192,768]{2,1,0:T(8,128)(2,1)}, bf16[8,64,768]{2,1,0:T(8,128)(2,1)}) %tuple.82), branch_computations={%region_7.8_spmd, %region_8.9_spmd} | conditional | flops 1 | bytes 7864357 | solution.py:573
  110.0 36.3 %all_to_all.28.refs_1_ = bf16[8,192,768]{2,1,0:T(8,128)(2,1)S(1)} all-to-all(bf16[8,192,768]{2,1,0:T(8,128)(2,1)} %get-tuple-element.35), channel_id=1, replica_groups={{0,2,4,6,8,10,12,14},{1,3,5,7,9,11,13,15},{16,18,20,22,24,26,28,30},{17..., dimensions={0} | all-to-all | bytes 4718592 | tf_op jit(solution)/shard_map/cond/branch_1_fun/all_to_all | solution.py:183
  146.3 1.1 products_far.1
  147.7 0.8 backward_11_0.1
  148.4 0.7 collective-permute-start.23
  149.1 0.8 backward_11_1.1
  149.9 1.4 collective-permute-start.22
  151.6 1.1 backward_12_1.1
  153.3 0.9 conditional.11
  153.4 0.8 copy.167
  154.2 2.1 %collective-permute-done.24 = bf16[2,2,256,256]{3,2,1,0:T(8,128)(2,1)S(1)} collective-permute-done((bf16[2,2,256,256]{3,2,1,0:T(8,128)(2,1)}, bf16[2,2,256,256]{3,2,1,0:T(8,128)(2,1)S(1)}, u32[]{:S(2)}, u32[]{:S(2)}) %collective-permute-start.24) | collective-permute-done | bytes 524320 | tf_op jit(solution)/shard_map/ppermute | solution.py:622
  156.6 10.7 %collective-permute-done.25 = bf16[2,256,256]{2,1,0:T(8,128)(2,1)S(1)} collective-permute-done((bf16[2,256,256]{2,1,0:T(8,128)(2,1)S(1)}, bf16[2,256,256]{2,1,0:T(8,128)(2,1)S(1)}, u32[]{:S(2)}, u32[]{:S(2)}) %collective-permute-start.25) | collective-permute-done | bytes 262176 | tf_op jit(solution)/shard_map/ppermute | solution.py:624
  167.3 1.5 multiply_reduce_fusion
  (77 shorter events, 5.1 us)
Async XLA Ops:
  0.6 0.8 copy-start.2
  1.6 2.9 %collective-permute-start.1 = (bf16[32,4096]{1,0:T(8,128)(2,1)S(1)}, bf16[32,4096]{1,0:T(8,128)(2,1)S(1)}, u32[]{:S(2)}, u32[]{:S(2)}) collective-permute-start(bf16[32,4096]{1,0:T(8,128)(2,1)S(1)} %get-tuple-element.261), channel_id=1, source_target_pairs={{0,16},{112,96},{1,17},{113,97},{2,18},{114,98},{3,19},{115,99},{4... | collective-permute-start | bytes 786440 | tf_op jit(solution)/shard_map/ppermute | solution.py:171
  2.3 0.8 copy-start.3
  2.4 5.1 %collective-permute-start = (bf16[32,4096]{1,0:T(8,128)(2,1)S(1)}, bf16[32,4096]{1,0:T(8,128)(2,1)S(1)}, u32[]{:S(2)}, u32[]{:S(2)}) collective-permute-start(bf16[32,4096]{1,0:T(8,128)(2,1)S(1)} %get-tuple-element.257), channel_id=1, source_target_pairs={{0,16},{112,96},{1,17},{113,97},{2,18},{114,98},{3,19},{115,99},{4... | collective-permute-start | bytes 786440 | tf_op jit(solution)/shard_map/ppermute | solution.py:171
  3.2 1.3 copy-start
  4.5 1.6 copy-start.1
  6.2 21.4 %collective-permute-start.3 = (bf16[32,4096]{1,0:T(8,128)(2,1)S(1)}, bf16[32,4096]{1,0:T(8,128)(2,1)S(1)}, u32[]{:S(2)}, u32[]{:S(2)}) collective-permute-start(bf16[32,4096]{1,0:T(8,128)(2,1)S(1)} %get-tuple-element.278), channel_id=1, source_target_pairs={{16,32},{96,80},{17,33},{97,81},{18,34},{98,82},{19,35},{99,83},{2... | collective-permute-start | bytes 786440 | tf_op jit(solution)/shard_map/ppermute | solution.py:171
  7.5 24.1 %collective-permute-start.2 = (bf16[32,4096]{1,0:T(8,128)(2,1)S(1)}, bf16[32,4096]{1,0:T(8,128)(2,1)S(1)}, u32[]{:S(2)}, u32[]{:S(2)}) collective-permute-start(bf16[32,4096]{1,0:T(8,128)(2,1)S(1)} %get-tuple-element.267), channel_id=1, source_target_pairs={{16,32},{96,80},{17,33},{97,81},{18,34},{98,82},{19,35},{99,83},{2... | collective-permute-start | bytes 786440 | tf_op jit(solution)/shard_map/ppermute | solution.py:171
  29.2 5.9 %collective-permute-start.5 = (bf16[32,4096]{1,0:T(8,128)(2,1)S(1)}, bf16[32,4096]{1,0:T(8,128)(2,1)S(1)}, u32[]{:S(2)}, u32[]{:S(2)}) collective-permute-start(bf16[32,4096]{1,0:T(8,128)(2,1)S(1)} %get-tuple-element.295), channel_id=1, source_target_pairs={{32,48},{80,64},{33,49},{81,65},{34,50},{82,66},{35,51},{83,67},{3... | collective-permute-start | bytes 786440 | tf_op jit(solution)/shard_map/ppermute | solution.py:171
  33.3 6.7 %collective-permute-start.4 = (bf16[32,4096]{1,0:T(8,128)(2,1)S(1)}, bf16[32,4096]{1,0:T(8,128)(2,1)S(1)}, u32[]{:S(2)}, u32[]{:S(2)}) collective-permute-start(bf16[32,4096]{1,0:T(8,128)(2,1)S(1)} %get-tuple-element.285), channel_id=1, source_target_pairs={{32,48},{80,64},{33,49},{81,65},{34,50},{82,66},{35,51},{83,67},{3... | collective-permute-start | bytes 786440 | tf_op jit(solution)/shard_map/ppermute | solution.py:171
  35.2 11.2 %collective-permute-start.7 = (bf16[32,4096]{1,0:T(8,128)(2,1)S(1)}, bf16[32,4096]{1,0:T(8,128)(2,1)S(1)}, u32[]{:S(2)}, u32[]{:S(2)}) collective-permute-start(bf16[32,4096]{1,0:T(8,128)(2,1)S(1)} %get-tuple-element.311), channel_id=1, source_target_pairs={{48,32},{64,80},{49,33},{65,81},{50,34},{66,82},{51,35},{67,83},{5... | collective-permute-start | bytes 786440 | tf_op jit(solution)/shard_map/ppermute | solution.py:171
  40.1 12.1 %collective-permute-start.6 = (bf16[32,4096]{1,0:T(8,128)(2,1)S(1)}, bf16[32,4096]{1,0:T(8,128)(2,1)S(1)}, u32[]{:S(2)}, u32[]{:S(2)}) collective-permute-start(bf16[32,4096]{1,0:T(8,128)(2,1)S(1)} %get-tuple-element.304), channel_id=1, source_target_pairs={{48,32},{64,80},{49,33},{65,81},{50,34},{66,82},{51,35},{67,83},{5... | collective-permute-start | bytes 786440 | tf_op jit(solution)/shard_map/ppermute | solution.py:171
  48.1 25.0 %collective-permute-start.9 = (bf16[32,4096]{1,0:T(8,128)(2,1)S(1)}, bf16[32,4096]{1,0:T(8,128)(2,1)S(1)}, u32[]{:S(2)}, u32[]{:S(2)}) collective-permute-start(bf16[32,4096]{1,0:T(8,128)(2,1)S(1)} %get-tuple-element.331), channel_id=1, source_target_pairs={{32,16},{80,96},{33,17},{81,97},{34,18},{82,98},{35,19},{83,99},{3... | collective-permute-start | bytes 786440 | tf_op jit(solution)/shard_map/ppermute | solution.py:171
  53.9 20.0 %collective-permute-start.8 = (bf16[32,4096]{1,0:T(8,128)(2,1)S(1)}, bf16[32,4096]{1,0:T(8,128)(2,1)S(1)}, u32[]{:S(2)}, u32[]{:S(2)}) collective-permute-start(bf16[32,4096]{1,0:T(8,128)(2,1)S(1)} %get-tuple-element.318), channel_id=1, source_target_pairs={{32,16},{80,96},{33,17},{81,97},{34,18},{82,98},{35,19},{83,99},{3... | collective-permute-start | bytes 786440 | tf_op jit(solution)/shard_map/ppermute | solution.py:171
  55.3 16.7 %all-to-all-start.1 = ((bf16[8,64,768]{2,1,0:T(8,128)(2,1)}), bf16[8,64,768]{2,1,0:T(8,128)(2,1)S(1)}, u32[]{:S(2)}, u32[]{:S(2)}) async-start(bf16[8,64,768]{2,1,0:T(8,128)(2,1)} %param.3), calls=%async_computation.1 | async-start | bytes 1572864 | tf_op jit(solution)/shard_map/cond/branch_1_fun/all_to_all | solution.py:183
  73.2 1.4 collective-permute-start.11
  73.9 1.5 collective-permute-start.10
  74.7 1.6 collective-permute-start.13
  75.5 2.2 %collective-permute-start.12 = (bf16[32,4096]{1,0:T(8,128)(2,1)S(1)}, bf16[32,4096]{1,0:T(8,128)(2,1)S(1)}, u32[]{:S(2)}, u32[]{:S(2)}) collective-permute-start(bf16[32,4096]{1,0:T(8,128)(2,1)S(1)} %get-tuple-element.346), channel_id=1, source_target_pairs={{0,16},{112,96},{1,17},{113,97},{2,18},{114,98},{3,19},{115,99},{4... | collective-permute-start | bytes 786440 | tf_op jit(solution)/shard_map/ppermute | solution.py:171
  76.4 9.5 %collective-permute-start.15 = (bf16[32,4096]{1,0:T(8,128)(2,1)S(1)}, bf16[32,4096]{1,0:T(8,128)(2,1)S(1)}, u32[]{:S(2)}, u32[]{:S(2)}) collective-permute-start(bf16[32,4096]{1,0:T(8,128)(2,1)S(1)} %get-tuple-element.375), channel_id=1, source_target_pairs={{16,32},{96,80},{17,33},{97,81},{18,34},{98,82},{19,35},{99,83},{2... | collective-permute-start | bytes 786440 | tf_op jit(solution)/shard_map/ppermute | solution.py:171
  77.8 11.0 %collective-permute-start.14 = (bf16[32,4096]{1,0:T(8,128)(2,1)S(1)}, bf16[32,4096]{1,0:T(8,128)(2,1)S(1)}, u32[]{:S(2)}, u32[]{:S(2)}) collective-permute-start(bf16[32,4096]{1,0:T(8,128)(2,1)S(1)} %get-tuple-element.355), channel_id=1, source_target_pairs={{16,32},{96,80},{17,33},{97,81},{18,34},{98,82},{19,35},{99,83},{2... | collective-permute-start | bytes 786440 | tf_op jit(solution)/shard_map/ppermute | solution.py:171
  87.4 5.8 %collective-permute-start.17 = (bf16[32,4096]{1,0:T(8,128)(2,1)S(1)}, bf16[32,4096]{1,0:T(8,128)(2,1)S(1)}, u32[]{:S(2)}, u32[]{:S(2)}) collective-permute-start(bf16[32,4096]{1,0:T(8,128)(2,1)S(1)} %get-tuple-element.389), channel_id=1, source_target_pairs={{32,48},{80,64},{33,49},{81,65},{34,50},{82,66},{35,51},{83,67},{3... | collective-permute-start | bytes 786440 | tf_op jit(solution)/shard_map/ppermute | solution.py:171
  90.2 5.8 %collective-permute-start.16 = (bf16[32,4096]{1,0:T(8,128)(2,1)S(1)}, bf16[32,4096]{1,0:T(8,128)(2,1)S(1)}, u32[]{:S(2)}, u32[]{:S(2)}) collective-permute-start(bf16[32,4096]{1,0:T(8,128)(2,1)S(1)} %get-tuple-element.379), channel_id=1, source_target_pairs={{32,48},{80,64},{33,49},{81,65},{34,50},{82,66},{35,51},{83,67},{3... | collective-permute-start | bytes 786440 | tf_op jit(solution)/shard_map/ppermute | solution.py:171
  93.3 10.3 %collective-permute-start.19 = (bf16[32,4096]{1,0:T(8,128)(2,1)S(1)}, bf16[32,4096]{1,0:T(8,128)(2,1)S(1)}, u32[]{:S(2)}, u32[]{:S(2)}) collective-permute-start(bf16[32,4096]{1,0:T(8,128)(2,1)S(1)} %get-tuple-element.403), channel_id=1, source_target_pairs={{48,32},{64,80},{49,33},{65,81},{50,34},{66,82},{51,35},{67,83},{5... | collective-permute-start | bytes 786440 | tf_op jit(solution)/shard_map/ppermute | solution.py:171
  96.1 11.1 %collective-permute-start.18 = (bf16[32,4096]{1,0:T(8,128)(2,1)S(1)}, bf16[32,4096]{1,0:T(8,128)(2,1)S(1)}, u32[]{:S(2)}, u32[]{:S(2)}) collective-permute-start(bf16[32,4096]{1,0:T(8,128)(2,1)S(1)} %get-tuple-element.393), channel_id=1, source_target_pairs={{48,32},{64,80},{49,33},{65,81},{50,34},{66,82},{51,35},{67,83},{5... | collective-permute-start | bytes 786440 | tf_op jit(solution)/shard_map/ppermute | solution.py:171
  105.1 42.6 %collective-permute-start.21 = (bf16[32,4096]{1,0:T(8,128)(2,1)S(1)}, bf16[32,4096]{1,0:T(8,128)(2,1)S(1)}, u32[]{:S(2)}, u32[]{:S(2)}) collective-permute-start(bf16[32,4096]{1,0:T(8,128)(2,1)S(1)} %get-tuple-element.425), channel_id=1, source_target_pairs={{32,16},{80,96},{33,17},{81,97},{34,18},{82,98},{35,19},{83,99},{3... | collective-permute-start | bytes 786440 | tf_op jit(solution)/shard_map/ppermute | solution.py:171
  108.6 40.5 %collective-permute-start.20 = (bf16[32,4096]{1,0:T(8,128)(2,1)S(1)}, bf16[32,4096]{1,0:T(8,128)(2,1)S(1)}, u32[]{:S(2)}, u32[]{:S(2)}) collective-permute-start(bf16[32,4096]{1,0:T(8,128)(2,1)S(1)} %get-tuple-element.407), channel_id=1, source_target_pairs={{32,16},{80,96},{33,17},{81,97},{34,18},{82,98},{35,19},{83,99},{3... | collective-permute-start | bytes 786440 | tf_op jit(solution)/shard_map/ppermute | solution.py:171
  110.0 36.3 %copy-start.7 = (bf16[8,64,768]{2,1,0:T(8,128)(2,1)S(1)}, bf16[8,64,768]{2,1,0:T(8,128)(2,1)}, u32[]{:S(2)}) copy-start(bf16[8,64,768]{2,1,0:T(8,128)(2,1)} %get-tuple-element.34.refs_0_) | copy-start | bytes 2359300 | tf_op jit(solution)/shard_map/cond
  148.4 3.1 %collective-permute-start.23 = (bf16[32,4096]{1,0:T(8,128)(2,1)}, bf16[32,4096]{1,0:T(8,128)(2,1)S(1)}, u32[]{:S(2)}, u32[]{:S(2)}) collective-permute-start(bf16[32,4096]{1,0:T(8,128)(2,1)} %get-tuple-element.447), channel_id=1, source_target_pairs={{16,0},{96,112},{17,1},{97,113},{18,2},{98,114},{19,3},{99,115},{2... | collective-permute-start | bytes 786440 | tf_op jit(solution)/shard_map/ppermute | solution.py:171
  149.9 1.7 %collective-permute-start.22 = (bf16[32,4096]{1,0:T(8,128)(2,1)}, bf16[32,4096]{1,0:T(8,128)(2,1)}, u32[]{:S(2)}, u32[]{:S(2)}) collective-permute-start(bf16[32,4096]{1,0:T(8,128)(2,1)} %get-tuple-element.429), channel_id=1, source_target_pairs={{16,0},{96,112},{17,1},{97,113},{18,2},{98,114},{19,3},{99,115},{2... | collective-permute-start | bytes 786440 | tf_op jit(solution)/shard_map/ppermute | solution.py:171
  151.6 1.5 copy-start.4
  151.6 1.7 copy-start.5
  154.2 2.4 %slice-start = ((f32[2,4096]{1,0:T(2,128)}), f32[1,4096]{1,0:T(1,128)S(1)}, s32[]{:S(2)}) async-start(f32[2,4096]{1,0:T(2,128)} %refs_2_.21), calls=%async_computation.7 | async-start | bytes 32768 | tf_op jit(solution)/shard_map/slice | solution.py:626
  154.2 2.1 %collective-permute-start.24 = (bf16[2,2,256,256]{3,2,1,0:T(8,128)(2,1)}, bf16[2,2,256,256]{3,2,1,0:T(8,128)(2,1)S(1)}, u32[]{:S(2)}, u32[]{:S(2)}) collective-permute-start(bf16[2,2,256,256]{3,2,1,0:T(8,128)(2,1)} %get-tuple-element.458), channel_id=1, source_target_pairs={{0,1},{1,0},{2,3},{3,2},{4,5},{5,4},{6,7},{7,6},{8,9},{9,8},{10,11... | collective-permute-start | bytes 1572872 | tf_op jit(solution)/shard_map/ppermute | solution.py:622
  156.4 10.8 %collective-permute-start.25 = (bf16[2,256,256]{2,1,0:T(8,128)(2,1)S(1)}, bf16[2,256,256]{2,1,0:T(8,128)(2,1)S(1)}, u32[]{:S(2)}, u32[]{:S(2)}) collective-permute-start(bf16[2,256,256]{2,1,0:T(8,128)(2,1)S(1)} %fusion.1), channel_id=1, source_target_pairs={{0,112},{16,96},{32,80},{48,64},{64,48},{80,32},{96,16},{112,0},{1... | collective-permute-start | bytes 786440 | tf_op jit(solution)/shard_map/ppermute | solution.py:624
  156.6 10.8 %slice-start.1 = ((bf16[2,4096,256]{2,1,0:T(8,128)(2,1)}), bf16[1,4096,256]{2,1,0:T(8,128)(2,1)S(1)}, s32[]{:S(2)}) async-start(bf16[2,4096,256]{2,1,0:T(8,128)(2,1)} %refs_0_.14), calls=%async_computation.8 | async-start | bytes 4194304 | tf_op jit(solution)/shard_map/slice | solution.py:627
